TPU v7x, 128 devices: a whole 4x4x4 slice. The times are simulated.
128 devices in a mesh: view: 8 (over x, core), band: 16 (over y, z).
Axes of the slice: x: 4, y: 4, z: 4, core: 2. Of those that a mesh axis runs over, the one named last changes fastest.
Arguments:
- positions: float32 [3, 65536], P(None, 'band'), may hold values from -48 to 48
- log_scales: float32 [3, 65536], P(None, 'band'), may hold values from -0.7 to 0.7
- rotations: float32 [4, 65536], P(None, 'band'), may hold values from 0.3 to 1.5
- opacity_logit: float32 [1, 65536], P(None, 'band'), may hold values from -6 to -2
- sh_coeffs: float32 [48, 65536], P(None, 'band'), may hold values from -1.8 to 1.8
- view_angles: float32 [8, 2], P('view'), may hold values from -3.140625 to 3.140625
- target: float32 [8, 768, 3, 256], P('view', 'band'), may hold values from -2 to 3
- fetch_index: int32 [8, 16, 16, 512], P('view', 'band'), may hold values from 0 to 4095, as said below
- tile_slots: int32 [8, 768, 256], P('view', 'band'), may hold values from 0 to 8191, as said below
- depth_order: int32 [8, 768, 256], P('view', 'band'), may hold values from 0 to 255, each once within a row
- block_count: int32 [8, 768], P('view', 'band'), may hold values from 64 to 256, as said below
Outputs:
- images: float32 [8, 768, 3, 256], P('view', 'band')
- view_loss: float32 [8], P('view')
- grad_positions: float32 [3, 65536], P(None, 'band')
- grad_log_scales: float32 [3, 65536], P(None, 'band')
- grad_rotations: float32 [4, 65536], P(None, 'band')
- grad_opacity: float32 [1, 65536], P(None, 'band')
- grad_sh: float32 [48, 65536], P(None, 'band')
Inputs may be any that keep to these rules, and one draw needn't show every extreme that they name: `fetch_index`: the 512 entries for one view, band and owner are distinct. `tile_slots`: entry o * 512 + c names the c-th Gaussian that the tile's band requests from owner o; in each view the last owner's request lists, and those of one owner drawn from the seed, are used in full by every band, the others' only in part. `block_count`: each band of each view has a tile with all 256 positions live.
All inputs are finite; a program needn't handle non-finite values.
Results may differ from a plain program's by a relative error of at most 0.0003.
Values sent between devices are 32-bit elements; how exact they have to be, the bound alone decides.
No kernel may reach another device: no remote copies, remote signals or barrier semaphores. Data moves between devices by JAX's collectives and lax.ppermute only.
A program may use at most 128 MiB of HBM per device.

v0:
```python
from functools import partial
import math

import jax
import jax.numpy as jnp
from jax import lax
from jax.sharding import PartitionSpec as P

TILE_SIDE = 16
TILE_BLOCK = 4


zero_term = 0.28209479177387814
first_term = 0.4886025119029199
second_terms = (
    1.0925484305920792,
    -1.0925484305920792,
    0.31539156525252005,
    -1.0925484305920792,
    0.5462742152960396,
)
third_terms = (
    -0.5900435899266435,
    2.890611442640554,
    -0.4570457994644658,
    0.3731763325901154,
    -0.4570457994644658,
    1.445305721320277,
    -0.5900435899266435,
)
dilation = 0.3
highest = lax.Precision.HIGHEST


def harmonic_basis(dir_x, dir_y, dir_z):
    square_x = dir_x * dir_x
    square_y = dir_y * dir_y
    square_z = dir_z * dir_z
    terms = [
        zero_term + 0.0 * dir_x,
        -first_term * dir_y,
        first_term * dir_z,
        -first_term * dir_x,
        second_terms[0] * dir_x * dir_y,
        second_terms[1] * dir_y * dir_z,
        second_terms[2] * (2.0 * square_z - square_x - square_y),
        second_terms[3] * dir_x * dir_z,
        second_terms[4] * (square_x - square_y),
        third_terms[0] * dir_y * (3.0 * square_x - square_y),
        third_terms[1] * dir_x * dir_y * dir_z,
        third_terms[2] * dir_y * (4.0 * square_z - square_x - square_y),
        third_terms[3] * dir_z * (2.0 * square_z - 3.0 * square_x - 3.0 * square_y),
        third_terms[4] * dir_x * (4.0 * square_z - square_x - square_y),
        third_terms[5] * dir_z * (square_x - square_y),
        third_terms[6] * dir_x * (square_x - 3.0 * square_y),
    ]
    return jnp.stack(terms)


def project(angles, positions, log_scales, rotations, opacity_logit, sh_coeffs):
    cos_a, sin_a = (jnp.cos(angles[0]), jnp.sin(angles[0]))
    cos_e, sin_e = (jnp.cos(angles[1]), jnp.sin(angles[1]))
    right = (-sin_a, cos_a, 0.0 * sin_a)
    upward = (-sin_e * cos_a, -sin_e * sin_a, cos_e)
    mean_x = right[0] * positions[0] + right[1] * positions[1] + right[2] * positions[2]
    mean_y = upward[0] * positions[0] + upward[1] * positions[1] + upward[2] * positions[2]
    length = jnp.sqrt(jnp.sum(rotations * rotations, axis=0))
    quat_w = rotations[0] / length
    quat_x = rotations[1] / length
    quat_y = rotations[2] / length
    quat_z = rotations[3] / length
    matrix = [
        [
            1.0 - 2.0 * (quat_y * quat_y + quat_z * quat_z),
            2.0 * (quat_x * quat_y - quat_w * quat_z),
            2.0 * (quat_x * quat_z + quat_w * quat_y),
        ],
        [
            2.0 * (quat_x * quat_y + quat_w * quat_z),
            1.0 - 2.0 * (quat_x * quat_x + quat_z * quat_z),
            2.0 * (quat_y * quat_z - quat_w * quat_x),
        ],
        [
            2.0 * (quat_x * quat_z - quat_w * quat_y),
            2.0 * (quat_y * quat_z + quat_w * quat_x),
            1.0 - 2.0 * (quat_x * quat_x + quat_y * quat_y),
        ],
    ]
    scales = jnp.exp(log_scales)

    def screen_row(axis_row):
        return [
            (
                axis_row[0] * matrix[0][col]
                + axis_row[1] * matrix[1][col]
                + axis_row[2] * matrix[2][col]
            )
            * scales[col]
            for col in range(3)
        ]

    first = screen_row(right)
    second = screen_row(upward)
    cov_a = first[0] * first[0] + first[1] * first[1] + first[2] * first[2] + dilation
    cov_b = first[0] * second[0] + first[1] * second[1] + first[2] * second[2]
    cov_c = second[0] * second[0] + second[1] * second[1] + second[2] * second[2] + dilation
    determinant = cov_a * cov_c - cov_b * cov_b
    opacity = jax.nn.sigmoid(opacity_logit[0])
    basis = harmonic_basis(cos_e * cos_a, cos_e * sin_a, sin_e)
    shaped = sh_coeffs.reshape((16, 3, sh_coeffs.shape[1]))
    colours = jnp.maximum(0.5 + jnp.sum(basis[:, None, None] * shaped, axis=0), 0.0)
    front = jnp.stack(
        [mean_x, mean_y, cov_c / determinant, -cov_b / determinant, cov_a / determinant, opacity]
    )
    return jnp.concatenate([front, colours], axis=0)


def blend_tile(compact, limit, goal):
    side = TILE_SIDE
    slot_total = compact.shape[1]
    pixel_ids = jnp.arange(side * side, dtype=jnp.int32)
    pixel_x = (pixel_ids % side).astype(jnp.float32) + 0.5
    pixel_y = (pixel_ids // side).astype(jnp.float32) + 0.5
    turn = 2.0 * math.pi / side
    delta_x = jnp.sin(turn * (pixel_x[:, None] - compact[0][None, :])) / turn
    delta_y = jnp.sin(turn * (pixel_y[:, None] - compact[1][None, :])) / turn
    power = (
        compact[2][None, :] * delta_x * delta_x
        + 2.0 * compact[3][None, :] * delta_x * delta_y
        + compact[4][None, :] * delta_y * delta_y
    )
    slot_ids = jnp.arange(slot_total, dtype=jnp.int32)
    live = (slot_ids < limit).astype(jnp.float32)
    alpha = (live * compact[5])[None, :] * jnp.exp(-0.5 * power)
    log_keep = jnp.log1p(-alpha)
    strict_upper = (slot_ids[:, None] < slot_ids[None, :]).astype(jnp.float32)
    depth = jnp.dot(log_keep, strict_upper, precision=highest, preferred_element_type=jnp.float32)
    weights = alpha * jnp.exp(depth)
    image = lax.dot_general(
        compact[6:9],
        weights,
        (((1,), (1,)), ((), ())),
        precision=highest,
        preferred_element_type=jnp.float32,
    )
    error = image - goal
    return (0.5 * jnp.sum(error * error), image)


def tile_terms(compact, limit, goal):
    (value, image), grad = jax.value_and_grad(blend_tile, has_aux=True)(compact, limit, goal)
    return (value, image, grad)


def local(
    positions,
    log_scales,
    rotations,
    opacity_logit,
    sh_coeffs,
    view_angles,
    target,
    fetch_index,
    tile_slots,
    depth_order,
    block_count,
):
    owners = lax.axis_size("band")
    capacity = fetch_index.shape[3]
    local_total = positions.shape[1]
    viewer = partial(project, view_angles[0])
    params = (positions, log_scales, rotations, opacity_logit, sh_coeffs)
    wanted = lax.all_to_all(
        fetch_index.reshape(owners, capacity), "band", split_axis=0, concat_axis=0, tiled=True
    )
    wanted_flat = wanted.reshape(-1)
    picked = [array[:, wanted_flat] for array in params]
    shaped = [piece.reshape(piece.shape[0], owners, capacity) for piece in picked]
    arrived = (
        lax.all_to_all(shaped[0], "band", split_axis=1, concat_axis=1, tiled=True),
        lax.all_to_all(shaped[1], "band", split_axis=1, concat_axis=1, tiled=True),
        lax.all_to_all(shaped[2], "band", split_axis=1, concat_axis=1, tiled=True),
        lax.all_to_all(shaped[3], "band", split_axis=1, concat_axis=1, tiled=True),
        lax.all_to_all(shaped[4], "band", split_axis=1, concat_axis=1, tiled=True),
    )
    fetched = [piece.reshape(piece.shape[0], -1) for piece in arrived]
    compact, pull = jax.vjp(viewer, *fetched)
    ordered = jnp.take_along_axis(tile_slots[0], depth_order[0], axis=1)
    tile_count = ordered.shape[0]
    slot_total = ordered.shape[1]
    steps = tile_count // TILE_BLOCK

    def tile_block(item):
        block_ids, limits, goals = item
        gathered = jnp.transpose(compact[:, block_ids], (1, 0, 2))
        return jax.vmap(tile_terms)(gathered, limits, goals)

    values, pictures, grads = lax.map(
        tile_block,
        (
            ordered.reshape(steps, TILE_BLOCK, slot_total),
            block_count[0].reshape(steps, TILE_BLOCK),
            target[0].reshape((steps, TILE_BLOCK) + target.shape[2:]),
        ),
    )
    grads = grads.reshape(tile_count, compact.shape[0], slot_total)
    flat_grads = jnp.transpose(grads, (1, 0, 2)).reshape(compact.shape[0], -1)
    cotangent = jnp.zeros_like(compact).at[:, ordered.reshape(-1)].add(flat_grads)
    pulled = pull(cotangent)
    going = [piece.reshape(piece.shape[0], owners, capacity) for piece in pulled]
    returned = (
        lax.all_to_all(going[0], "band", split_axis=1, concat_axis=1, tiled=True),
        lax.all_to_all(going[1], "band", split_axis=1, concat_axis=1, tiled=True),
        lax.all_to_all(going[2], "band", split_axis=1, concat_axis=1, tiled=True),
        lax.all_to_all(going[3], "band", split_axis=1, concat_axis=1, tiled=True),
        lax.all_to_all(going[4], "band", split_axis=1, concat_axis=1, tiled=True),
    )
    owner_terms = [piece.reshape(piece.shape[0], -1) for piece in returned]
    partial_sums = [
        jnp.zeros((piece.shape[0], local_total), jnp.float32).at[:, wanted_flat].add(piece)
        for piece in owner_terms
    ]
    totals = lax.psum(
        (partial_sums[0], partial_sums[1], partial_sums[2], partial_sums[3], partial_sums[4]),
        "view",
    )
    squares = 2.0 * jnp.sum(values)
    whole = lax.psum(squares, "band")
    pixels = target.shape[3]
    view_loss = (whole / (tile_count * owners * pixels * 3)).reshape(1)
    images = pictures.reshape((1, tile_count) + target.shape[2:])
    return (images, view_loss, totals[0], totals[1], totals[2], totals[3], totals[4])


def solution(mesh):
    in_specs = (
        P(None, "band"),
        P(None, "band"),
        P(None, "band"),
        P(None, "band"),
        P(None, "band"),
        P("view", None),
        P("view", "band", None, None),
        P("view", "band", None, None),
        P("view", "band", None),
        P("view", "band", None),
        P("view", "band"),
    )
    out_specs = (
        P("view", "band", None, None),
        P("view"),
        P(None, "band"),
        P(None, "band"),
        P(None, "band"),
        P(None, "band"),
        P(None, "band"),
    )
    return jax.shard_map(local, mesh=mesh, in_specs=in_specs, out_specs=out_specs, check_vma=False)
```

profile of v0, /device:TPU:1, one launch (start us, length us, event | category | flops | bytes accessed | tf_op | source)
XLA Modules:
  0.0 1569.2 jit_solution(9721336413522606800)
XLA Ops:
  19.7 97.2 %gather_fusion.6 = s32[12288]{0:T(1024)S(1)} fusion(s32[48,256]{1,0:T(8,128)S(1)} %bitcast.190, s32[12288]{0:T(1024)S(1)} %bitcast.192), kind=kCustom, calls=%fused_computation.6 | custom fusion | bytes 196608 | tf_op jit(solution)/shard_map/jit(take_along_axis)/gather | solution.py:188
  119.1 80.6 %gather_fusion.4 = f32[8192]{0:T(1024)} fusion(f32[4096]{0:T(1024)S(1)} %bitcast.191, s32[8192]{0:T(1024)S(1)} %broadcast_clamp_fusion.1), kind=kCustom, calls=%fused_computation.4 | custom fusion | bytes 98304 | tf_op jit(solution)/shard_map/gather | solution.py:177
  221.2 29.5 %gather_fusion.1 = f32[8192,3]{1,0:T(8,128)} fusion(f32[3,4096]{0,1:T(8,128)} %copy.268, s32[8192]{0:T(1024)S(1)} %broadcast_clamp_fusion.1), kind=kCustom, calls=%fused_computation.1 | custom fusion | bytes 229376 | tf_op jit(solution)/shard_map/gather | solution.py:177
  254.2 29.5 %gather_fusion.3 = f32[8192,3]{1,0:T(8,128)} fusion(f32[3,4096]{0,1:T(8,128)} %copy.272, s32[8192]{0:T(1024)S(1)} %broadcast_clamp_fusion.1), kind=kCustom, calls=%fused_computation.3 | custom fusion | bytes 229376 | tf_op jit(solution)/shard_map/gather | solution.py:177
  287.2 29.5 %gather_fusion.2 = f32[8192,4]{1,0:T(8,128)} fusion(f32[4,4096]{0,1:T(8,128)} %copy.270, s32[8192]{0:T(1024)S(1)} %broadcast_clamp_fusion.1), kind=kCustom, calls=%fused_computation.2 | custom fusion | bytes 294912 | tf_op jit(solution)/shard_map/gather | solution.py:177
  320.1 27.9 %gather_fusion.5 = f32[8192,48]{1,0:T(8,128)} fusion(f32[48,4096]{0,1:T(8,128)S(1)} %copy.275, s32[8192]{0:T(1024)S(1)} %broadcast_clamp_fusion.1), kind=kCustom, calls=%fused_computation.5 | custom fusion | bytes 3178496 | tf_op jit(solution)/shard_map/gather | solution.py:177
  424.6 654.9 %while.16 = (s32[]{:T(128)}, f32[12,4]{1,0:T(8,128)S(1)}, f32[12,4,3,256]{3,2,1,0:T(4,128)}, f32[12,4,9,256]{3,2,1,0:T(8,128)S(1)}, s32[12,4,256]{2,1,0:T(4,128)...) while((s32[]{:T(128)}, f32[12,4]{1,0:T(8,128)S(1)}, ...), condition=%wide.region_10.11_spmd, body=%wide.region_2.10_spmd.sunk | while | flops 1671127040 | bytes 7055637 | solution.py:198
  460.3 18.1 %multiply_reduce_fusion.12 = (f32[4,256]{1,0:T(4,128)S(1)}, f32[4,256]{1,0:T(4,128)S(1)}, f32[4,256]{1,0:T(4,128)S(1)}, f32[4,256]{1,0:T(4,128)S(1)}, f32[4,256]{1,0:T(4,128)S(1)}, /*index=5*/f32[4,256]{1,0:T(4,128)S(1)}) fusion(f32[4,256]{1,0:T(4,128)S(1)} %get-tuple-element.380, f32[256]{0:T(256)S(1)} %get-tuple-element.381, ...), kind=kOutput, calls=%fused_computation.21.clone.1 | convolution fusion | flops 823977984 | bytes 2160640 | tf_op jit(solution)/shard_map/while/body/eval_jaxpr/vmap(transpose(jvp()))/dot_general | solution.py:137
  514.3 17.9 %multiply_reduce_fusion.12 = (f32[4,256]{1,0:T(4,128)S(1)}, f32[4,256]{1,0:T(4,128)S(1)}, f32[4,256]{1,0:T(4,128)S(1)}, f32[4,256]{1,0:T(4,128)S(1)}, f32[4,256]{1,0:T(4,128)S(1)}, /*index=5*/f32[4,256]{1,0:T(4,128)S(1)}) fusion(f32[4,256]{1,0:T(4,128)S(1)} %get-tuple-element.380, f32[256]{0:T(256)S(1)} %get-tuple-element.381, ...), kind=kOutput, calls=%fused_computation.21.clone.1 | convolution fusion | flops 823977984 | bytes 2160640 | tf_op jit(solution)/shard_map/while/body/eval_jaxpr/vmap(transpose(jvp()))/dot_general | solution.py:137
  568.0 18.1 %multiply_reduce_fusion.12 = (f32[4,256]{1,0:T(4,128)S(1)}, f32[4,256]{1,0:T(4,128)S(1)}, f32[4,256]{1,0:T(4,128)S(1)}, f32[4,256]{1,0:T(4,128)S(1)}, f32[4,256]{1,0:T(4,128)S(1)}, /*index=5*/f32[4,256]{1,0:T(4,128)S(1)}) fusion(f32[4,256]{1,0:T(4,128)S(1)} %get-tuple-element.380, f32[256]{0:T(256)S(1)} %get-tuple-element.381, ...), kind=kOutput, calls=%fused_computation.21.clone.1 | convolution fusion | flops 823977984 | bytes 2160640 | tf_op jit(solution)/shard_map/while/body/eval_jaxpr/vmap(transpose(jvp()))/dot_general | solution.py:137
  675.7 18.1 %multiply_reduce_fusion.12 = (f32[4,256]{1,0:T(4,128)S(1)}, f32[4,256]{1,0:T(4,128)S(1)}, f32[4,256]{1,0:T(4,128)S(1)}, f32[4,256]{1,0:T(4,128)S(1)}, f32[4,256]{1,0:T(4,128)S(1)}, /*index=5*/f32[4,256]{1,0:T(4,128)S(1)}) fusion(f32[4,256]{1,0:T(4,128)S(1)} %get-tuple-element.380, f32[256]{0:T(256)S(1)} %get-tuple-element.381, ...), kind=kOutput, calls=%fused_computation.21.clone.1 | convolution fusion | flops 823977984 | bytes 2160640 | tf_op jit(solution)/shard_map/while/body/eval_jaxpr/vmap(transpose(jvp()))/dot_general | solution.py:137
  729.6 17.9 %multiply_reduce_fusion.12 = (f32[4,256]{1,0:T(4,128)S(1)}, f32[4,256]{1,0:T(4,128)S(1)}, f32[4,256]{1,0:T(4,128)S(1)}, f32[4,256]{1,0:T(4,128)S(1)}, f32[4,256]{1,0:T(4,128)S(1)}, /*index=5*/f32[4,256]{1,0:T(4,128)S(1)}) fusion(f32[4,256]{1,0:T(4,128)S(1)} %get-tuple-element.380, f32[256]{0:T(256)S(1)} %get-tuple-element.381, ...), kind=kOutput, calls=%fused_computation.21.clone.1 | convolution fusion | flops 823977984 | bytes 2160640 | tf_op jit(solution)/shard_map/while/body/eval_jaxpr/vmap(transpose(jvp()))/dot_general | solution.py:137
  783.4 18.1 %multiply_reduce_fusion.12 = (f32[4,256]{1,0:T(4,128)S(1)}, f32[4,256]{1,0:T(4,128)S(1)}, f32[4,256]{1,0:T(4,128)S(1)}, f32[4,256]{1,0:T(4,128)S(1)}, f32[4,256]{1,0:T(4,128)S(1)}, /*index=5*/f32[4,256]{1,0:T(4,128)S(1)}) fusion(f32[4,256]{1,0:T(4,128)S(1)} %get-tuple-element.380, f32[256]{0:T(256)S(1)} %get-tuple-element.381, ...), kind=kOutput, calls=%fused_computation.21.clone.1 | convolution fusion | flops 823977984 | bytes 2160640 | tf_op jit(solution)/shard_map/while/body/eval_jaxpr/vmap(transpose(jvp()))/dot_general | solution.py:137
  837.3 17.9 %multiply_reduce_fusion.12 = (f32[4,256]{1,0:T(4,128)S(1)}, f32[4,256]{1,0:T(4,128)S(1)}, f32[4,256]{1,0:T(4,128)S(1)}, f32[4,256]{1,0:T(4,128)S(1)}, f32[4,256]{1,0:T(4,128)S(1)}, /*index=5*/f32[4,256]{1,0:T(4,128)S(1)}) fusion(f32[4,256]{1,0:T(4,128)S(1)} %get-tuple-element.380, f32[256]{0:T(256)S(1)} %get-tuple-element.381, ...), kind=kOutput, calls=%fused_computation.21.clone.1 | convolution fusion | flops 823977984 | bytes 2160640 | tf_op jit(solution)/shard_map/while/body/eval_jaxpr/vmap(transpose(jvp()))/dot_general | solution.py:137
  891.0 18.1 %multiply_reduce_fusion.12 = (f32[4,256]{1,0:T(4,128)S(1)}, f32[4,256]{1,0:T(4,128)S(1)}, f32[4,256]{1,0:T(4,128)S(1)}, f32[4,256]{1,0:T(4,128)S(1)}, f32[4,256]{1,0:T(4,128)S(1)}, /*index=5*/f32[4,256]{1,0:T(4,128)S(1)}) fusion(f32[4,256]{1,0:T(4,128)S(1)} %get-tuple-element.380, f32[256]{0:T(256)S(1)} %get-tuple-element.381, ...), kind=kOutput, calls=%fused_computation.21.clone.1 | convolution fusion | flops 823977984 | bytes 2160640 | tf_op jit(solution)/shard_map/while/body/eval_jaxpr/vmap(transpose(jvp()))/dot_general | solution.py:137
  998.7 18.1 %multiply_reduce_fusion.12 = (f32[4,256]{1,0:T(4,128)S(1)}, f32[4,256]{1,0:T(4,128)S(1)}, f32[4,256]{1,0:T(4,128)S(1)}, f32[4,256]{1,0:T(4,128)S(1)}, f32[4,256]{1,0:T(4,128)S(1)}, /*index=5*/f32[4,256]{1,0:T(4,128)S(1)}) fusion(f32[4,256]{1,0:T(4,128)S(1)} %get-tuple-element.380, f32[256]{0:T(256)S(1)} %get-tuple-element.381, ...), kind=kOutput, calls=%fused_computation.21.clone.1 | convolution fusion | flops 823977984 | bytes 2160640 | tf_op jit(solution)/shard_map/while/body/eval_jaxpr/vmap(transpose(jvp()))/dot_general | solution.py:137
  1083.5 68.2 %scatter_custom_fusion = f32[9,8192]{0,1:T(8,128)} fusion(s32[12288]{0:T(1024)} %bitcast.269, f32[12288,9]{1,0:T(8,128)} %bitcast.196, f32[]{:T(128)} %constant.171.clone.1), kind=kCustom, calls=%fused_computation.103 | custom fusion | flops 110592 | bytes 295424 | tf_op jit(solution)/shard_map/scatter-add | solution.py:208
  1234.1 43.9 %scatter_custom_fusion.4 = f32[4096]{0:T(1024)} fusion(s32[8192]{0:T(1024)} %bitcast.259, f32[8192]{0:T(1024)} %bitcast.270, f32[]{:T(128)} %constant.171.clone.1), kind=kCustom, calls=%fused_computation.248 | custom fusion | flops 8192 | bytes 16896 | tf_op jit(solution)/shard_map/scatter-add | solution.py:220
  1280.7 45.7 %scatter_custom_fusion.2 = f32[3,4096]{0,1:T(8,128)} fusion(s32[8192]{0:T(1024)} %bitcast.260, f32[8192,3]{1,0:T(8,128)} %copy.292, f32[]{:T(128)} %constant.171.clone.1), kind=kCustom, calls=%fused_computation.110 | custom fusion | flops 24576 | bytes 49664 | tf_op jit(solution)/shard_map/scatter-add | solution.py:220
  1329.1 45.7 %scatter_custom_fusion.1 = f32[3,4096]{0,1:T(8,128)} fusion(s32[8192]{0:T(1024)} %bitcast.261, f32[8192,3]{1,0:T(8,128)} %copy.287, f32[]{:T(128)} %constant.171.clone.1), kind=kCustom, calls=%fused_computation.112 | custom fusion | flops 24576 | bytes 49664 | tf_op jit(solution)/shard_map/scatter-add | solution.py:220
  1377.6 45.7 %scatter_custom_fusion.3 = f32[4,4096]{0,1:T(8,128)} fusion(s32[8192]{0:T(1024)} %bitcast.262, f32[8192,4]{1,0:T(8,128)} %copy.294, f32[]{:T(128)} %constant.171.clone.1), kind=kCustom, calls=%fused_computation.108 | custom fusion | flops 32768 | bytes 66048 | tf_op jit(solution)/shard_map/scatter-add | solution.py:220
  1426.3 45.8 %scatter_custom_fusion.5 = f32[48,4096]{0,1:T(8,128)} fusion(s32[8192]{0:T(1024)} %bitcast.263, f32[8192,48]{1,0:T(8,128)} %copy.299, f32[]{:T(128)} %constant.171.clone.1), kind=kCustom, calls=%fused_computation.106 | custom fusion | flops 393216 | bytes 786944 | tf_op jit(solution)/shard_map/scatter-add | solution.py:220
  1473.4 33.6 %psum.42 = f32[]{:T(128)} all-reduce(f32[]{:T(128)S(6)} %mul.2718), channel_id=1, replica_groups=mesh['view'=8,'band'=16] {'band'}, use_global_device_ids=true, to_apply=%region_12.13 | all-reduce | flops 1 | bytes 8 | tf_op jit(solution)/shard_map/psum | solution.py:228
  1514.2 40.2 %all-reduce.30.cloned.1.call-done = (f32[4,4096]{0,1:T(8,128)}, f32[48,4096]{0,1:T(8,128)}) async-done(((f32[4,4096]{0,1:T(8,128)}, f32[48,4096]{0,1:T(8,128)}), (f32[4,4096]{0,1:T(8,128)}, f32[48,4096]{0,1:T(8,128)})) %all-reduce.30.cloned.1.call-update) | async-done | bytes 851984 | tf_op jit(solution)/shard_map/psum | solution.py:223
  (612 shorter events, 709.2 us)
Async XLA Ops:
  8.6 109.8 %all-to-all-start = ((s32[16,1,512]{2,1,0:T(1,128)}), s32[16,1,512]{2,1,0:T(1,128)S(1)}, u32[]{:S(2)}, u32[]{:S(2)}) async-start(s32[16,1,512]{2,1,0:T(1,128)} %all_to_all.36), calls=%async_computation | async-start | bytes 65536 | tf_op jit(solution)/shard_map/all_to_all | solution.py:173
  119.1 87.4 %copy-start.47 = (f32[1,2]{1,0:T(1,128)S(1)}, f32[1,2]{1,0:T(1,128)}, u32[]{:S(2)}) copy-start(f32[1,2]{1,0:T(1,128)} %param.18) | copy-start | bytes 28
  119.1 91.5 %copy-start.49 = (s32[1,48]{1,0:T(1,128)S(1)}, s32[1,48]{1,0:T(1,128)}, u32[]{:S(2)}) copy-start(s32[1,48]{1,0:T(1,128)} %param.23) | copy-start | bytes 580
  119.1 93.7 %copy-start.15 = (f32[1,48,3,256]{3,1,2,0:T(8,128)S(1)}, f32[1,48,3,256]{3,1,2,0:T(8,128)}, u32[]{:S(2)}) copy-start(f32[1,48,3,256]{3,1,2,0:T(8,128)} %param.19) | copy-start | bytes 442372
  119.1 94.5 %copy-start.37 = (f32[3,4096]{1,0:T(4,128)S(1)}, f32[3,4096]{1,0:T(4,128)}, u32[]{:S(2)}) copy-start(f32[3,4096]{1,0:T(4,128)} %param.13) | copy-start | bytes 147460
  119.1 96.4 %copy-start.38 = (f32[3,4096]{1,0:T(4,128)S(1)}, f32[3,4096]{1,0:T(4,128)}, u32[]{:S(2)}) copy-start(f32[3,4096]{1,0:T(4,128)} %param.14) | copy-start | bytes 147460
  199.7 152.0 %all-to-all-start.4 = ((f32[1,16,512]{2,0,1:T(1,128)}), f32[1,16,512]{2,0,1:T(1,128)S(1)}, u32[]{:S(2)}, u32[]{:S(2)}) async-start(f32[1,16,512]{2,0,1:T(1,128)} %bitcast.37), calls=%async_computation.4 | async-start | bytes 65536 | tf_op jit(solution)/shard_map/all_to_all | solution.py:183
  351.7 23.7 %copy-start.12 = (f32[1,16,512]{2,0,1:T(1,128)}, f32[1,16,512]{2,0,1:T(1,128)S(1)}, u32[]{:S(2)}) copy-start(f32[1,16,512]{2,0,1:T(1,128)S(1)} %all-to-all-done.4) | copy-start | bytes 98308
  351.7 13.4 all-to-all-start.3
  365.1 10.3 all-to-all-start.1
  375.4 10.1 all-to-all-start.2
  385.5 20.0 %all-to-all-start.5 = ((f32[48,16,512]{2,0,1:T(8,128)}), f32[48,16,512]{2,0,1:T(8,128)S(1)}, u32[]{:S(2)}, u32[]{:S(2)}) async-start(f32[48,16,512]{2,0,1:T(8,128)} %copy.276), calls=%async_computation.5 | async-start | bytes 3145728 | tf_op jit(solution)/shard_map/all_to_all | solution.py:184
  1079.6 72.1 %copy-start.43 = (f32[12,4]{1,0:T(8,128)}, f32[12,4]{1,0:T(8,128)S(1)}, u32[]{:S(2)}) copy-start(f32[12,4]{1,0:T(8,128)S(1)} %get-tuple-element.114) | copy-start | bytes 580
  1169.8 23.9 %all-to-all-start.9 = ((f32[1,16,512]{2,0,1:T(1,128)}), f32[1,16,512]{2,0,1:T(1,128)S(1)}, u32[]{:S(2)}, u32[]{:S(2)}) async-start(f32[1,16,512]{2,0,1:T(1,128)} %copy.295), calls=%async_computation.9 | async-start | bytes 65536 | tf_op jit(solution)/shard_map/all_to_all | solution.py:215
  1193.7 13.4 all-to-all-start.6
  1207.1 10.3 all-to-all-start.7
  1217.4 12.9 all-to-all-start.8
  1230.3 192.9 %all-to-all-start.10 = ((f32[48,16,512]{2,0,1:T(8,128)}), f32[48,16,512]{2,0,1:T(8,128)S(1)}, u32[]{:S(2)}, u32[]{:S(2)}) async-start(f32[48,16,512]{2,0,1:T(8,128)} %copy.297), calls=%async_computation.10 | async-start | bytes 3145728 | tf_op jit(solution)/shard_map/all_to_all | solution.py:216
  1234.1 274.4 %all-reduce.28.cloned.1.call-start = ((), (), s32[]{:S(2)}) async-start(), calls=%async_computation.11 | async-start | bytes 8421376 | tf_op jit(solution)/shard_map/psum | solution.py:223
  1374.9 179.6 %all-reduce.30.cloned.1.call-start = ((), (), s32[]{:S(2)}) async-start(), calls=%async_computation.12 | async-start | bytes 8388608 | tf_op jit(solution)/shard_map/psum | solution.py:223
  1426.3 45.8 %copy-start.44 = (f32[12,4]{1,0:T(8,128)S(1)}, f32[12,4]{1,0:T(8,128)}, u32[]{:S(2)}) copy-start(f32[12,4]{1,0:T(8,128)} %copy-done.43) | copy-start | bytes 580
  1426.3 80.7 %copy-start.14 = (f32[12,4,3,256]{3,2,1,0:T(4,128)S(1)}, f32[12,4,3,256]{3,2,1,0:T(4,128)}, u32[]{:S(2)}) copy-start(f32[12,4,3,256]{3,2,1,0:T(4,128)} %get-tuple-element.113) | copy-start | bytes 442372
  1508.4 52.5 %copy-start.1 = (s32[1,48,256]{2,1,0:T(8,128)S(1)}, s32[1,48,256]{2,1,0:T(8,128)}, u32[]{:S(2)}) copy-start(s32[1,48,256]{2,1,0:T(8,128)} %param.21) | copy-start | bytes 147460
  1508.4 51.9 %copy-start.41 = (f32[1,4096]{1,0:T(1,128)S(1)}, f32[1,4096]{1,0:T(1,128)}, u32[]{:S(2)}) copy-start(f32[1,4096]{1,0:T(1,128)} %get-tuple-element.434) | copy-start | bytes 49156
  (39 other events, 300.1 us)
Sparse Core Ops, SparseCore 0:
  1375.0 82.2 all-reduce.27
  1472.3 82.1 all-reduce.29
where the time goes:
time: 1580 us; the launch traced here: 1570 us
  matrix products  543 us (34%)
  local copies, waits for them, and re-layouts  483 us (31%)
  other arithmetic  335 us (21%)
  waiting for transfers between devices  81 us (5%)
  starting transfers between devices  58.8 us (4%)
  blocking collectives  33.6 us (2%)
  between operations  20.7 us (1%)
    dot_general x24, matrix products, blend_tile(): jnp.dot(log_keep, strict_upper, precision=highest, preferred_element_type...  316 us
    scatter-add x5, other arithmetic, local(): jnp.zeros((piece.shape[0], local_total), jnp.float32).at[:, wanted_flat]  227 us
    dot_general x36, matrix products, blend_tile(): lax.dot_general(compact[6:9], weights, (((1,), (1,)), ((), ())), precisio...  226 us
    gather x5, local copies, waits for them, and re-layouts, local(): picked = [array[:, wanted_flat] for array in params]  197 us
    gather x2, local copies, waits for them, and re-layouts, local(): ordered = jnp.take_along_axis(tile_slots[0], depth_order[0], axis=1)  97.3 us
    scatter-add x1, other arithmetic, local(): jnp.zeros_like(compact).at[:, ordered.reshape(-1)].add(flat_grads)  68.2 us
    gather x24, local copies, waits for them, and re-layouts, tile_block(): gathered = jnp.transpose(compact[:, block_ids], (1, 0, 2))  62.2 us
    psum x2, waiting for transfers between devices, local(): lax.psum((partial_sums[0], partial_sums[1], partial_sums[2], partial_sums...  40.3 us
  transfers between devices with their start and end apart: 13, of which 8 were waited for; matrix products, arithmetic and copies ran while one was open for 33% of the time, Pallas kernels for 0%

commit v1 on v0

v1 whole, which is shorter than its diff:
```python
import math

import jax
import jax.numpy as jnp
import ml_dtypes
import numpy as np
from jax import lax
from jax.experimental import pallas as pl
from jax.experimental.pallas import tpu as pltpu
from jax.sharding import PartitionSpec as P

SIDE = 16
PIX = SIDE * SIDE
SLOTS = 256
TILES = 48
CAP = 512
OWNERS = 16
LOCAL = 4096
VIEWS = 8
GROUP = 8
GROUPS = TILES // GROUP
ROWS = GROUP * SLOTS
CHUNK = 256
CHUNK_K = CHUNK // GROUP
CHUNKS = ROWS // CHUNK
SCAT = 512
TURN = 2.0 * math.pi / SIDE
KAPPA = 0.5 / (TURN * TURN)
LOG2E = 1.4426950408889634
DEAD = -1024.0
SEND_ROWS = 48
BACK_ROWS = 56
WIDE = LOCAL + 512 + 128

f32 = jnp.float32
bf16 = jnp.bfloat16

zero_term = 0.28209479177387814
first_term = 0.4886025119029199
second_terms = (
    1.0925484305920792,
    -1.0925484305920792,
    0.31539156525252005,
    -1.0925484305920792,
    0.5462742152960396,
)
third_terms = (
    -0.5900435899266435,
    2.890611442640554,
    -0.4570457994644658,
    0.3731763325901154,
    -0.4570457994644658,
    1.445305721320277,
    -0.5900435899266435,
)
dilation = 0.3


def pixel_tables():
    pixel = np.arange(PIX)
    ang_x = TURN * (pixel % SIDE + 0.5)
    ang_y = TURN * (pixel // SIDE + 0.5)
    sx, cx, sy, cy = np.sin(ang_x), np.cos(ang_x), np.sin(ang_y), np.cos(ang_y)
    rows = np.stack(
        [
            np.ones(PIX),
            np.cos(2 * ang_x),
            np.sin(2 * ang_x),
            np.cos(2 * ang_y),
            np.sin(2 * ang_y),
            sx * sy,
            sx * cy,
            cx * sy,
            cx * cy,
        ]
    )
    kind = ml_dtypes.bfloat16
    parts = []
    rest = rows
    for _ in range(3):
        part = rest.astype(kind)
        parts.append(part)
        rest = rest - part.astype(np.float64)
    order = (0, 1, 2, 0, 1, 0)
    front = np.zeros((128, PIX), kind)
    for at, which in enumerate(order):
        front[8 * at : 8 * at + 8] = parts[which][:8]
        front[48 + at] = parts[which][8]
    back = np.zeros((32, PIX), kind)
    back[0:9] = parts[0]
    back[16:25] = parts[1]
    return front, back


def harmonic_basis(dir_x, dir_y, dir_z):
    square_x = dir_x * dir_x
    square_y = dir_y * dir_y
    square_z = dir_z * dir_z
    return [
        zero_term + 0.0 * dir_x,
        -first_term * dir_y,
        first_term * dir_z,
        -first_term * dir_x,
        second_terms[0] * dir_x * dir_y,
        second_terms[1] * dir_y * dir_z,
        second_terms[2] * (2.0 * square_z - square_x - square_y),
        second_terms[3] * dir_x * dir_z,
        second_terms[4] * (square_x - square_y),
        third_terms[0] * dir_y * (3.0 * square_x - square_y),
        third_terms[1] * dir_x * dir_y * dir_z,
        third_terms[2] * dir_y * (4.0 * square_z - square_x - square_y),
        third_terms[3] * dir_z * (2.0 * square_z - 3.0 * square_x - 3.0 * square_y),
        third_terms[4] * dir_x * (4.0 * square_z - square_x - square_y),
        third_terms[5] * dir_z * (square_x - square_y),
        third_terms[6] * dir_x * (square_x - 3.0 * square_y),
    ]


def iota(shape, axis):
    return lax.broadcasted_iota(jnp.int32, shape, axis)


def wave(mean):
    cycles = mean * (1.0 / SIDE)
    part = cycles - jnp.floor(cycles + 0.5)
    x = part * math.pi
    x2 = x * x
    sine = 1.0 / 6227020800.0
    for scale in (-1.0 / 39916800.0, 1.0 / 362880.0, -1.0 / 5040.0, 1.0 / 120.0, -1.0 / 6.0, 1.0):
        sine = sine * x2 + scale
    sine = sine * x
    cosine = -1.0 / 87178291200.0
    for scale in (
        1.0 / 479001600.0,
        -1.0 / 3628800.0,
        1.0 / 40320.0,
        -1.0 / 720.0,
        1.0 / 24.0,
        -0.5,
        1.0,
    ):
        cosine = cosine * x2 + scale
    return 2.0 * sine * cosine, 1.0 - 2.0 * sine * sine


def rotation(rows):
    length = jnp.sqrt(
        rows[0] * rows[0] + rows[1] * rows[1] + rows[2] * rows[2] + rows[3] * rows[3]
    )
    inverse = 1.0 / length
    w, x, y, z = [row * inverse for row in rows]
    matrix = [
        [1.0 - 2.0 * (y * y + z * z), 2.0 * (x * y - w * z), 2.0 * (x * z + w * y)],
        [2.0 * (x * y + w * z), 1.0 - 2.0 * (x * x + z * z), 2.0 * (y * z - w * x)],
        [2.0 * (x * z - w * y), 2.0 * (y * z + w * x), 1.0 - 2.0 * (x * x + y * y)],
    ]
    return inverse, (w, x, y, z), matrix


def halves(value):
    high = value.astype(bf16)
    low = (value - high.astype(f32)).astype(bf16)
    return high, low


def pick(table, lanes):
    return jnp.take_along_axis(table, lanes, axis=1)


def project_kernel(cam, wanted, positions, log_scales, rotations, logit, sh, send, aux, tab):
    cos_a, sin_a, cos_e, sin_e = cam[0, 0], cam[0, 1], cam[0, 2], cam[0, 3]
    right = (-sin_a, cos_a)
    upward = (-sin_e * cos_a, -sin_e * sin_a, cos_e)
    basis = harmonic_basis(cos_e * cos_a, cos_e * sin_a, sin_e)
    pos = [positions[i : i + 1, :] for i in range(3)]
    mean_x = right[0] * pos[0] + right[1] * pos[1]
    mean_y = upward[0] * pos[0] + upward[1] * pos[1] + upward[2] * pos[2]
    _, _, matrix = rotation([rotations[i : i + 1, :] for i in range(4)])
    scales = [jnp.exp(log_scales[i : i + 1, :]) for i in range(3)]
    first = [(right[0] * matrix[0][j] + right[1] * matrix[1][j]) * scales[j] for j in range(3)]
    second = [
        (upward[0] * matrix[0][j] + upward[1] * matrix[1][j] + upward[2] * matrix[2][j])
        * scales[j]
        for j in range(3)
    ]
    cov_a = first[0] * first[0] + first[1] * first[1] + first[2] * first[2] + dilation
    cov_b = first[0] * second[0] + first[1] * second[1] + first[2] * second[2]
    cov_c = second[0] * second[0] + second[1] * second[1] + second[2] * second[2] + dilation
    inverse = 1.0 / (cov_a * cov_c - cov_b * cov_b)
    c0, c1, c2 = cov_c * inverse, -cov_b * inverse, cov_a * inverse
    sa, ca = wave(mean_x)
    sb, cb = wave(mean_y)
    unit = KAPPA * LOG2E
    g0 = -LOG2E * jnp.log(1.0 + jnp.exp(-logit[...])) - (0.5 * unit) * (c0 + c2)
    cross = (-2.0 * unit) * c1
    half_x, half_y = (0.5 * unit) * c0, (0.5 * unit) * c2
    features = [
        g0,
        half_x * (1.0 - 2.0 * sa * sa),
        half_x * (2.0 * sa * ca),
        half_y * (1.0 - 2.0 * sb * sb),
        half_y * (2.0 * sb * cb),
        cross * ca * cb,
        -cross * ca * sb,
        -cross * sa * cb,
        cross * sa * sb,
    ]
    row48 = iota((48, 128), 0)
    weight = jnp.zeros((48, 128), f32)
    for k in range(16):
        weight = jnp.where(row48 // 3 == k, basis[k], weight)
    residue = row48 % 3
    masks = [jnp.where(residue == c, weight, 0.0) for c in range(3)]
    for block in range(LOCAL // 128):
        lanes = slice(128 * block, 128 * block + 128)
        piece = sh[:, lanes]
        for c in range(3):
            raw = 0.5 + jnp.sum(masks[c] * piece, axis=0, keepdims=True)
            aux[7 + c : 8 + c, lanes] = raw
            tab[9 + c : 10 + c, lanes] = jnp.maximum(raw, 0.0)
    for at, row in enumerate(features):
        tab[at : at + 1, :] = row
    for at, row in enumerate((ca, sa, cb, sb, c0, c1, c2)):
        aux[at : at + 1, 0:LOCAL] = row
    aux[10:16, 0:LOCAL] = jnp.zeros((6, LOCAL), f32)
    lane = iota((8, 128), 1)
    sub = iota((8, 128), 0)
    coef = jnp.zeros((8, 128), f32)
    for k in range(16):
        coef = jnp.where((lane // 3 == k) & (sub == 5 + lane % 3), basis[k], coef)

    def put(base, row, at, value):
        return jnp.where((sub == row) & (lane == at), value, base)

    for i in range(3):
        if i < 2:
            coef = put(coef, 0, 48 + i, right[i])
        coef = put(coef, 1, 48 + i, upward[i])
    at = 51
    for i in range(3):
        for j in range(i, 3):
            if j < 2:
                coef = put(coef, 2, at, 2.0 * right[i] * right[j])
            mixed = 0.0
            if i < 2:
                mixed = mixed + right[i] * upward[j]
            if j < 2:
                mixed = mixed + right[j] * upward[i]
            if i < 2 or j < 2:
                coef = put(coef, 3, at, 2.0 * mixed)
            coef = put(coef, 4, at, 2.0 * upward[i] * upward[j])
            at += 1
    aux[0:8, LOCAL : LOCAL + 128] = coef
    aux[8:16, LOCAL : LOCAL + 128] = jnp.zeros((8, 128), f32)

    upper = sub >= 4

    def gather_band(band, carry):
        ids = [jnp.broadcast_to(wanted[band, j : j + 1, :], (8, 128)) for j in range(4)]
        spots = [value & 127 for value in ids]
        blocks = [lax.shift_right_logical(value, 7) for value in ids]
        acc = [jnp.zeros((8, 128), f32)] * 4
        low = [jnp.zeros((8, 128), f32)] * 4
        for block in range(LOCAL // 128):
            front = tab[0:8, 128 * block : 128 * block + 128]
            for j in range(4):
                acc[j] = jnp.where(blocks[j] == block, pick(front, spots[j]), acc[j])
        for pair in range(LOCAL // 256):
            first_half = tab[8:12, 256 * pair : 256 * pair + 128]
            second_half = tab[8:12, 256 * pair + 128 : 256 * pair + 256]
            both = jnp.concatenate([first_half, second_half], axis=0)
            which = jnp.where(upper, 2 * pair + 1, 2 * pair)
            for j in range(4):
                low[j] = jnp.where(blocks[j] == which, pick(both, spots[j]), low[j])
        for j in range(4):
            send[band, 8 * j : 8 * j + 8, :] = acc[j]
            whole = low[j] + pltpu.roll(low[j], 4, 0)
            send[band, 32 + 4 * j : 36 + 4 * j, :] = whole[0:4]
        return carry

    lax.fori_loop(0, OWNERS, gather_band, 0)


def blend_kernel(
    table,
    slots,
    order,
    counts,
    target,
    front,
    back,
    images,
    answer,
    lhs,
    colours,
    alpha_ref,
    weight_ref,
    high_ref,
    low_ref,
    ids_ref,
    grads,
    total,
):
    lane = iota((8, 128), 1)
    sub = iota((8, 128), 0)
    upper = sub >= 4
    diagonal = sub == (lane & 7)
    diag_wide = iota((8, CHUNK), 0) == (iota((8, CHUNK), 1) & 7)
    total[...] = jnp.zeros_like(total)

    def one_group(group, loss):
        start = pl.multiple_of(group * GROUP, GROUP)
        limit = jnp.broadcast_to(counts[pl.ds(group, 1), :], (8, 128))
        own = slots[pl.ds(start, GROUP), :]
        sequence = order[pl.ds(start, GROUP), :]
        ordered = []
        for half in range(2):
            seq = sequence[:, 128 * half : 128 * half + 128]
            spot = seq & 127
            ordered.append(
                jnp.where(seq < 128, pick(own[:, 0:128], spot), pick(own[:, 128:256], spot))
            )
        for half in range(2):

            def gather_part(part, carry, half=half):
                spots, blocks = [], []
                for j in range(4):
                    base = (part * 4 + j) * 16
                    value = pick(ordered[half], base + lax.shift_right_logical(lane, 3))
                    value = jnp.sum(jnp.where(diagonal, value, 0), axis=0, keepdims=True)
                    value = jnp.broadcast_to(value, (8, 128))
                    at = pl.multiple_of((half * 8 + part * 4 + j) * 128, 128)
                    ids_ref[:, pl.ds(at, 128)] = value
                    spots.append(value & 127)
                    blocks.append(lax.shift_right_logical(value, 7))
                acc = [jnp.zeros((8, 128), f32)] * 4
                low = [jnp.zeros((8, 128), f32)] * 4
                for block in range(64):
                    rows = table[block // 4, 8 * (block % 4) : 8 * (block % 4) + 8, :]
                    for j in range(4):
                        acc[j] = jnp.where(blocks[j] == block, pick(rows, spots[j]), acc[j])
                for pair in range(32):
                    rows = table[pair // 2, 32 + 8 * (pair % 2) : 40 + 8 * (pair % 2), :]
                    which = jnp.where(upper, 2 * pair + 1, 2 * pair)
                    for j in range(4):
                        low[j] = jnp.where(blocks[j] == which, pick(rows, spots[j]), low[j])
                for j in range(4):
                    at = pl.multiple_of((half * 8 + part * 4 + j) * 128, 128)
                    position = (half * 8 + part * 4 + j) * 16 + lax.shift_right_logical(lane, 3)
                    dead = position >= limit
                    value = jnp.where(dead & (sub == 0), DEAD, acc[j])
                    rest = low[j] + pltpu.roll(low[j], 4, 0)
                    p1 = value.astype(bf16).astype(f32)
                    p2 = (value - p1).astype(bf16).astype(f32)
                    p3 = value - p1 - p2
                    last = jnp.broadcast_to(rest[0:1], (8, 128))
                    q1 = last.astype(bf16).astype(f32)
                    q2 = (last - q1).astype(bf16).astype(f32)
                    q3 = last - q1 - q2
                    tail = jnp.where(
                        sub < 3,
                        q1,
                        jnp.where(sub < 5, q2, jnp.where(sub == 5, q3, 0.0)),
                    )
                    tops, lows = [], []
                    for c in range(3):
                        colour = jnp.where(
                            diagonal, jnp.broadcast_to(rest[1 + c : 2 + c], (8, 128)), 0.0
                        )
                        top = colour.astype(bf16).astype(f32)
                        tops.append(top)
                        lows.append(colour - top)
                    stack = jnp.concatenate(
                        [p1, p1, p1, p2, p2, p3, tail] + tops + tops + lows, axis=0
                    )
                    lhs[pl.ds(at, 128), :] = stack.T.astype(bf16)
                    colours[:, pl.ds(at, 128)] = jnp.concatenate(tops + lows, axis=0).astype(bf16)
                return carry

            lax.fori_loop(0, 2, gather_part, 0)

        def forward(chunk, carry):
            passing, picture = carry
            at = pl.multiple_of(chunk * CHUNK, CHUNK)
            power = jnp.dot(lhs[pl.ds(at, CHUNK), :], front[...], preferred_element_type=f32)
            alpha = jnp.exp2(power)
            alpha_ref[pl.ds(at, CHUNK), :] = alpha
            pieces = []
            for k in range(CHUNK_K):
                piece = alpha[8 * k : 8 * k + 8] * passing
                passing = passing - piece
                pieces.append(piece)
            weight = jnp.concatenate(pieces, axis=0)
            weight_ref[pl.ds(at, CHUNK), :] = weight
            high, low = halves(weight)
            high_ref[pl.ds(at, CHUNK), :] = high
            low_ref[pl.ds(at, CHUNK), :] = low
            own = colours[:, pl.ds(at, CHUNK)]
            picture = picture + jnp.dot(own, high, preferred_element_type=f32)
            picture = picture + jnp.dot(own, low, preferred_element_type=f32)
            return passing, picture

        _, picture = lax.fori_loop(
            0, CHUNKS, forward, (jnp.ones((8, PIX), f32), jnp.zeros((48, PIX), f32))
        )
        picture = picture[0:24] + picture[24:48]
        errors = []
        for c in range(3):
            image = picture[8 * c : 8 * c + 8]
            images[pl.ds(start, GROUP), c, :] = image
            errors.append(image - target[pl.ds(start, GROUP), c, :])
        for error in errors:
            square = error * error
            loss = loss + square[:, 0:128] + square[:, 128:256]
        error = jnp.concatenate(errors, axis=0)
        top = error.astype(bf16).astype(f32)
        bottom = error - top
        right = jnp.concatenate([jnp.zeros((56, PIX), f32), top, bottom, top], axis=0)
        right = right.astype(bf16)
        errs = jnp.concatenate([top, bottom], axis=0).astype(bf16)

        def backward(step, behind):
            at = pl.multiple_of((CHUNKS - 1 - step) * CHUNK, CHUNK)
            gain = jnp.dot(lhs[pl.ds(at, CHUNK), :], right, preferred_element_type=f32)
            alpha = alpha_ref[pl.ds(at, CHUNK), :]
            weight = weight_ref[pl.ds(at, CHUNK), :]
            pieces = [None] * CHUNK_K
            for k in reversed(range(CHUNK_K)):
                rows = slice(8 * k, 8 * k + 8)
                gap = gain[rows] - behind
                pieces[k] = weight[rows] * gap
                behind = behind + alpha[rows] * gap
            high, low = halves(jnp.concatenate(pieces, axis=0))
            contract = (((1,), (1,)), ((), ()))
            shape = lax.dot_general(back[...], high, contract, preferred_element_type=f32)
            shape = shape + lax.dot_general(back[...], low, contract, preferred_element_type=f32)
            shape = shape[0:16] + shape[16:32]
            paint = lax.dot_general(
                errs, high_ref[pl.ds(at, CHUNK), :], contract, preferred_element_type=f32
            )
            paint = paint + lax.dot_general(
                errs, low_ref[pl.ds(at, CHUNK), :], contract, preferred_element_type=f32
            )
            paint = paint[0:24] + paint[24:48]
            second = shape[8:16]
            row = iota((8, CHUNK), 0)
            for c in range(3):
                own = jnp.where(diag_wide, paint[8 * c : 8 * c + 8], 0.0)
                own = jnp.sum(own, axis=0, keepdims=True)
                second = jnp.where(row == 1 + c, jnp.broadcast_to(own, (8, CHUNK)), second)
            found = jnp.concatenate([shape[0:8], second], axis=0)
            high, low = halves(found)
            grads[0, :, pl.ds(at, CHUNK)] = high
            grads[1, :, pl.ds(at, CHUNK)] = low
            return behind

        lax.fori_loop(0, CHUNKS, backward, jnp.zeros((8, PIX), f32))

        def scatter(step, carry):
            at = pl.multiple_of(step * SCAT, SCAT)
            ids = ids_ref[:, pl.ds(at, SCAT)]
            block = lax.shift_right_logical(ids, 8)
            spot = ids & 255
            high = grads[0, :, pl.ds(at, SCAT)]
            low = grads[1, :, pl.ds(at, SCAT)]
            tops, lows = [], []
            for h in range(32):
                mask = jnp.where(block == h, 1.0, 0.0)
                mask = jnp.concatenate([mask, mask], axis=0).astype(bf16)
                tops.append(mask * high)
                lows.append(mask * low)
            left = jnp.concatenate(
                [jnp.concatenate(tops, axis=0), jnp.concatenate(lows, axis=0)], axis=1
            )
            row = iota((8, SCAT), 0)
            hot = jnp.concatenate(
                [jnp.where(spot == row + 8 * s, 1.0, 0.0) for s in range(32)], axis=0
            ).astype(bf16)
            hot = jnp.concatenate([hot, hot], axis=1)
            total[...] += lax.dot_general(
                left, hot, (((1,), (1,)), ((), ())), preferred_element_type=f32
            )
            return carry

        lax.fori_loop(0, ROWS // SCAT, scatter, 0)
        return loss

    loss = lax.fori_loop(0, GROUPS, one_group, jnp.zeros((8, 128), f32))
    for owner in range(OWNERS):
        for j in range(4):
            base = 16 * (2 * owner + j // 2)
            lanes = slice(128 * (j % 2), 128 * (j % 2) + 128)
            answer[owner, 8 * j : 8 * j + 8, :] = total[base : base + 8, lanes]
            answer[owner, 32 + 4 * j : 36 + 4 * j, :] = total[base + 8 : base + 12, lanes]
        answer[owner, 48:56, :] = loss


def collect_kernel(back, wanted, aux, out, loss, total):
    total[...] = jnp.zeros_like(total)

    def one_band(band, squares):
        tops, lows, blocks, spots = [], [], [], []
        for j in range(4):
            value = jnp.concatenate(
                [
                    back[band, 8 * j : 8 * j + 8, :],
                    back[band, 32 + 4 * j : 36 + 4 * j, :],
                    jnp.zeros((4, 128), f32),
                ],
                axis=0,
            )
            high, low = halves(value)
            tops.append(high)
            lows.append(low)
            ids = jnp.broadcast_to(wanted[band, j : j + 1, :], (8, 128))
            blocks.append(lax.shift_right_logical(ids, 8))
            spots.append(ids & 255)
        high = jnp.concatenate(tops, axis=1)
        low = jnp.concatenate(lows, axis=1)
        block = jnp.concatenate(blocks, axis=1)
        spot = jnp.concatenate(spots, axis=1)
        left_top, left_low = [], []
        for h in range(16):
            mask = jnp.where(block == h, 1.0, 0.0)
            mask = jnp.concatenate([mask, mask], axis=0).astype(bf16)
            left_top.append(mask * high)
            left_low.append(mask * low)
        left = jnp.concatenate(
            [jnp.concatenate(left_top, axis=0), jnp.concatenate(left_low, axis=0)], axis=1
        )
        row = iota((8, CAP), 0)
        hot = jnp.concatenate(
            [jnp.where(spot == row + 8 * s, 1.0, 0.0) for s in range(32)], axis=0
        ).astype(bf16)
        hot = jnp.concatenate([hot, hot], axis=1)
        total[...] += lax.dot_general(
            left, hot, (((1,), (1,)), ((), ())), preferred_element_type=f32
        )
        return squares + back[band, 48:56, :]

    squares = lax.fori_loop(0, OWNERS, one_band, jnp.zeros((8, 128), f32))
    whole = jnp.sum(jnp.sum(squares, axis=1, keepdims=True), axis=0, keepdims=True)
    loss[...] = whole * (1.0 / (TILES * OWNERS * PIX * 3))
    for h in range(16):
        lanes = slice(256 * h, 256 * h + 256)
        gain = [total[16 * h + c : 16 * h + c + 1, :] for c in range(12)]
        ca, sa, cb, sb, c0, c1, c2 = [aux[c : c + 1, lanes] for c in range(7)]
        cos_x, sin_x = 1.0 - 2.0 * sa * sa, 2.0 * sa * ca
        cos_y, sin_y = 1.0 - 2.0 * sb * sb, 2.0 * sb * cb
        d0 = (0.5 * KAPPA) * (cos_x * gain[1] + sin_x * gain[2] - gain[0])
        d2 = (0.5 * KAPPA) * (cos_y * gain[3] + sin_y * gain[4] - gain[0])
        cacb, casb, sacb, sasb = ca * cb, ca * sb, sa * cb, sa * sb
        d1 = (2.0 * KAPPA) * (casb * gain[6] - cacb * gain[5] + sacb * gain[7] - sasb * gain[8])
        twist = (2.0 * KAPPA) * c1
        da = KAPPA * c0 * (cos_x * gain[2] - sin_x * gain[1]) + twist * (
            sacb * gain[5] - sasb * gain[6] + cacb * gain[7] - casb * gain[8]
        )
        db = KAPPA * c2 * (cos_y * gain[4] - sin_y * gain[3]) + twist * (
            casb * gain[5] + cacb * gain[6] - sasb * gain[7] - sacb * gain[8]
        )
        out[0:1, lanes] = TURN * da
        out[1:2, lanes] = TURN * db
        out[2:3, lanes] = -(c0 * c0 * d0 + c0 * c1 * d1 + c1 * c1 * d2)
        out[3:4, lanes] = -(c0 * c1 * d0 + 0.5 * (c0 * c2 + c1 * c1) * d1 + c1 * c2 * d2)
        out[4:5, lanes] = -(c1 * c1 * d0 + c1 * c2 * d1 + c2 * c2 * d2)
        for c in range(3):
            raw = aux[7 + c : 8 + c, lanes]
            share = jnp.where(raw > 0.0, 1.0, jnp.where(raw == 0.0, 0.5, 0.0))
            out[5 + c : 6 + c, lanes] = share * gain[9 + c]
        spot = LOCAL + 256 * (h % 2)
        out[h // 2 : h // 2 + 1, spot : spot + 256] = gain[0]
    out[:, LOCAL + 512 :] = aux[0:8, LOCAL : LOCAL + 128]


def finish_kernel(
    gathered, log_scales, rotations, logit, grad_pos, grad_log, grad_rot, grad_op, grad_sh, work
):
    coef = jnp.concatenate([gathered[view, :, LOCAL + 512 :] for view in range(VIEWS)], axis=0)
    high, low = halves(coef.T)
    left = jnp.concatenate([high, low, high], axis=1)[0:64]
    for block in range(LOCAL // 512):
        lanes = slice(512 * block, 512 * block + 512)
        value = jnp.concatenate([gathered[view, :, lanes] for view in range(VIEWS)], axis=0)
        top, bottom = halves(value)
        right = jnp.concatenate([top, top, bottom], axis=0)
        work[:, lanes] = jnp.dot(left, right, preferred_element_type=f32)
    grad_sh[...] = work[0:48, :]
    grad_pos[...] = work[48:51, :]
    shade = gathered[0, :, LOCAL : LOCAL + 512]
    for view in range(1, VIEWS):
        shade = shade + gathered[view, :, LOCAL : LOCAL + 512]
    shade = jnp.concatenate([shade[s : s + 1, :] for s in range(8)], axis=1)
    grad_op[...] = shade / (1.0 + jnp.exp(logit[...]))
    k00, k01, k02, k11, k12, k22 = [work[51 + i : 52 + i, :] for i in range(6)]
    spread = [[k00, k01, k02], [k01, k11, k12], [k02, k12, k22]]
    inverse, (w, x, y, z), matrix = rotation([rotations[i : i + 1, :] for i in range(4)])
    d = [[None] * 3 for _ in range(3)]
    for j in range(3):
        scale = jnp.exp(log_scales[j : j + 1, :])
        square = scale * scale
        grad = None
        for i in range(3):
            value = (
                spread[i][0] * matrix[0][j]
                + spread[i][1] * matrix[1][j]
                + spread[i][2] * matrix[2][j]
            ) * square
            d[i][j] = value
            term = value * matrix[i][j]
            grad = term if grad is None else grad + term
        grad_log[j : j + 1, :] = grad
    dw = 2.0 * (x * (d[2][1] - d[1][2]) + y * (d[0][2] - d[2][0]) + z * (d[1][0] - d[0][1]))
    dx = 2.0 * (
        y * (d[0][1] + d[1][0])
        + z * (d[0][2] + d[2][0])
        + w * (d[2][1] - d[1][2])
        - 2.0 * x * (d[1][1] + d[2][2])
    )
    dy = 2.0 * (
        x * (d[0][1] + d[1][0])
        + z * (d[1][2] + d[2][1])
        + w * (d[0][2] - d[2][0])
        - 2.0 * y * (d[0][0] + d[2][2])
    )
    dz = 2.0 * (
        x * (d[0][2] + d[2][0])
        + y * (d[1][2] + d[2][1])
        + w * (d[1][0] - d[0][1])
        - 2.0 * z * (d[0][0] + d[1][1])
    )
    along = w * dw + x * dx + y * dy + z * dz
    for at, (part, unit) in enumerate(((dw, w), (dx, x), (dy, y), (dz, z))):
        grad_rot[at : at + 1, :] = (part - unit * along) * inverse


def whole():
    return pl.BlockSpec(memory_space=pltpu.VMEM)


def params(mega):
    return pltpu.CompilerParams(vmem_limit_bytes=mega << 20)


def shape(*dims):
    return jax.ShapeDtypeStruct(dims, f32)


def local(
    positions,
    log_scales,
    rotations,
    opacity_logit,
    sh_coeffs,
    view_angles,
    target,
    fetch_index,
    tile_slots,
    depth_order,
    block_count,
):
    wanted = lax.all_to_all(
        fetch_index.reshape(OWNERS, 4, 128), "band", split_axis=0, concat_axis=0, tiled=True
    )
    azimuth, elevation = view_angles[0, 0], view_angles[0, 1]
    cam = jnp.stack(
        [jnp.cos(azimuth), jnp.sin(azimuth), jnp.cos(elevation), jnp.sin(elevation)]
    ).reshape(1, 4)
    counts = jnp.tile(block_count.reshape(GROUPS, GROUP), (1, 16))
    front, back = pixel_tables()
    send, aux = pl.pallas_call(
        project_kernel,
        out_shape=(shape(OWNERS, SEND_ROWS, 128), shape(16, LOCAL + 128)),
        in_specs=[pl.BlockSpec(memory_space=pltpu.SMEM)] + [whole()] * 6,
        out_specs=(whole(), whole()),
        scratch_shapes=[pltpu.VMEM((16, LOCAL), f32)],
        compiler_params=params(32),
        name="project",
    )(cam, wanted, positions, log_scales, rotations, opacity_logit, sh_coeffs)
    table = lax.all_to_all(send, "band", split_axis=0, concat_axis=0, tiled=True)
    images, answer = pl.pallas_call(
        blend_kernel,
        out_shape=(shape(TILES, 3, PIX), shape(OWNERS, BACK_ROWS, 128)),
        in_specs=[whole()] * 7,
        out_specs=(whole(), whole()),
        scratch_shapes=[
            pltpu.VMEM((ROWS, 128), bf16),
            pltpu.VMEM((48, ROWS), bf16),
            pltpu.VMEM((ROWS, PIX), f32),
            pltpu.VMEM((ROWS, PIX), f32),
            pltpu.VMEM((ROWS, PIX), bf16),
            pltpu.VMEM((ROWS, PIX), bf16),
            pltpu.VMEM((8, ROWS), jnp.int32),
            pltpu.VMEM((2, 16, ROWS), bf16),
            pltpu.VMEM((512, 256), f32),
        ],
        compiler_params=params(48),
        name="blend",
    )(
        table,
        tile_slots[0],
        depth_order[0],
        counts,
        target[0],
        jnp.asarray(front),
        jnp.asarray(back),
    )
    returned = lax.all_to_all(answer, "band", split_axis=0, concat_axis=0, tiled=True)
    share, loss = pl.pallas_call(
        collect_kernel,
        out_shape=(shape(8, WIDE), shape(1, 1)),
        in_specs=[whole()] * 3,
        out_specs=(whole(), whole()),
        scratch_shapes=[pltpu.VMEM((256, 256), f32)],
        compiler_params=params(32),
        name="collect",
    )(returned, wanted, aux)
    gathered = lax.all_gather(share, "view", axis=0, tiled=False)
    grads = pl.pallas_call(
        finish_kernel,
        out_shape=(
            shape(3, LOCAL),
            shape(3, LOCAL),
            shape(4, LOCAL),
            shape(1, LOCAL),
            shape(48, LOCAL),
        ),
        in_specs=[whole()] * 4,
        out_specs=(whole(),) * 5,
        scratch_shapes=[pltpu.VMEM((64, LOCAL), f32)],
        compiler_params=params(32),
        name="finish",
    )(gathered, log_scales, rotations, opacity_logit)
    return (images[None], loss.reshape(1)) + tuple(grads)


def solution(mesh):
    in_specs = (
        P(None, "band"),
        P(None, "band"),
        P(None, "band"),
        P(None, "band"),
        P(None, "band"),
        P("view", None),
        P("view", "band", None, None),
        P("view", "band", None, None),
        P("view", "band", None),
        P("view", "band", None),
        P("view", "band"),
    )
    out_specs = (
        P("view", "band", None, None),
        P("view"),
        P(None, "band"),
        P(None, "band"),
        P(None, "band"),
        P(None, "band"),
        P(None, "band"),
    )
    return jax.shard_map(local, mesh=mesh, in_specs=in_specs, out_specs=out_specs, check_vma=False)
```

time: 1580 us -> 195 us (0.12)
  matrix products: 543 us -> 0 us
  local copies, waits for them, and re-layouts: 483 us -> 9.92 us
  other arithmetic: 335 us -> 0.74 us
  Pallas kernels: 0 us -> 108 us
  waiting for transfers between devices: 81 us -> 33.3 us
  starting transfers between devices: 58.8 us -> 13.1 us
  blocking collectives: 33.6 us -> 12.2 us
    dot_general x60 -> x0, matrix products: 543 us -> none  [the longest x24 316 us: blend_tile(): jnp.dot(log_keep, strict_upper, precision=highest, preferred_element_type...]
    gather x31 -> x0, local copies, waits for them, and re-layouts: 356 us -> none  [the longest x5 197 us: local(): picked = [array[:, wanted_flat] for array in params]]
    scatter-add x6 -> x0, other arithmetic: 295 us -> none  [the longest x5 227 us: local(): jnp.zeros((piece.shape[0], local_total), jnp.float32).at[:, wanted_flat]]
    pallas_call x0 -> x4, Pallas kernels: none -> 108 us  [the longest x1 88.5 us: local(): pl.pallas_call(blend_kernel, out_shape=(shape(TILES, 3, PIX), shape(OWNER...]
    all_to_all x11 -> x2, starting transfers between devices: 58.7 us -> 13.1 us  [the longest x1 8.6 us: local(): lax.all_to_all(fetch_index.reshape(OWNERS, 4, 128), 'band', split_axis=0,...]
    psum x2 -> x0, waiting for transfers between devices: 40.3 us -> none  [local(): lax.psum((partial_sums[0], partial_sums[1], partial_sums[2], partial_sums...]
    psum x1 -> x0, blocking collectives: 33.6 us -> none  [local(): whole = lax.psum(squares, 'band')]
    all_to_all x11 -> x2, waiting for transfers between devices: 40.7 us -> 8.8 us  [the longest x1 6.6 us: local(): lax.all_to_all(send, 'band', split_axis=0, concat_axis=0, tiled=True)]
  transfers between devices with their start and end apart: 13 -> 3, of which waited for: 8 -> 3; matrix products, arithmetic and copies ran while one was open for 33% -> 2% of each run, Pallas kernels for 0% -> 0%
where the time goes in v1:
time: 195 us; the launch traced here: 194 us
  Pallas kernels  108 us (55%)
  waiting for transfers between devices  33.3 us (17%)
  between operations  17.1 us (9%)
  starting transfers between devices  13.1 us (7%)
  blocking collectives  12.2 us (6%)
  local copies, waits for them, and re-layouts  9.92 us (5%)
    pallas_call x1, Pallas kernels, local(): pl.pallas_call(blend_kernel, out_shape=(shape(TILES, 3, PIX), shape(OWNER...  88.5 us
    all_gather x1, waiting for transfers between devices, local(): gathered = lax.all_gather(share, 'view', axis=0, tiled=False)  24.5 us
    all_to_all x1, blocking collectives, local(): lax.all_to_all(answer, 'band', split_axis=0, concat_axis=0, tiled=True)  12.2 us
    pallas_call x1, Pallas kernels, local(): pl.pallas_call(project_kernel, out_shape=(shape(OWNERS, SEND_ROWS, 128),...  11.5 us
    all_to_all x1, starting transfers between devices, local(): lax.all_to_all(fetch_index.reshape(OWNERS, 4, 128), 'band', split_axis=0,...  8.6 us
    unnamed x33, local copies, waits for them, and re-layouts  7 us
    all_to_all x1, waiting for transfers between devices, local(): lax.all_to_all(send, 'band', split_axis=0, concat_axis=0, tiled=True)  6.6 us
    pallas_call x1, Pallas kernels, local(): pl.pallas_call(collect_kernel, out_shape=(shape(8, WIDE), shape(1, 1)), i...  6.42 us
  transfers between devices with their start and end apart: 3, of which 3 were waited for; matrix products, arithmetic and copies ran while one was open for 2% of the time, Pallas kernels for 0%

profile of v1, /device:TPU:1, one launch (start us, length us, event | category | flops | bytes accessed | tf_op | source)
XLA Modules:
  0.0 194.2 jit_solution(5541379942741598744)
XLA Ops:
  7.2 1.4 reshape.36
  8.6 8.6 %all-to-all-start = ((s32[16,4,128]{2,1,0:T(4,128)}), s32[16,4,128]{2,1,0:T(4,128)S(1)}, u32[]{:S(2)}, u32[]{:S(2)}) async-start(s32[16,4,128]{2,1,0:T(4,128)} %reshape.36), calls=%async_computation | async-start | bytes 65536 | tf_op jit(solution)/shard_map/all_to_all | solution.py:661
  17.2 1.3 fusion
  21.5 2.2 %all-to-all-done.wanted = s32[16,4,128]{2,1,0:T(4,128)S(1)} async-done(((s32[16,4,128]{2,1,0:T(4,128)}), s32[16,4,128]{2,1,0:T(4,128)S(1)}, u32[]{:S(2)}, u32[]{:S(2)}) %all-to-all-start) | async-done | bytes 32800 | tf_op jit(solution)/shard_map/all_to_all | solution.py:661
  23.7 1.1 copy-done.1
  24.9 0.8 copy-done.2
  25.7 0.8 copy-done.4
  26.5 0.7 copy-done.6
  27.3 0.8 copy-done.8
  28.1 11.5 %project.1 = (f32[16,48,128]{2,1,0:T(8,128)}, f32[16,4224]{1,0:T(8,128)S(1)}) custom-call(f32[1,4]{1,0:T(1,128)S(1)} %maximum_bitcast_fusion.cam, s32[16,4,128]{2,1,0:T(4,128)S(1)} %all-to-all-done.wanted, f32[3,4096]{1,0:T(4,128)S(1)} %copy-done.8, f32[3,4096]{1,0:T(4,128)S(1)} %copy-done.2, f32[4,4096]{1,0:T(4,128)S(1)} %copy-done.4, ...), custom_call_target="tpu_custom_call" | custom-call | tf_op jit(solution)/shard_map/project/pallas_call | solution.py:670
  39.6 4.5 %all-to-all-start.1 = ((f32[16,48,128]{2,1,0:T(8,128)}), f32[16,48,128]{2,1,0:T(8,128)S(1)}, u32[]{:S(2)}, u32[]{:S(2)}) async-start(f32[16,48,128]{2,1,0:T(8,128)} %get-tuple-element.18), calls=%async_computation.1 | async-start | bytes 786432 | tf_op jit(solution)/shard_map/all_to_all | solution.py:679
  44.1 0.5 broadcast.5
  44.6 0.7 reduce.3
  45.3 0.1 tile.10
  45.4 0.1 tile.12.counts
  45.5 0.1 copy.25
  45.6 6.6 %all-to-all-done.1.table = f32[16,48,128]{2,1,0:T(8,128)S(1)} async-done(((f32[16,48,128]{2,1,0:T(8,128)}), f32[16,48,128]{2,1,0:T(8,128)S(1)}, u32[]{:S(2)}, u32[]{:S(2)}) %all-to-all-start.1) | async-done | bytes 393248 | tf_op jit(solution)/shard_map/all_to_all | solution.py:679
  52.2 88.5 %blend.1 = (f32[48,3,256]{2,1,0:T(4,128)S(1)}, f32[16,56,128]{2,1,0:T(8,128)S(1)}) custom-call(f32[16,48,128]{2,1,0:T(8,128)S(1)} %all-to-all-done.1.table, s32[48,256]{1,0:T(8,128)S(1)} %bitcast.19, s32[48,256]{1,0:T(8,128)S(1)} %bitcast.20, s32[6,128]{1,0:T(8,128)S(1)} %tile.12.counts, f32[48,3,256]{2,1,0:T(4,128)S(1)} %bitcast.17, ...), custom_call_target="tpu_custom_call" | custom-call | tf_op jit(solution)/shard_map/blend/pallas_call | solution.py:680
  140.7 12.2 %all_to_all.15.back = f32[16,56,128]{2,1,0:T(8,128)S(1)} all-to-all(f32[16,56,128]{2,1,0:T(8,128)S(1)} %get-tuple-element.20), channel_id=1, replica_groups=mesh['view'=8,'band'=16] {'band'}, dimensions={0} | all-to-all | bytes 917504 | tf_op jit(solution)/shard_map/all_to_all | solution.py:707
  152.9 6.4 %collect.1 = (f32[8,4736]{1,0:T(8,128)}, f32[1,1]{1,0:T(1,128)}) custom-call(f32[16,56,128]{2,1,0:T(8,128)S(1)} %all_to_all.15.back, s32[16,4,128]{2,1,0:T(4,128)S(1)} %all-to-all-done.wanted, f32[16,4224]{1,0:T(8,128)S(1)} %get-tuple-element.21.aux), custom_call_target="tpu_custom_call" | custom-call | tf_op jit(solution)/shard_map/collect/pallas_call | solution.py:708
  159.4 0.7 copy.23
  160.1 24.5 %all-gather.3.cloned.1.call-done = f32[64,4736]{1,0:T(8,128)} async-done(((f32[8,4736]{1,0:T(8,128)}), f32[64,4736]{1,0:T(8,128)}) %all-gather.3.cloned.1.call-update) | async-done | bytes 1212432 | tf_op jit(solution)/shard_map/all_gather | solution.py:717
  184.6 1.3 copy-done
  185.8 1.5 finish.1
  (28 shorter events, 0.2 us)
Async XLA Ops:
  7.2 45.0 %copy-start.9 = (bf16[128,256]{1,0:T(8,128)(2,1)S(1)}, bf16[128,256]{1,0:T(8,128)(2,1)}, u32[]{:S(2)}) copy-start(bf16[128,256]{1,0:T(8,128)(2,1)} %constant.4.clone.front) | copy-start | bytes 196612
  7.2 45.0 %copy-start.12 = (bf16[32,256]{1,0:T(8,128)(2,1)S(1)}, bf16[32,256]{1,0:T(8,128)(2,1)}, u32[]{:S(2)}) copy-start(bf16[32,256]{1,0:T(8,128)(2,1)} %constant.5.clone.back) | copy-start | bytes 49156
  7.2 37.4 %copy-start.14 = (s32[1,48]{1,0:T(1,128)S(1)}, s32[1,48]{1,0:T(1,128)}, u32[]{:S(2)}) copy-start(s32[1,48]{1,0:T(1,128)} %param.23) | copy-start | bytes 580
  7.2 45.0 %copy-start.10 = (s32[1,48,256]{2,1,0:T(8,128)S(1)}, s32[1,48,256]{2,1,0:T(8,128)}, u32[]{:S(2)}) copy-start(s32[1,48,256]{2,1,0:T(8,128)} %param.21) | copy-start | bytes 147460
  8.6 15.1 %all-to-all-start = ((s32[16,4,128]{2,1,0:T(4,128)}), s32[16,4,128]{2,1,0:T(4,128)S(1)}, u32[]{:S(2)}, u32[]{:S(2)}) async-start(s32[16,4,128]{2,1,0:T(4,128)} %reshape.36), calls=%async_computation | async-start | bytes 65536 | tf_op jit(solution)/shard_map/all_to_all | solution.py:661
  23.7 1.1 copy-start.1
  24.9 0.8 copy-start.2
  25.7 0.8 copy-start.4
  26.5 0.7 copy-start.6
  27.3 0.8 copy-start.8
  28.1 17.4 %copy-start.13 = (f32[1,48,3,256]{3,1,2,0:T(8,128)S(1)}, f32[1,48,3,256]{3,1,2,0:T(8,128)}, u32[]{:S(2)}) copy-start(f32[1,48,3,256]{3,1,2,0:T(8,128)} %param.19) | copy-start | bytes 442372
  28.1 24.1 %copy-start.11 = (s32[1,48,256]{2,1,0:T(8,128)S(1)}, s32[1,48,256]{2,1,0:T(8,128)}, u32[]{:S(2)}) copy-start(s32[1,48,256]{2,1,0:T(8,128)} %param.22) | copy-start | bytes 147460
  39.6 12.6 %all-to-all-start.1 = ((f32[16,48,128]{2,1,0:T(8,128)}), f32[16,48,128]{2,1,0:T(8,128)S(1)}, u32[]{:S(2)}, u32[]{:S(2)}) async-start(f32[16,48,128]{2,1,0:T(8,128)} %get-tuple-element.18), calls=%async_computation.1 | async-start | bytes 786432 | tf_op jit(solution)/shard_map/all_to_all | solution.py:679
  44.0 140.5 %all-gather.3.cloned.1.call-start = ((), (), s32[]{:S(2)}) async-start(), calls=%async_computation.3 | async-start | bytes 1363968 | tf_op jit(solution)/shard_map/all_gather | solution.py:717
  140.7 43.8 %copy-start.3 = (f32[3,4096]{1,0:T(4,128)S(1)}, f32[3,4096]{1,0:T(4,128)}, u32[]{:S(2)}) copy-start(f32[3,4096]{1,0:T(4,128)} %log_scales.3) | copy-start | bytes 147460
  140.7 43.8 %copy-start.5 = (f32[4,4096]{1,0:T(4,128)S(1)}, f32[4,4096]{1,0:T(4,128)}, u32[]{:S(2)}) copy-start(f32[4,4096]{1,0:T(4,128)} %rotations.3) | copy-start | bytes 196612
  140.7 43.8 %copy-start.7 = (f32[1,4096]{1,0:T(1,128)S(1)}, f32[1,4096]{1,0:T(1,128)}, u32[]{:S(2)}) copy-start(f32[1,4096]{1,0:T(1,128)} %logit.3) | copy-start | bytes 49156
  184.6 1.3 copy-start
Sparse Core Ops, SparseCore 0:
  159.5 24.9 all-gather.2

commit v2 on v1

--- a/solution.py
+++ b/solution.py
@@ -24,6 +24,13 @@
 CHUNK_K = CHUNK // GROUP
 CHUNKS = ROWS // CHUNK
 SCAT = 512
+TOGETHER = 3
+UNROLL_GATHER = 4
+UNROLL_FORWARD = 4
+UNROLL_BACKWARD = 8
+UNROLL_SCATTER = 4
+UNROLL_SELECT = 4
+UNROLL_COLLECT = 4
 TURN = 2.0 * math.pi / SIDE
 KAPPA = 0.5 / (TURN * TURN)
 LOG2E = 1.4426950408889634
@@ -81,11 +88,11 @@
         part = rest.astype(kind)
         parts.append(part)
         rest = rest - part.astype(np.float64)
-    order = (0, 1, 2, 0, 1, 0)
+    order = (0, 1, 2, 0, 1)
     front = np.zeros((128, PIX), kind)
     for at, which in enumerate(order):
         front[8 * at : 8 * at + 8] = parts[which][:8]
-        front[48 + at] = parts[which][8]
+        front[40 + at] = parts[which][8]
     back = np.zeros((32, PIX), kind)
     back[0:9] = parts[0]
     back[16:25] = parts[1]
@@ -167,7 +174,7 @@
     return jnp.take_along_axis(table, lanes, axis=1)
 
 
-def project_kernel(cam, wanted, positions, log_scales, rotations, logit, sh, send, aux, tab):
+def project_kernel(cam, positions, log_scales, rotations, logit, sh, parts, aux, tab):
     cos_a, sin_a, cos_e, sin_e = cam[0, 0], cam[0, 1], cam[0, 2], cam[0, 3]
     right = (-sin_a, cos_a)
     upward = (-sin_e * cos_a, -sin_e * sin_a, cos_e)
@@ -253,32 +260,68 @@
     aux[0:8, LOCAL : LOCAL + 128] = coef
     aux[8:16, LOCAL : LOCAL + 128] = jnp.zeros((8, 128), f32)
 
-    upper = sub >= 4
-
-    def gather_band(band, carry):
-        ids = [jnp.broadcast_to(wanted[band, j : j + 1, :], (8, 128)) for j in range(4)]
-        spots = [value & 127 for value in ids]
-        blocks = [lax.shift_right_logical(value, 7) for value in ids]
-        acc = [jnp.zeros((8, 128), f32)] * 4
-        low = [jnp.zeros((8, 128), f32)] * 4
-        for block in range(LOCAL // 128):
-            front = tab[0:8, 128 * block : 128 * block + 128]
-            for j in range(4):
-                acc[j] = jnp.where(blocks[j] == block, pick(front, spots[j]), acc[j])
-        for pair in range(LOCAL // 256):
-            first_half = tab[8:12, 256 * pair : 256 * pair + 128]
-            second_half = tab[8:12, 256 * pair + 128 : 256 * pair + 256]
-            both = jnp.concatenate([first_half, second_half], axis=0)
-            which = jnp.where(upper, 2 * pair + 1, 2 * pair)
-            for j in range(4):
-                low[j] = jnp.where(blocks[j] == which, pick(both, spots[j]), low[j])
+    for h in range(16):
+        lanes = slice(256 * h, 256 * h + 256)
+        value = tab[0:8, lanes]
+        rest = tab[8:12, lanes]
+        top = value.astype(bf16).astype(f32)
+        peak = rest.astype(bf16).astype(f32)
+        stack = jnp.concatenate([top, value - top, peak, rest - peak], axis=0)
+        if h % 2 == 0:
+            before = stack
+        else:
+            both = jnp.concatenate([before, stack], axis=0)
+            parts[24 * h - 24 : 24 * h + 24, :] = both.astype(bf16)
+
+
+def unit_rows(spot, width):
+    row = iota((16, width), 0).astype(f32)
+    one, zero = jnp.ones((16, width), bf16), jnp.zeros((16, width), bf16)
+    return jnp.concatenate(
+        [jnp.where(spot == (row + 16.0 * s).astype(bf16), one, zero) for s in range(16)], axis=0
+    )
+
+
+def small(ids):
+    wide = ids.astype(f32)
+    return jnp.concatenate([wide, wide], axis=0).astype(bf16)
+
+
+def masked_rows(block, count, high, low):
+    none = jnp.zeros_like(high)
+    tops, lows = [], []
+    for h in range(count):
+        mask = block == jnp.full(block.shape, h, bf16)
+        tops.append(jnp.where(mask, high, none))
+        lows.append(jnp.where(mask, low, none))
+    return jnp.concatenate(
+        [jnp.concatenate(tops, axis=0), jnp.concatenate(lows, axis=0)], axis=1
+    )
+
+
+def select_kernel(wanted, parts, send):
+    def one_band(band, carry):
+        ids = jnp.concatenate(
+            [jnp.broadcast_to(wanted[band, j : j + 1, :], (8, 128)) for j in range(4)], axis=1
+        )
+        block = lax.shift_right_logical(ids, 8)
+        hot = unit_rows(small(ids & 255), CAP)
+        found = jnp.dot(parts[...], hot, preferred_element_type=f32)
+        acc = [jnp.zeros((8, CAP), f32)] * 3
+        for h in range(16):
+            mask = block == h
+            for part in range(3):
+                start = 24 * h + 8 * part
+                acc[part] = jnp.where(mask, found[start : start + 8], acc[part])
+        value = acc[0] + acc[1]
+        rest = acc[2] + pltpu.roll(acc[2], 4, 0)
         for j in range(4):
-            send[band, 8 * j : 8 * j + 8, :] = acc[j]
-            whole = low[j] + pltpu.roll(low[j], 4, 0)
-            send[band, 32 + 4 * j : 36 + 4 * j, :] = whole[0:4]
+            lanes = slice(128 * j, 128 * j + 128)
+            send[band, 8 * j : 8 * j + 8, :] = value[:, lanes]
+            send[band, 32 + 4 * j : 36 + 4 * j, :] = rest[0:4, lanes]
         return carry
 
-    lax.fori_loop(0, OWNERS, gather_band, 0)
+    lax.fori_loop(0, OWNERS, one_band, 0, unroll=UNROLL_SELECT)
 
 
 def blend_kernel(
@@ -291,201 +334,215 @@
     back,
     images,
     answer,
+    tab,
     lhs,
     colours,
     alpha_ref,
     weight_ref,
     high_ref,
     low_ref,
-    ids_ref,
+    hot_ref,
+    block_ref,
     grads,
     total,
 ):
     lane = iota((8, 128), 1)
     sub = iota((8, 128), 0)
-    upper = sub >= 4
     diagonal = sub == (lane & 7)
     diag_wide = iota((8, CHUNK), 0) == (iota((8, CHUNK), 1) & 7)
+    depth = lax.shift_right_logical(lane, 3)
     total[...] = jnp.zeros_like(total)
-
-    def one_group(group, loss):
-        start = pl.multiple_of(group * GROUP, GROUP)
-        limit = jnp.broadcast_to(counts[pl.ds(group, 1), :], (8, 128))
-        own = slots[pl.ds(start, GROUP), :]
-        sequence = order[pl.ds(start, GROUP), :]
-        ordered = []
-        for half in range(2):
-            seq = sequence[:, 128 * half : 128 * half + 128]
-            spot = seq & 127
-            ordered.append(
-                jnp.where(seq < 128, pick(own[:, 0:128], spot), pick(own[:, 128:256], spot))
-            )
-        for half in range(2):
-
-            def gather_part(part, carry, half=half):
-                spots, blocks = [], []
-                for j in range(4):
-                    base = (part * 4 + j) * 16
-                    value = pick(ordered[half], base + lax.shift_right_logical(lane, 3))
+    for owner in range(OWNERS):
+        pieces = []
+        for part in range(2):
+            tops, lows = [], []
+            for j in (2 * part, 2 * part + 1):
+                value = table[owner, 8 * j : 8 * j + 8, :]
+                rest = table[owner, 32 + 4 * j : 36 + 4 * j, :]
+                top = value.astype(bf16).astype(f32)
+                peak = rest.astype(bf16).astype(f32)
+                tops.append(jnp.concatenate([top, value - top, peak, rest - peak], axis=0))
+            pieces.append(jnp.concatenate(tops, axis=1))
+        tab[48 * owner : 48 * owner + 48, :] = jnp.concatenate(pieces, axis=0).astype(bf16)
+
+    def one_set(index, loss):
+        groups = [index * TOGETHER + g for g in range(TOGETHER)]
+        starts = [pl.multiple_of(group * GROUP, GROUP) for group in groups]
+        limits, ordered = [], []
+        for g in range(TOGETHER):
+            limits.append(jnp.broadcast_to(counts[pl.ds(groups[g], 1), :], (8, 128)))
+            own = slots[pl.ds(starts[g], GROUP), :]
+            sequence = order[pl.ds(starts[g], GROUP), :]
+            for half in range(2):
+                seq = sequence[:, 128 * half : 128 * half + 128]
+                spot = seq & 127
+                ordered.append(
+                    jnp.where(seq < 128, pick(own[:, 0:128], spot), pick(own[:, 128:256], spot))
+                )
+
+        def gather(chunk, carry):
+            at = pl.multiple_of(chunk * CHUNK, CHUNK)
+            for g in range(TOGETHER):
+                values = []
+                for j in range(2):
+                    base = (2 * chunk + j) * 16 + depth
+                    value = jnp.where(
+                        base < 128,
+                        pick(ordered[2 * g], base & 127),
+                        pick(ordered[2 * g + 1], base & 127),
+                    )
                     value = jnp.sum(jnp.where(diagonal, value, 0), axis=0, keepdims=True)
-                    value = jnp.broadcast_to(value, (8, 128))
-                    at = pl.multiple_of((half * 8 + part * 4 + j) * 128, 128)
-                    ids_ref[:, pl.ds(at, 128)] = value
-                    spots.append(value & 127)
-                    blocks.append(lax.shift_right_logical(value, 7))
-                acc = [jnp.zeros((8, 128), f32)] * 4
-                low = [jnp.zeros((8, 128), f32)] * 4
-                for block in range(64):
-                    rows = table[block // 4, 8 * (block % 4) : 8 * (block % 4) + 8, :]
-                    for j in range(4):
-                        acc[j] = jnp.where(blocks[j] == block, pick(rows, spots[j]), acc[j])
-                for pair in range(32):
-                    rows = table[pair // 2, 32 + 8 * (pair % 2) : 40 + 8 * (pair % 2), :]
-                    which = jnp.where(upper, 2 * pair + 1, 2 * pair)
-                    for j in range(4):
-                        low[j] = jnp.where(blocks[j] == which, pick(rows, spots[j]), low[j])
-                for j in range(4):
-                    at = pl.multiple_of((half * 8 + part * 4 + j) * 128, 128)
-                    position = (half * 8 + part * 4 + j) * 16 + lax.shift_right_logical(lane, 3)
-                    dead = position >= limit
-                    value = jnp.where(dead & (sub == 0), DEAD, acc[j])
-                    rest = low[j] + pltpu.roll(low[j], 4, 0)
-                    p1 = value.astype(bf16).astype(f32)
-                    p2 = (value - p1).astype(bf16).astype(f32)
-                    p3 = value - p1 - p2
-                    last = jnp.broadcast_to(rest[0:1], (8, 128))
-                    q1 = last.astype(bf16).astype(f32)
-                    q2 = (last - q1).astype(bf16).astype(f32)
-                    q3 = last - q1 - q2
-                    tail = jnp.where(
-                        sub < 3,
-                        q1,
-                        jnp.where(sub < 5, q2, jnp.where(sub == 5, q3, 0.0)),
-                    )
-                    tops, lows = [], []
-                    for c in range(3):
-                        colour = jnp.where(
-                            diagonal, jnp.broadcast_to(rest[1 + c : 2 + c], (8, 128)), 0.0
-                        )
-                        top = colour.astype(bf16).astype(f32)
-                        tops.append(top)
-                        lows.append(colour - top)
-                    stack = jnp.concatenate(
-                        [p1, p1, p1, p2, p2, p3, tail] + tops + tops + lows, axis=0
-                    )
-                    lhs[pl.ds(at, 128), :] = stack.T.astype(bf16)
-                    colours[:, pl.ds(at, 128)] = jnp.concatenate(tops + lows, axis=0).astype(bf16)
-                return carry
-
-            lax.fori_loop(0, 2, gather_part, 0)
+                    values.append(jnp.broadcast_to(value, (8, 128)))
+                ids = jnp.concatenate(values, axis=1)
+                block = lax.shift_right_logical(ids, 8)
+                hot = unit_rows(small(ids & 255), CHUNK)
+                hot_ref[g, :, pl.ds(at, CHUNK)] = hot
+                block_ref[g, :, pl.ds(at, CHUNK)] = small(block)
+                found = jnp.dot(tab[...], hot, preferred_element_type=f32)
+                acc = [jnp.zeros((8, CHUNK), f32)] * 3
+                for h in range(32):
+                    mask = block == h
+                    for part in range(3):
+                        start = 24 * h + 8 * part
+                        acc[part] = jnp.where(mask, found[start : start + 8], acc[part])
+                base = chunk * CHUNK_K + lax.shift_right_logical(iota((8, CHUNK), 1), 3)
+                limit = jnp.concatenate([limits[g], limits[g]], axis=1)
+                line = iota((8, CHUNK), 0)
+                p1 = jnp.where((base >= limit) & (line == 0), DEAD, acc[0])
+                p2 = acc[1]
+
+                def spread(which):
+                    return jnp.broadcast_to(acc[2][which : which + 1], (8, CHUNK))
+
+                tail = jnp.where(line < 3, spread(0), jnp.where(line < 5, spread(4), 0.0))
+                tops = [jnp.where(diag_wide, spread(1 + c), 0.0) for c in range(3)]
+                lows = [jnp.where(diag_wide, spread(5 + c), 0.0) for c in range(3)]
+                blank = jnp.zeros((8, CHUNK), f32)
+                stack = jnp.concatenate(
+                    [p1, p1, p1, p2, p2, tail, blank] + tops + tops + lows, axis=0
+                )
+                lhs[g, pl.ds(at, CHUNK), :] = stack.T.astype(bf16)
+                colours[g, :, pl.ds(at, CHUNK)] = jnp.concatenate(tops + lows, axis=0).astype(bf16)
+            return carry
+
+        lax.fori_loop(0, CHUNKS, gather, 0, unroll=UNROLL_GATHER)
 
         def forward(chunk, carry):
-            passing, picture = carry
             at = pl.multiple_of(chunk * CHUNK, CHUNK)
-            power = jnp.dot(lhs[pl.ds(at, CHUNK), :], front[...], preferred_element_type=f32)
-            alpha = jnp.exp2(power)
-            alpha_ref[pl.ds(at, CHUNK), :] = alpha
-            pieces = []
-            for k in range(CHUNK_K):
-                piece = alpha[8 * k : 8 * k + 8] * passing
-                passing = passing - piece
-                pieces.append(piece)
-            weight = jnp.concatenate(pieces, axis=0)
-            weight_ref[pl.ds(at, CHUNK), :] = weight
-            high, low = halves(weight)
-            high_ref[pl.ds(at, CHUNK), :] = high
-            low_ref[pl.ds(at, CHUNK), :] = low
-            own = colours[:, pl.ds(at, CHUNK)]
-            picture = picture + jnp.dot(own, high, preferred_element_type=f32)
-            picture = picture + jnp.dot(own, low, preferred_element_type=f32)
-            return passing, picture
-
-        _, picture = lax.fori_loop(
-            0, CHUNKS, forward, (jnp.ones((8, PIX), f32), jnp.zeros((48, PIX), f32))
+            result = []
+            for g in range(TOGETHER):
+                passing, picture = carry[2 * g], carry[2 * g + 1]
+                power = jnp.dot(
+                    lhs[g, pl.ds(at, CHUNK), :], front[...], preferred_element_type=f32
+                )
+                alpha = jnp.exp2(power)
+                alpha_ref[g, pl.ds(at, CHUNK), :] = alpha
+                pieces = []
+                for k in range(CHUNK_K):
+                    piece = alpha[8 * k : 8 * k + 8] * passing
+                    passing = passing - piece
+                    pieces.append(piece)
+                weight = jnp.concatenate(pieces, axis=0)
+                weight_ref[g, pl.ds(at, CHUNK), :] = weight
+                high, low = halves(weight)
+                high_ref[g, pl.ds(at, CHUNK), :] = high
+                low_ref[g, pl.ds(at, CHUNK), :] = low
+                own = colours[g, :, pl.ds(at, CHUNK)]
+                picture = picture + jnp.dot(own, high, preferred_element_type=f32)
+                picture = picture + jnp.dot(own, low, preferred_element_type=f32)
+                result += [passing, picture]
+            return tuple(result)
+
+        begin = (jnp.ones((8, PIX), f32), jnp.zeros((48, PIX), f32)) * TOGETHER
+        done = lax.fori_loop(0, CHUNKS, forward, begin, unroll=UNROLL_FORWARD)
+        rights, errs = [], []
+        for g in range(TOGETHER):
+            picture = done[2 * g + 1]
+            picture = picture[0:24] + picture[24:48]
+            errors = []
+            for c in range(3):
+                image = picture[8 * c : 8 * c + 8]
+                images[pl.ds(starts[g], GROUP), c, :] = image
+                errors.append(image - target[pl.ds(starts[g], GROUP), c, :])
+            for error in errors:
+                square = error * error
+                loss = loss + square[:, 0:128] + square[:, 128:256]
+            error = jnp.concatenate(errors, axis=0)
+            top = error.astype(bf16).astype(f32)
+            bottom = error - top
+            right = jnp.concatenate([jnp.zeros((56, PIX), f32), top, bottom, top], axis=0)
+            rights.append(right.astype(bf16))
+            errs.append(jnp.concatenate([top, bottom], axis=0).astype(bf16))
+
+        def backward(step, carry):
+            at = pl.multiple_of((CHUNKS - 1 - step) * CHUNK, CHUNK)
+            result = []
+            for g in range(TOGETHER):
+                behind = carry[g]
+                gain = jnp.dot(
+                    lhs[g, pl.ds(at, CHUNK), :], rights[g], preferred_element_type=f32
+                )
+                alpha = alpha_ref[g, pl.ds(at, CHUNK), :]
+                weight = weight_ref[g, pl.ds(at, CHUNK), :]
+                pieces = [None] * CHUNK_K
+                for k in reversed(range(CHUNK_K)):
+                    rows = slice(8 * k, 8 * k + 8)
+                    gap = gain[rows] - behind
+                    pieces[k] = weight[rows] * gap
+                    behind = behind + alpha[rows] * gap
+                result.append(behind)
+                high, low = halves(jnp.concatenate(pieces, axis=0))
+                contract = (((1,), (1,)), ((), ()))
+                shape = lax.dot_general(back[...], high, contract, preferred_element_type=f32)
+                shape = shape + lax.dot_general(
+                    back[...], low, contract, preferred_element_type=f32
+                )
+                shape = shape[0:16] + shape[16:32]
+                paint = lax.dot_general(
+                    errs[g], high_ref[g, pl.ds(at, CHUNK), :], contract, preferred_element_type=f32
+                )
+                paint = paint + lax.dot_general(
+                    errs[g], low_ref[g, pl.ds(at, CHUNK), :], contract, preferred_element_type=f32
+                )
+                paint = paint[0:24] + paint[24:48]
+                second = shape[8:16]
+                row = iota((8, CHUNK), 0)
+                for c in range(3):
+                    own = jnp.where(diag_wide, paint[8 * c : 8 * c + 8], 0.0)
+                    own = jnp.sum(own, axis=0, keepdims=True)
+                    second = jnp.where(row == 1 + c, jnp.broadcast_to(own, (8, CHUNK)), second)
+                found = jnp.concatenate([shape[0:8], second], axis=0)
+                high, low = halves(found)
+                grads[g, 0, :, pl.ds(at, CHUNK)] = high
+                grads[g, 1, :, pl.ds(at, CHUNK)] = low
+            return tuple(result)
+
+        lax.fori_loop(
+            0,
+            CHUNKS,
+            backward,
+            (jnp.zeros((8, PIX), f32),) * TOGETHER,
+            unroll=UNROLL_BACKWARD,
         )
-        picture = picture[0:24] + picture[24:48]
-        errors = []
-        for c in range(3):
-            image = picture[8 * c : 8 * c + 8]
-            images[pl.ds(start, GROUP), c, :] = image
-            errors.append(image - target[pl.ds(start, GROUP), c, :])
-        for error in errors:
-            square = error * error
-            loss = loss + square[:, 0:128] + square[:, 128:256]
-        error = jnp.concatenate(errors, axis=0)
-        top = error.astype(bf16).astype(f32)
-        bottom = error - top
-        right = jnp.concatenate([jnp.zeros((56, PIX), f32), top, bottom, top], axis=0)
-        right = right.astype(bf16)
-        errs = jnp.concatenate([top, bottom], axis=0).astype(bf16)
-
-        def backward(step, behind):
-            at = pl.multiple_of((CHUNKS - 1 - step) * CHUNK, CHUNK)
-            gain = jnp.dot(lhs[pl.ds(at, CHUNK), :], right, preferred_element_type=f32)
-            alpha = alpha_ref[pl.ds(at, CHUNK), :]
-            weight = weight_ref[pl.ds(at, CHUNK), :]
-            pieces = [None] * CHUNK_K
-            for k in reversed(range(CHUNK_K)):
-                rows = slice(8 * k, 8 * k + 8)
-                gap = gain[rows] - behind
-                pieces[k] = weight[rows] * gap
-                behind = behind + alpha[rows] * gap
-            high, low = halves(jnp.concatenate(pieces, axis=0))
-            contract = (((1,), (1,)), ((), ()))
-            shape = lax.dot_general(back[...], high, contract, preferred_element_type=f32)
-            shape = shape + lax.dot_general(back[...], low, contract, preferred_element_type=f32)
-            shape = shape[0:16] + shape[16:32]
-            paint = lax.dot_general(
-                errs, high_ref[pl.ds(at, CHUNK), :], contract, preferred_element_type=f32
-            )
-            paint = paint + lax.dot_general(
-                errs, low_ref[pl.ds(at, CHUNK), :], contract, preferred_element_type=f32
-            )
-            paint = paint[0:24] + paint[24:48]
-            second = shape[8:16]
-            row = iota((8, CHUNK), 0)
-            for c in range(3):
-                own = jnp.where(diag_wide, paint[8 * c : 8 * c + 8], 0.0)
-                own = jnp.sum(own, axis=0, keepdims=True)
-                second = jnp.where(row == 1 + c, jnp.broadcast_to(own, (8, CHUNK)), second)
-            found = jnp.concatenate([shape[0:8], second], axis=0)
-            high, low = halves(found)
-            grads[0, :, pl.ds(at, CHUNK)] = high
-            grads[1, :, pl.ds(at, CHUNK)] = low
-            return behind
-
-        lax.fori_loop(0, CHUNKS, backward, jnp.zeros((8, PIX), f32))
 
         def scatter(step, carry):
             at = pl.multiple_of(step * SCAT, SCAT)
-            ids = ids_ref[:, pl.ds(at, SCAT)]
-            block = lax.shift_right_logical(ids, 8)
-            spot = ids & 255
-            high = grads[0, :, pl.ds(at, SCAT)]
-            low = grads[1, :, pl.ds(at, SCAT)]
-            tops, lows = [], []
-            for h in range(32):
-                mask = jnp.where(block == h, 1.0, 0.0)
-                mask = jnp.concatenate([mask, mask], axis=0).astype(bf16)
-                tops.append(mask * high)
-                lows.append(mask * low)
-            left = jnp.concatenate(
-                [jnp.concatenate(tops, axis=0), jnp.concatenate(lows, axis=0)], axis=1
-            )
-            row = iota((8, SCAT), 0)
-            hot = jnp.concatenate(
-                [jnp.where(spot == row + 8 * s, 1.0, 0.0) for s in range(32)], axis=0
-            ).astype(bf16)
-            hot = jnp.concatenate([hot, hot], axis=1)
-            total[...] += lax.dot_general(
-                left, hot, (((1,), (1,)), ((), ())), preferred_element_type=f32
-            )
+            for g in range(TOGETHER):
+                block = block_ref[g, :, pl.ds(at, SCAT)]
+                high = grads[g, 0, :, pl.ds(at, SCAT)]
+                low = grads[g, 1, :, pl.ds(at, SCAT)]
+                left = masked_rows(block, 32, high, low)
+                hot = hot_ref[g, :, pl.ds(at, SCAT)]
+                hot = jnp.concatenate([hot, hot], axis=1)
+                total[...] += lax.dot_general(
+                    left, hot, (((1,), (1,)), ((), ())), preferred_element_type=f32
+                )
             return carry
 
-        lax.fori_loop(0, ROWS // SCAT, scatter, 0)
+        lax.fori_loop(0, ROWS // SCAT, scatter, 0, unroll=UNROLL_SCATTER)
         return loss
 
-    loss = lax.fori_loop(0, GROUPS, one_group, jnp.zeros((8, 128), f32))
+    loss = lax.fori_loop(0, GROUPS // TOGETHER, one_set, jnp.zeros((8, 128), f32))
     for owner in range(OWNERS):
         for j in range(4):
             base = 16 * (2 * owner + j // 2)
@@ -493,6 +550,22 @@
             answer[owner, 8 * j : 8 * j + 8, :] = total[base : base + 8, lanes]
             answer[owner, 32 + 4 * j : 36 + 4 * j, :] = total[base + 8 : base + 12, lanes]
         answer[owner, 48:56, :] = loss
+
+
+def blend_scratch():
+    return [
+        pltpu.VMEM((768, 256), bf16),
+        pltpu.VMEM((TOGETHER, ROWS, 128), bf16),
+        pltpu.VMEM((TOGETHER, 48, ROWS), bf16),
+        pltpu.VMEM((TOGETHER, ROWS, PIX), f32),
+        pltpu.VMEM((TOGETHER, ROWS, PIX), f32),
+        pltpu.VMEM((TOGETHER, ROWS, PIX), bf16),
+        pltpu.VMEM((TOGETHER, ROWS, PIX), bf16),
+        pltpu.VMEM((TOGETHER, 256, ROWS), bf16),
+        pltpu.VMEM((TOGETHER, 16, ROWS), bf16),
+        pltpu.VMEM((TOGETHER, 2, 16, ROWS), bf16),
+        pltpu.VMEM((512, 256), f32),
+    ]
 
 
 def collect_kernel(back, wanted, aux, out, loss, total):
@@ -519,26 +592,17 @@
         low = jnp.concatenate(lows, axis=1)
         block = jnp.concatenate(blocks, axis=1)
         spot = jnp.concatenate(spots, axis=1)
-        left_top, left_low = [], []
-        for h in range(16):
-            mask = jnp.where(block == h, 1.0, 0.0)
-            mask = jnp.concatenate([mask, mask], axis=0).astype(bf16)
-            left_top.append(mask * high)
-            left_low.append(mask * low)
-        left = jnp.concatenate(
-            [jnp.concatenate(left_top, axis=0), jnp.concatenate(left_low, axis=0)], axis=1
-        )
-        row = iota((8, CAP), 0)
-        hot = jnp.concatenate(
-            [jnp.where(spot == row + 8 * s, 1.0, 0.0) for s in range(32)], axis=0
-        ).astype(bf16)
+        left = masked_rows(small(block), 16, high, low)
+        hot = unit_rows(small(spot), CAP)
         hot = jnp.concatenate([hot, hot], axis=1)
         total[...] += lax.dot_general(
             left, hot, (((1,), (1,)), ((), ())), preferred_element_type=f32
         )
         return squares + back[band, 48:56, :]
 
-    squares = lax.fori_loop(0, OWNERS, one_band, jnp.zeros((8, 128), f32))
+    squares = lax.fori_loop(
+        0, OWNERS, one_band, jnp.zeros((8, 128), f32), unroll=UNROLL_COLLECT
+    )
     whole = jnp.sum(jnp.sum(squares, axis=1, keepdims=True), axis=0, keepdims=True)
     loss[...] = whole * (1.0 / (TILES * OWNERS * PIX * 3))
     for h in range(16):
@@ -573,22 +637,23 @@
 
 
 def finish_kernel(
-    gathered, log_scales, rotations, logit, grad_pos, grad_log, grad_rot, grad_op, grad_sh, work
+    near, far, log_scales, rotations, logit, grad_pos, grad_log, grad_rot, grad_op, grad_sh, work
 ):
-    coef = jnp.concatenate([gathered[view, :, LOCAL + 512 :] for view in range(VIEWS)], axis=0)
+    gathered = [ref.at[i] for ref in (near, far) for i in range(VIEWS // 2)]
+    coef = jnp.concatenate([gathered[view][:, LOCAL + 512 :] for view in range(VIEWS)], axis=0)
     high, low = halves(coef.T)
     left = jnp.concatenate([high, low, high], axis=1)[0:64]
     for block in range(LOCAL // 512):
         lanes = slice(512 * block, 512 * block + 512)
-        value = jnp.concatenate([gathered[view, :, lanes] for view in range(VIEWS)], axis=0)
+        value = jnp.concatenate([gathered[view][:, lanes] for view in range(VIEWS)], axis=0)
         top, bottom = halves(value)
         right = jnp.concatenate([top, top, bottom], axis=0)
         work[:, lanes] = jnp.dot(left, right, preferred_element_type=f32)
     grad_sh[...] = work[0:48, :]
     grad_pos[...] = work[48:51, :]
-    shade = gathered[0, :, LOCAL : LOCAL + 512]
+    shade = gathered[0][:, LOCAL : LOCAL + 512]
     for view in range(1, VIEWS):
-        shade = shade + gathered[view, :, LOCAL : LOCAL + 512]
+        shade = shade + gathered[view][:, LOCAL : LOCAL + 512]
     shade = jnp.concatenate([shade[s : s + 1, :] for s in range(8)], axis=1)
     grad_op[...] = shade / (1.0 + jnp.exp(logit[...]))
     k00, k01, k02, k11, k12, k22 = [work[51 + i : 52 + i, :] for i in range(6)]
@@ -667,32 +732,30 @@
     ).reshape(1, 4)
     counts = jnp.tile(block_count.reshape(GROUPS, GROUP), (1, 16))
     front, back = pixel_tables()
-    send, aux = pl.pallas_call(
+    parts, aux = pl.pallas_call(
         project_kernel,
-        out_shape=(shape(OWNERS, SEND_ROWS, 128), shape(16, LOCAL + 128)),
-        in_specs=[pl.BlockSpec(memory_space=pltpu.SMEM)] + [whole()] * 6,
+        out_shape=(jax.ShapeDtypeStruct((384, 256), bf16), shape(16, LOCAL + 128)),
+        in_specs=[pl.BlockSpec(memory_space=pltpu.SMEM)] + [whole()] * 5,
         out_specs=(whole(), whole()),
         scratch_shapes=[pltpu.VMEM((16, LOCAL), f32)],
         compiler_params=params(32),
         name="project",
-    )(cam, wanted, positions, log_scales, rotations, opacity_logit, sh_coeffs)
+    )(cam, positions, log_scales, rotations, opacity_logit, sh_coeffs)
+    send = pl.pallas_call(
+        select_kernel,
+        out_shape=shape(OWNERS, SEND_ROWS, 128),
+        in_specs=[whole()] * 2,
+        out_specs=whole(),
+        compiler_params=params(32),
+        name="select",
+    )(wanted, parts)
     table = lax.all_to_all(send, "band", split_axis=0, concat_axis=0, tiled=True)
     images, answer = pl.pallas_call(
         blend_kernel,
         out_shape=(shape(TILES, 3, PIX), shape(OWNERS, BACK_ROWS, 128)),
         in_specs=[whole()] * 7,
         out_specs=(whole(), whole()),
-        scratch_shapes=[
-            pltpu.VMEM((ROWS, 128), bf16),
-            pltpu.VMEM((48, ROWS), bf16),
-            pltpu.VMEM((ROWS, PIX), f32),
-            pltpu.VMEM((ROWS, PIX), f32),
-            pltpu.VMEM((ROWS, PIX), bf16),
-            pltpu.VMEM((ROWS, PIX), bf16),
-            pltpu.VMEM((8, ROWS), jnp.int32),
-            pltpu.VMEM((2, 16, ROWS), bf16),
-            pltpu.VMEM((512, 256), f32),
-        ],
+        scratch_shapes=blend_scratch(),
         compiler_params=params(48),
         name="blend",
     )(
@@ -714,7 +777,12 @@
         compiler_params=params(32),
         name="collect",
     )(returned, wanted, aux)
-    gathered = lax.all_gather(share, "view", axis=0, tiled=False)
+    around = [share]
+    for step in (4, 2, 6):
+        ring = [(v, (v + step) % VIEWS) for v in range(VIEWS)]
+        around.append(lax.ppermute(share, "view", ring))
+    near = jnp.stack(around)
+    far = lax.ppermute(near, "view", [(v, v ^ 1) for v in range(VIEWS)])
     grads = pl.pallas_call(
         finish_kernel,
         out_shape=(
@@ -724,12 +792,12 @@
             shape(1, LOCAL),
             shape(48, LOCAL),
         ),
-        in_specs=[whole()] * 4,
+        in_specs=[whole()] * 5,
         out_specs=(whole(),) * 5,
         scratch_shapes=[pltpu.VMEM((64, LOCAL), f32)],
         compiler_params=params(32),
         name="finish",
-    )(gathered, log_scales, rotations, opacity_logit)
+    )(near, far, log_scales, rotations, opacity_logit)
     return (images[None], loss.reshape(1)) + tuple(grads)
 
 

time: 195 us -> 110 us (0.56)
  Pallas kernels: 108 us -> 49.4 us
  waiting for transfers between devices: 33.3 us -> 12.6 us
  between operations: 17.1 us -> 3.69 us
  starting transfers between devices: 13.1 us -> 24.9 us
  local copies, waits for them, and re-layouts: 9.92 us -> 6.36 us
    pallas_call x1, Pallas kernels: 88.5 us -> 40.1 us  [local(): pl.pallas_call(blend_kernel, out_shape=(shape(TILES, 3, PIX), shape(OWNER...]
    all_gather x1 -> x0, waiting for transfers between devices: 24.5 us -> none  [local(): gathered = lax.all_gather(share, 'view', axis=0, tiled=False)]
    ppermute x0 -> x4, starting transfers between devices: none -> 9.55 us  [the longest x1 5.34 us: local(): far = lax.ppermute(near, 'view', [(v, v ^ 1) for v in range(VIEWS)])]
    pallas_call x1 -> x2, Pallas kernels: 11.5 us -> 4.12 us  [the longest x1 3.09 us: local(): pl.pallas_call(select_kernel, out_shape=shape(OWNERS, SEND_ROWS, 128), in...]
    ppermute x0 -> x4, waiting for transfers between devices: none -> 6.1 us  [the longest x3 5.14 us: local(): around.append(lax.ppermute(share, 'view', ring))]
    unnamed x33 -> x25, local copies, waits for them, and re-layouts: 7 us -> 3.45 us
    pallas_call x1, Pallas kernels: 6.42 us -> 3.59 us  [local(): pl.pallas_call(collect_kernel, out_shape=(shape(8, WIDE), shape(1, 1)), i...]
    all_to_all x1, starting transfers between devices: 4.47 us -> 6.79 us  [local(): lax.all_to_all(send, 'band', split_axis=0, concat_axis=0, tiled=True)]
  transfers between devices with their start and end apart: 3 -> 6, of which waited for: 3 -> 4; matrix products, arithmetic and copies ran while one was open for 2% -> 3% of each run, Pallas kernels for 0% -> 1%
where the time goes in v2:
time: 110 us
  Pallas kernels  49.4 us (45%)
  starting transfers between devices  24.9 us (23%)
  waiting for transfers between devices  12.6 us (11%)
  blocking collectives  12.1 us (11%)
  local copies, waits for them, and re-layouts  6.36 us (6%)
  between operations  3.69 us (3%)
    pallas_call x1, Pallas kernels, local(): pl.pallas_call(blend_kernel, out_shape=(shape(TILES, 3, PIX), shape(OWNER...  40.1 us
    all_to_all x1, blocking collectives, local(): lax.all_to_all(answer, 'band', split_axis=0, concat_axis=0, tiled=True)  12.1 us
    all_to_all x1, starting transfers between devices, local(): lax.all_to_all(fetch_index.reshape(OWNERS, 4, 128), 'band', split_axis=0,...  8.6 us
    all_to_all x1, starting transfers between devices, local(): lax.all_to_all(send, 'band', split_axis=0, concat_axis=0, tiled=True)  6.79 us
    all_to_all x1, waiting for transfers between devices, local(): lax.all_to_all(send, 'band', split_axis=0, concat_axis=0, tiled=True)  6.46 us
    ppermute x1, starting transfers between devices, local(): far = lax.ppermute(near, 'view', [(v, v ^ 1) for v in range(VIEWS)])  5.34 us
    ppermute x3, waiting for transfers between devices, local(): around.append(lax.ppermute(share, 'view', ring))  5.14 us
    ppermute x3, starting transfers between devices, local(): around.append(lax.ppermute(share, 'view', ring))  4.21 us
  transfers between devices with their start and end apart: 6, of which 4 were waited for; matrix products, arithmetic and copies ran while one was open for 3% of the time, Pallas kernels for 1%

profile of v2, /device:TPU:1, one launch (start us, length us, event | category | flops | bytes accessed | tf_op | source)
XLA Modules:
  0.0 109.8 jit_solution(12165583739836894671)
XLA Ops:
  0.7 1.4 %reshape.35 = s32[16,4,128]{2,1,0:T(4,128)} reshape(s32[1,1,16,512]{3,2,1,0:T(8,128)} %param.20) | data formatting | bytes 65536 | tf_op jit(solution)/shard_map/reshape | solution.py:727
  2.1 8.6 %all-to-all-start = ((s32[16,4,128]{2,1,0:T(4,128)}), s32[16,4,128]{2,1,0:T(4,128)S(1)}, u32[]{:S(2)}, u32[]{:S(2)}) async-start(s32[16,4,128]{2,1,0:T(4,128)} %reshape.35), calls=%async_computation | async-start | bytes 65536 | tf_op jit(solution)/shard_map/all_to_all | solution.py:726
  10.7 1.3 %fusion = (f32[1,1]{1,0:T(1,128)}, f32[1,1]{1,0:T(1,128)}) fusion(f32[1,2]{1,0:T(1,128)} %param.18), kind=kLoop, calls=%fused_computation.3 | loop fusion | bytes 16 | tf_op jit(solution)/shard_map/slice | solution.py:729
  15.0 1.1 %copy-done = f32[48,4096]{1,0:T(8,128)S(1)} copy-done((f32[48,4096]{1,0:T(8,128)S(1)}, f32[48,4096]{1,0:T(8,128)}, u32[]{:S(2)}) %copy-start) | copy-done | bytes 786456
  16.1 0.8 copy-done.4
  17.0 1.0 project.1
  18.0 3.1 %select.1 = f32[16,48,128]{2,1,0:T(8,128)} custom-call(s32[16,4,128]{2,1,0:T(4,128)S(1)} %all-to-all-done.wanted, bf16[384,256]{1,0:T(8,128)(2,1)S(1)} %get-tuple-element.18.parts), custom_call_target="tpu_custom_call" | custom-call | tf_op jit(solution)/shard_map/select/pallas_call | solution.py:744
  21.1 6.8 %all-to-all-start.1 = ((f32[16,48,128]{2,1,0:T(8,128)}), f32[16,48,128]{2,1,0:T(8,128)S(1)}, u32[]{:S(2)}, u32[]{:S(2)}) async-start(f32[16,48,128]{2,1,0:T(8,128)} %select.1), calls=%async_computation.1 | async-start | bytes 786432 | tf_op jit(solution)/shard_map/all_to_all | solution.py:752
  27.9 0.5 broadcast.5
  28.4 0.1 copy-done.10
  28.6 0.7 reduce.3
  29.5 0.1 copy.25
  29.6 6.5 %all-to-all-done.1.table = f32[16,48,128]{2,1,0:T(8,128)S(1)} async-done(((f32[16,48,128]{2,1,0:T(8,128)}), f32[16,48,128]{2,1,0:T(8,128)S(1)}, u32[]{:S(2)}, u32[]{:S(2)}) %all-to-all-start.1) | async-done | bytes 393248 | tf_op jit(solution)/shard_map/all_to_all | solution.py:752
  36.1 40.1 %blend.1 = (f32[48,3,256]{2,1,0:T(4,128)S(1)}, f32[16,56,128]{2,1,0:T(8,128)S(1)}) custom-call(f32[16,48,128]{2,1,0:T(8,128)S(1)} %all-to-all-done.1.table, s32[48,256]{1,0:T(8,128)S(1)} %bitcast.22, s32[48,256]{1,0:T(8,128)S(1)} %bitcast.23, s32[6,128]{1,0:T(8,128)S(1)} %tile.12.counts, f32[48,3,256]{2,1,0:T(4,128)S(1)} %bitcast.19, ...), custom_call_target="tpu_custom_call" | custom-call | tf_op jit(solution)/shard_map/blend/pallas_call | solution.py:753
  76.2 12.1 %all_to_all.15.back = f32[16,56,128]{2,1,0:T(8,128)S(1)} all-to-all(f32[16,56,128]{2,1,0:T(8,128)S(1)} %get-tuple-element.20), channel_id=1, replica_groups=mesh['view'=8,'band'=16] {'band'}, dimensions={0} | all-to-all | bytes 917504 | tf_op jit(solution)/shard_map/all_to_all | solution.py:770
  88.3 3.6 %collect.1 = (f32[8,4736]{1,0:T(8,128)S(1)}, f32[1,1]{1,0:T(1,128)}) custom-call(f32[16,56,128]{2,1,0:T(8,128)S(1)} %all_to_all.15.back, s32[16,4,128]{2,1,0:T(4,128)S(1)} %all-to-all-done.wanted, f32[16,4224]{1,0:T(8,128)S(1)} %get-tuple-element.21.aux), custom_call_target="tpu_custom_call" | custom-call | tf_op jit(solution)/shard_map/collect/pallas_call | solution.py:771
  91.9 2.5 %collective-permute-start.2 = (f32[8,4736]{1,0:T(8,128)S(1)}, f32[8,4736]{1,0:T(8,128)S(1)}, u32[]{:S(2)}, u32[]{:S(2)}) collective-permute-start(f32[8,4736]{1,0:T(8,128)S(1)} %get-tuple-element.23), channel_id=1, source_target_pairs={{0,96},{16,112},{32,0},{48,16},{64,32},{80,48},{96,64},{112,80},{1... | collective-permute-start | bytes 454664 | tf_op jit(solution)/shard_map/ppermute | solution.py:783
  94.3 1.7 %collective-permute-start = (f32[8,4736]{1,0:T(8,128)S(1)}, f32[8,4736]{1,0:T(8,128)S(1)}, u32[]{:S(2)}, u32[]{:S(2)}) collective-permute-start(f32[8,4736]{1,0:T(8,128)S(1)} %get-tuple-element.23), channel_id=1, source_target_pairs={{0,64},{16,80},{32,96},{48,112},{64,0},{80,16},{96,32},{112,48},{1... | collective-permute-start | bytes 454664 | tf_op jit(solution)/shard_map/ppermute | solution.py:783
  96.1 0.4 collective-permute-done.2
  96.5 4.7 %collective-permute-done.1 = f32[8,4736]{1,0:T(8,128)S(1)} collective-permute-done((f32[8,4736]{1,0:T(8,128)S(1)}, f32[8,4736]{1,0:T(8,128)S(1)}, u32[]{:S(2)}, u32[]{:S(2)}) %collective-permute-start.1) | collective-permute-done | bytes 151584 | tf_op jit(solution)/shard_map/ppermute | solution.py:783
  101.3 5.3 %collective-permute-start.3 = (f32[4,8,4736]{2,1,0:T(8,128)S(1)}, f32[4,8,4736]{2,1,0:T(8,128)S(1)}, u32[]{:S(2)}, u32[]{:S(2)}) collective-permute-start(f32[4,8,4736]{2,1,0:T(8,128)S(1)} %pad_maximum_fusion.near), channel_id=1, source_target_pairs={{0,16},{16,0},{32,48},{48,32},{64,80},{80,64},{96,112},{112,96},{1... | collective-permute-start | bytes 1818632 | tf_op jit(solution)/shard_map/ppermute | solution.py:785
  106.6 0.7 copy.23
  107.3 1.0 collective-permute-done.3.far
  108.3 1.5 %finish.1 = (f32[3,4096]{1,0:T(4,128)}, f32[3,4096]{1,0:T(4,128)}, f32[4,4096]{1,0:T(4,128)}, f32[1,4096]{1,0:T(1,128)}, f32[48,4096]{1,0:T(8,128)}) custom-call(f32[4,8,4736]{2,1,0:T(8,128)S(1)} %pad_maximum_fusion.near, f32[4,8,4736]{2,1,0:T(8,128)S(1)} %collective-permute-done.3.far, f32[3,4096]{1,0:T(4,128)S(1)} %copy-done.1, f32[4,4096]{1,0:T(4,128)S(1)} %copy-done.2, ...), custom_call_target="tpu_custom_call" | custom-call | tf_op jit(solution)/shard_map/finish/pallas_call | solution.py:786
  (27 shorter events, 0.4 us)
Async XLA Ops:
  0.6 14.3 %copy-start.2 = (f32[4,4096]{1,0:T(4,128)S(1)}, f32[4,4096]{1,0:T(4,128)}, u32[]{:S(2)}) copy-start(f32[4,4096]{1,0:T(4,128)} %rotations.3) | copy-start | bytes 196612
  0.6 14.3 %copy-start.1 = (f32[3,4096]{1,0:T(4,128)S(1)}, f32[3,4096]{1,0:T(4,128)}, u32[]{:S(2)}) copy-start(f32[3,4096]{1,0:T(4,128)} %log_scales.3) | copy-start | bytes 147460
  2.1 15.9 %all-to-all-start = ((s32[16,4,128]{2,1,0:T(4,128)}), s32[16,4,128]{2,1,0:T(4,128)S(1)}, u32[]{:S(2)}, u32[]{:S(2)}) async-start(s32[16,4,128]{2,1,0:T(4,128)} %reshape.35), calls=%async_computation | async-start | bytes 65536 | tf_op jit(solution)/shard_map/all_to_all | solution.py:726
  10.7 4.3 %copy-start.3 = (f32[1,4096]{1,0:T(1,128)S(1)}, f32[1,4096]{1,0:T(1,128)}, u32[]{:S(2)}) copy-start(f32[1,4096]{1,0:T(1,128)} %logit.3) | copy-start | bytes 49156
  15.0 1.1 %copy-start = (f32[48,4096]{1,0:T(8,128)S(1)}, f32[48,4096]{1,0:T(8,128)}, u32[]{:S(2)}) copy-start(f32[48,4096]{1,0:T(8,128)} %sh.1) | copy-start | bytes 2359300
  16.1 0.8 copy-start.4
  21.1 8.3 %copy-start.9 = (f32[1,48,3,256]{3,1,2,0:T(8,128)S(1)}, f32[1,48,3,256]{3,1,2,0:T(8,128)}, u32[]{:S(2)}) copy-start(f32[1,48,3,256]{3,1,2,0:T(8,128)} %param.19) | copy-start | bytes 442372
  21.1 14.9 %all-to-all-start.1 = ((f32[16,48,128]{2,1,0:T(8,128)}), f32[16,48,128]{2,1,0:T(8,128)S(1)}, u32[]{:S(2)}, u32[]{:S(2)}) async-start(f32[16,48,128]{2,1,0:T(8,128)} %select.1), calls=%async_computation.1 | async-start | bytes 786432 | tf_op jit(solution)/shard_map/all_to_all | solution.py:752
  27.9 0.7 copy-start.10
  29.4 6.6 %copy-start.5 = (bf16[128,256]{1,0:T(8,128)(2,1)S(1)}, bf16[128,256]{1,0:T(8,128)(2,1)}, u32[]{:S(2)}) copy-start(bf16[128,256]{1,0:T(8,128)(2,1)} %constant.4.clone.front) | copy-start | bytes 196612
  29.4 6.6 %copy-start.6 = (s32[1,48,256]{2,1,0:T(8,128)S(1)}, s32[1,48,256]{2,1,0:T(8,128)}, u32[]{:S(2)}) copy-start(s32[1,48,256]{2,1,0:T(8,128)} %param.21) | copy-start | bytes 147460
  29.4 6.6 %copy-start.7 = (s32[1,48,256]{2,1,0:T(8,128)S(1)}, s32[1,48,256]{2,1,0:T(8,128)}, u32[]{:S(2)}) copy-start(s32[1,48,256]{2,1,0:T(8,128)} %param.22) | copy-start | bytes 147460
  29.4 6.6 %copy-start.8 = (bf16[32,256]{1,0:T(8,128)(2,1)S(1)}, bf16[32,256]{1,0:T(8,128)(2,1)}, u32[]{:S(2)}) copy-start(bf16[32,256]{1,0:T(8,128)(2,1)} %constant.5.clone.back) | copy-start | bytes 49156
  91.9 4.6 %collective-permute-start.2 = (f32[8,4736]{1,0:T(8,128)S(1)}, f32[8,4736]{1,0:T(8,128)S(1)}, u32[]{:S(2)}, u32[]{:S(2)}) collective-permute-start(f32[8,4736]{1,0:T(8,128)S(1)} %get-tuple-element.23), channel_id=1, source_target_pairs={{0,96},{16,112},{32,0},{48,16},{64,32},{80,48},{96,64},{112,80},{1... | collective-permute-start | bytes 454664 | tf_op jit(solution)/shard_map/ppermute | solution.py:783
  94.3 6.9 %collective-permute-start.1 = (f32[8,4736]{1,0:T(8,128)S(1)}, f32[8,4736]{1,0:T(8,128)S(1)}, u32[]{:S(2)}, u32[]{:S(2)}) collective-permute-start(f32[8,4736]{1,0:T(8,128)S(1)} %get-tuple-element.23), channel_id=1, source_target_pairs={{0,32},{16,48},{32,64},{48,80},{64,96},{80,112},{96,0},{112,16},{1... | collective-permute-start | bytes 454664 | tf_op jit(solution)/shard_map/ppermute | solution.py:783
  94.3 6.9 %collective-permute-start = (f32[8,4736]{1,0:T(8,128)S(1)}, f32[8,4736]{1,0:T(8,128)S(1)}, u32[]{:S(2)}, u32[]{:S(2)}) collective-permute-start(f32[8,4736]{1,0:T(8,128)S(1)} %get-tuple-element.23), channel_id=1, source_target_pairs={{0,64},{16,80},{32,96},{48,112},{64,0},{80,16},{96,32},{112,48},{1... | collective-permute-start | bytes 454664 | tf_op jit(solution)/shard_map/ppermute | solution.py:783
  101.3 7.0 %collective-permute-start.3 = (f32[4,8,4736]{2,1,0:T(8,128)S(1)}, f32[4,8,4736]{2,1,0:T(8,128)S(1)}, u32[]{:S(2)}, u32[]{:S(2)}) collective-permute-start(f32[4,8,4736]{2,1,0:T(8,128)S(1)} %pad_maximum_fusion.near), channel_id=1, source_target_pairs={{0,16},{16,0},{32,48},{48,32},{64,80},{80,64},{96,112},{112,96},{1... | collective-permute-start | bytes 1818632 | tf_op jit(solution)/shard_map/ppermute | solution.py:785

commit v3 on v2

--- a/solution.py
+++ b/solution.py
@@ -24,6 +24,8 @@
 CHUNK_K = CHUNK // GROUP
 CHUNKS = ROWS // CHUNK
 SCAT = 512
+BLOCK = 512
+UNROLL_REDUCE = 4
 TOGETHER = 3
 UNROLL_GATHER = 4
 UNROLL_FORWARD = 4
@@ -127,8 +129,7 @@
     return lax.broadcasted_iota(jnp.int32, shape, axis)
 
 
-def wave(mean):
-    cycles = mean * (1.0 / SIDE)
+def wave(cycles):
     part = cycles - jnp.floor(cycles + 0.5)
     x = part * math.pi
     x2 = x * x
@@ -174,11 +175,45 @@
     return jnp.take_along_axis(table, lanes, axis=1)
 
 
-def project_kernel(cam, positions, log_scales, rotations, logit, sh, parts, aux, tab):
-    cos_a, sin_a, cos_e, sin_e = cam[0, 0], cam[0, 1], cam[0, 2], cam[0, 3]
+def project_kernel(
+    angles,
+    positions_in,
+    log_scales_in,
+    rotations_in,
+    logit_in,
+    sh_in,
+    parts,
+    aux,
+    tab,
+    positions,
+    log_scales,
+    rotations,
+    logit,
+    sh,
+    arrived,
+):
+    copies = [
+        pltpu.make_async_copy(source, place, arrived.at[i])
+        for i, (source, place) in enumerate(
+            (
+                (positions_in, positions),
+                (rotations_in, rotations),
+                (log_scales_in, log_scales),
+                (logit_in, logit),
+                (sh_in, sh),
+            )
+        )
+    ]
+    for copy in copies:
+        copy.start()
+    turns = 0.5 / math.pi
+    sin_a, cos_a = wave(angles[0:1, 0:1] * turns)
+    sin_e, cos_e = wave(angles[0:1, 1:2] * turns)
     right = (-sin_a, cos_a)
     upward = (-sin_e * cos_a, -sin_e * sin_a, cos_e)
     basis = harmonic_basis(cos_e * cos_a, cos_e * sin_a, sin_e)
+    for copy in copies:
+        copy.wait()
     pos = [positions[i : i + 1, :] for i in range(3)]
     mean_x = right[0] * pos[0] + right[1] * pos[1]
     mean_y = upward[0] * pos[0] + upward[1] * pos[1] + upward[2] * pos[2]
@@ -195,8 +230,8 @@
     cov_c = second[0] * second[0] + second[1] * second[1] + second[2] * second[2] + dilation
     inverse = 1.0 / (cov_a * cov_c - cov_b * cov_b)
     c0, c1, c2 = cov_c * inverse, -cov_b * inverse, cov_a * inverse
-    sa, ca = wave(mean_x)
-    sb, cb = wave(mean_y)
+    sa, ca = wave(mean_x * (1.0 / SIDE))
+    sb, cb = wave(mean_y * (1.0 / SIDE))
     unit = KAPPA * LOG2E
     g0 = -LOG2E * jnp.log(1.0 + jnp.exp(-logit[...])) - (0.5 * unit) * (c0 + c2)
     cross = (-2.0 * unit) * c1
@@ -343,6 +378,8 @@
     low_ref,
     hot_ref,
     block_ref,
+    rise_ref,
+    fall_ref,
     grads,
     total,
 ):
@@ -472,7 +509,14 @@
             bottom = error - top
             right = jnp.concatenate([jnp.zeros((56, PIX), f32), top, bottom, top], axis=0)
             rights.append(right.astype(bf16))
-            errs.append(jnp.concatenate([top, bottom], axis=0).astype(bf16))
+            errs.append(jnp.concatenate([top, bottom], axis=0))
+
+        sides = []
+        for g in range(TOGETHER):
+            blank = jnp.zeros((96, PIX), f32)
+            form = jnp.concatenate([back[...].astype(f32), blank], axis=0).T
+            paint = jnp.concatenate([blank[0:32], errs[g], blank[0:48]], axis=0).T
+            sides.append(jnp.concatenate([form, form, paint, paint], axis=0).astype(bf16))
 
         def backward(step, carry):
             at = pl.multiple_of((CHUNKS - 1 - step) * CHUNK, CHUNK)
@@ -492,29 +536,8 @@
                     behind = behind + alpha[rows] * gap
                 result.append(behind)
                 high, low = halves(jnp.concatenate(pieces, axis=0))
-                contract = (((1,), (1,)), ((), ()))
-                shape = lax.dot_general(back[...], high, contract, preferred_element_type=f32)
-                shape = shape + lax.dot_general(
-                    back[...], low, contract, preferred_element_type=f32
-                )
-                shape = shape[0:16] + shape[16:32]
-                paint = lax.dot_general(
-                    errs[g], high_ref[g, pl.ds(at, CHUNK), :], contract, preferred_element_type=f32
-                )
-                paint = paint + lax.dot_general(
-                    errs[g], low_ref[g, pl.ds(at, CHUNK), :], contract, preferred_element_type=f32
-                )
-                paint = paint[0:24] + paint[24:48]
-                second = shape[8:16]
-                row = iota((8, CHUNK), 0)
-                for c in range(3):
-                    own = jnp.where(diag_wide, paint[8 * c : 8 * c + 8], 0.0)
-                    own = jnp.sum(own, axis=0, keepdims=True)
-                    second = jnp.where(row == 1 + c, jnp.broadcast_to(own, (8, CHUNK)), second)
-                found = jnp.concatenate([shape[0:8], second], axis=0)
-                high, low = halves(found)
-                grads[g, 0, :, pl.ds(at, CHUNK)] = high
-                grads[g, 1, :, pl.ds(at, CHUNK)] = low
+                rise_ref[g, pl.ds(at, CHUNK), :] = high
+                fall_ref[g, pl.ds(at, CHUNK), :] = low
             return tuple(result)
 
         lax.fori_loop(
@@ -524,6 +547,31 @@
             (jnp.zeros((8, PIX), f32),) * TOGETHER,
             unroll=UNROLL_BACKWARD,
         )
+
+        def reduce(step, carry):
+            at = pl.multiple_of(step * BLOCK, BLOCK)
+            row = iota((8, BLOCK), 0)
+            match = row == (iota((8, BLOCK), 1) & 7)
+            for g in range(TOGETHER):
+                pieces = [
+                    ref[g, pl.ds(at, BLOCK), :] for ref in (rise_ref, fall_ref, high_ref, low_ref)
+                ]
+                sums = jnp.dot(
+                    jnp.concatenate(pieces, axis=1), sides[g], preferred_element_type=f32
+                ).T
+                form = sums[0:16] + sums[16:32]
+                paint = sums[32:56] + sums[56:80]
+                second = form[8:16]
+                for c in range(3):
+                    own = jnp.where(match, paint[8 * c : 8 * c + 8], 0.0)
+                    own = jnp.sum(own, axis=0, keepdims=True)
+                    second = jnp.where(row == 1 + c, jnp.broadcast_to(own, (8, BLOCK)), second)
+                high, low = halves(jnp.concatenate([form[0:8], second], axis=0))
+                grads[g, 0, :, pl.ds(at, BLOCK)] = high
+                grads[g, 1, :, pl.ds(at, BLOCK)] = low
+            return carry
+
+        lax.fori_loop(0, ROWS // BLOCK, reduce, 0, unroll=UNROLL_REDUCE)
 
         def scatter(step, carry):
             at = pl.multiple_of(step * SCAT, SCAT)
@@ -563,6 +611,8 @@
         pltpu.VMEM((TOGETHER, ROWS, PIX), bf16),
         pltpu.VMEM((TOGETHER, 256, ROWS), bf16),
         pltpu.VMEM((TOGETHER, 16, ROWS), bf16),
+        pltpu.VMEM((TOGETHER, ROWS, PIX), bf16),
+        pltpu.VMEM((TOGETHER, ROWS, PIX), bf16),
         pltpu.VMEM((TOGETHER, 2, 16, ROWS), bf16),
         pltpu.VMEM((512, 256), f32),
     ]
@@ -726,21 +776,18 @@
     wanted = lax.all_to_all(
         fetch_index.reshape(OWNERS, 4, 128), "band", split_axis=0, concat_axis=0, tiled=True
     )
-    azimuth, elevation = view_angles[0, 0], view_angles[0, 1]
-    cam = jnp.stack(
-        [jnp.cos(azimuth), jnp.sin(azimuth), jnp.cos(elevation), jnp.sin(elevation)]
-    ).reshape(1, 4)
     counts = jnp.tile(block_count.reshape(GROUPS, GROUP), (1, 16))
     front, back = pixel_tables()
     parts, aux = pl.pallas_call(
         project_kernel,
         out_shape=(jax.ShapeDtypeStruct((384, 256), bf16), shape(16, LOCAL + 128)),
-        in_specs=[pl.BlockSpec(memory_space=pltpu.SMEM)] + [whole()] * 5,
+        in_specs=[whole()] + [pl.BlockSpec(memory_space=pl.ANY)] * 5,
         out_specs=(whole(), whole()),
-        scratch_shapes=[pltpu.VMEM((16, LOCAL), f32)],
-        compiler_params=params(32),
+        scratch_shapes=[pltpu.VMEM((rows, LOCAL), f32) for rows in (16, 3, 3, 4, 1, 48)]
+        + [pltpu.SemaphoreType.DMA((5,))],
+        compiler_params=params(56),
         name="project",
-    )(cam, positions, log_scales, rotations, opacity_logit, sh_coeffs)
+    )(view_angles, positions, log_scales, rotations, opacity_logit, sh_coeffs)
     send = pl.pallas_call(
         select_kernel,
         out_shape=shape(OWNERS, SEND_ROWS, 128),
@@ -756,7 +803,7 @@
         in_specs=[whole()] * 7,
         out_specs=(whole(), whole()),
         scratch_shapes=blend_scratch(),
-        compiler_params=params(48),
+        compiler_params=params(42),
         name="blend",
     )(
         table,

time: 110 us -> 96.3 us (0.88)
  Pallas kernels: 49.4 us -> 40.4 us
  between operations: 3.69 us -> 0.76 us
  waiting for transfers between devices: 12.6 us -> 15.4 us
  starting transfers between devices: 24.9 us -> 22.3 us
  local copies, waits for them, and re-layouts: 6.36 us -> 3.97 us
    pallas_call x1, Pallas kernels: 40.1 us -> 28.7 us  [local(): pl.pallas_call(blend_kernel, out_shape=(shape(TILES, 3, PIX), shape(OWNER...]
    all_to_all x1, waiting for transfers between devices: 0.01 us -> 2.96 us  [local(): lax.all_to_all(fetch_index.reshape(OWNERS, 4, 128), 'band', split_axis=0,...]
    all_to_all x1, starting transfers between devices: 6.79 us -> 3.83 us  [local(): lax.all_to_all(send, 'band', split_axis=0, concat_axis=0, tiled=True)]
    pallas_call x1, Pallas kernels: 1.03 us -> 3.5 us  [local(): pl.pallas_call(project_kernel, out_shape=(jax.ShapeDtypeStruct((384, 256)...]
    slice x1 -> x0, local copies, waits for them, and re-layouts: 1.31 us -> none  [local(): azimuth, elevation = (view_angles[0, 0], view_angles[0, 1])]
  transfers between devices with their start and end apart: 6 -> 6, of which waited for: 4 -> 5; matrix products, arithmetic and copies ran while one was open for 3% -> 2% of each run, Pallas kernels for 1% -> 4%
where the time goes in v3:
time: 96.3 us; the launch traced here: 95.9 us
  Pallas kernels  40.4 us (42%)
  starting transfers between devices  22.3 us (23%)
  waiting for transfers between devices  15.4 us (16%)
  blocking collectives  12.3 us (13%)
  local copies, waits for them, and re-layouts  3.97 us (4%)
    pallas_call x1, Pallas kernels, local(): pl.pallas_call(blend_kernel, out_shape=(shape(TILES, 3, PIX), shape(OWNER...  28.7 us
    all_to_all x1, blocking collectives, local(): lax.all_to_all(answer, 'band', split_axis=0, concat_axis=0, tiled=True)  12.3 us
    all_to_all x1, starting transfers between devices, local(): lax.all_to_all(fetch_index.reshape(OWNERS, 4, 128), 'band', split_axis=0,...  8.6 us
    all_to_all x1, waiting for transfers between devices, local(): lax.all_to_all(send, 'band', split_axis=0, concat_axis=0, tiled=True)  6.3 us
    ppermute x1, starting transfers between devices, local(): far = lax.ppermute(near, 'view', [(v, v ^ 1) for v in range(VIEWS)])  5.69 us
    ppermute x3, waiting for transfers between devices, local(): around.append(lax.ppermute(share, 'view', ring))  5.13 us
    ppermute x3, starting transfers between devices, local(): around.append(lax.ppermute(share, 'view', ring))  4.22 us
    all_to_all x1, starting transfers between devices, local(): lax.all_to_all(send, 'band', split_axis=0, concat_axis=0, tiled=True)  3.83 us
  transfers between devices with their start and end apart: 6, of which 5 were waited for; matrix products, arithmetic and copies ran while one was open for 2% of the time, Pallas kernels for 4%

profile of v3, /device:TPU:1, one launch (start us, length us, event | category | flops | bytes accessed | tf_op | source)
XLA Modules:
  0.0 95.9 jit_solution(13567151591768640934)
XLA Ops:
  0.6 1.4 %reshape.24 = s32[16,4,128]{2,1,0:T(4,128)} reshape(s32[1,1,16,512]{3,2,1,0:T(8,128)} %param.20) | data formatting | bytes 65536 | tf_op jit(solution)/shard_map/reshape | solution.py:777
  2.0 8.6 %all-to-all-start = ((s32[16,4,128]{2,1,0:T(4,128)}), s32[16,4,128]{2,1,0:T(4,128)S(1)}, u32[]{:S(2)}, u32[]{:S(2)}) async-start(s32[16,4,128]{2,1,0:T(4,128)} %reshape.24), calls=%async_computation | async-start | bytes 65536 | tf_op jit(solution)/shard_map/all_to_all | solution.py:776
  10.6 3.5 %project.1 = (bf16[384,256]{1,0:T(8,128)(2,1)}, f32[16,4224]{1,0:T(8,128)}) custom-call(f32[1,2]{1,0:T(1,128)} %angles.1, f32[3,4096]{1,0:T(4,128)} %positions_in.1, f32[3,4096]{1,0:T(4,128)} %log_scales.1, f32[4,4096]{1,0:T(4,128)} %rotations.1, f32[1,4096]{1,0:T(1,128)} %logit.1, f32[48,4096]{1,0:T(8,128)} %sh_in.1), custom_call_target="tpu_custom_call" | custom-call | tf_op jit(solution)/shard_map/project/pallas_call | solution.py:781
  14.1 3.0 %all-to-all-done.wanted = s32[16,4,128]{2,1,0:T(4,128)S(1)} async-done(((s32[16,4,128]{2,1,0:T(4,128)}), s32[16,4,128]{2,1,0:T(4,128)S(1)}, u32[]{:S(2)}, u32[]{:S(2)}) %all-to-all-start) | async-done | bytes 32800 | tf_op jit(solution)/shard_map/all_to_all | solution.py:776
  17.1 0.9 copy-done.3
  18.0 3.1 %select.1 = f32[16,48,128]{2,1,0:T(8,128)} custom-call(s32[16,4,128]{2,1,0:T(4,128)S(1)} %all-to-all-done.wanted, bf16[384,256]{1,0:T(8,128)(2,1)S(1)} %copy-done.3), custom_call_target="tpu_custom_call" | custom-call | tf_op jit(solution)/shard_map/select/pallas_call | solution.py:791
  21.1 3.8 %all-to-all-start.1 = ((f32[16,48,128]{2,1,0:T(8,128)}), f32[16,48,128]{2,1,0:T(8,128)S(1)}, u32[]{:S(2)}, u32[]{:S(2)}) async-start(f32[16,48,128]{2,1,0:T(8,128)} %select.1), calls=%async_computation.1 | async-start | bytes 786432 | tf_op jit(solution)/shard_map/all_to_all | solution.py:799
  25.0 0.5 broadcast.5
  25.5 0.1 copy-done.10
  25.6 0.7 reduce.3
  26.4 0.1 tile.12.counts
  26.5 0.1 copy.25
  26.6 6.3 %all-to-all-done.1.table = f32[16,48,128]{2,1,0:T(8,128)S(1)} async-done(((f32[16,48,128]{2,1,0:T(8,128)}), f32[16,48,128]{2,1,0:T(8,128)S(1)}, u32[]{:S(2)}, u32[]{:S(2)}) %all-to-all-start.1) | async-done | bytes 393248 | tf_op jit(solution)/shard_map/all_to_all | solution.py:799
  33.0 28.7 %blend.1 = (f32[48,3,256]{2,1,0:T(4,128)S(1)}, f32[16,56,128]{2,1,0:T(8,128)S(1)}) custom-call(f32[16,48,128]{2,1,0:T(8,128)S(1)} %all-to-all-done.1.table, s32[48,256]{1,0:T(8,128)S(1)} %bitcast.16, s32[48,256]{1,0:T(8,128)S(1)} %bitcast.17, s32[6,128]{1,0:T(8,128)S(1)} %tile.12.counts, f32[48,3,256]{2,1,0:T(4,128)S(1)} %bitcast.13, ...), custom_call_target="tpu_custom_call" | custom-call | tf_op jit(solution)/shard_map/blend/pallas_call | solution.py:800
  61.7 12.3 %all_to_all.15.back = f32[16,56,128]{2,1,0:T(8,128)S(1)} all-to-all(f32[16,56,128]{2,1,0:T(8,128)S(1)} %get-tuple-element.20), channel_id=1, replica_groups=mesh['view'=8,'band'=16] {'band'}, dimensions={0} | all-to-all | bytes 917504 | tf_op jit(solution)/shard_map/all_to_all | solution.py:817
  74.0 3.6 %collect.1 = (f32[8,4736]{1,0:T(8,128)S(1)}, f32[1,1]{1,0:T(1,128)}) custom-call(f32[16,56,128]{2,1,0:T(8,128)S(1)} %all_to_all.15.back, s32[16,4,128]{2,1,0:T(4,128)S(1)} %all-to-all-done.wanted, f32[16,4224]{1,0:T(8,128)S(1)} %copy-done), custom_call_target="tpu_custom_call" | custom-call | tf_op jit(solution)/shard_map/collect/pallas_call | solution.py:818
  77.6 2.5 %collective-permute-start.2 = (f32[8,4736]{1,0:T(8,128)S(1)}, f32[8,4736]{1,0:T(8,128)S(1)}, u32[]{:S(2)}, u32[]{:S(2)}) collective-permute-start(f32[8,4736]{1,0:T(8,128)S(1)} %get-tuple-element.23), channel_id=1, source_target_pairs={{0,96},{16,112},{32,0},{48,16},{64,32},{80,48},{96,64},{112,80},{1... | collective-permute-start | bytes 454664 | tf_op jit(solution)/shard_map/ppermute | solution.py:830
  80.1 1.7 %collective-permute-start = (f32[8,4736]{1,0:T(8,128)S(1)}, f32[8,4736]{1,0:T(8,128)S(1)}, u32[]{:S(2)}, u32[]{:S(2)}) collective-permute-start(f32[8,4736]{1,0:T(8,128)S(1)} %get-tuple-element.23), channel_id=1, source_target_pairs={{0,64},{16,80},{32,96},{48,112},{64,0},{80,16},{96,32},{112,48},{1... | collective-permute-start | bytes 454664 | tf_op jit(solution)/shard_map/ppermute | solution.py:830
  81.8 0.4 collective-permute-done.2
  82.2 4.7 %collective-permute-done.1 = f32[8,4736]{1,0:T(8,128)S(1)} collective-permute-done((f32[8,4736]{1,0:T(8,128)S(1)}, f32[8,4736]{1,0:T(8,128)S(1)}, u32[]{:S(2)}, u32[]{:S(2)}) %collective-permute-start.1) | collective-permute-done | bytes 151584 | tf_op jit(solution)/shard_map/ppermute | solution.py:830
  87.0 5.7 %collective-permute-start.3 = (f32[4,8,4736]{2,1,0:T(8,128)S(1)}, f32[4,8,4736]{2,1,0:T(8,128)S(1)}, u32[]{:S(2)}, u32[]{:S(2)}) collective-permute-start(f32[4,8,4736]{2,1,0:T(8,128)S(1)} %pad_maximum_fusion.near), channel_id=1, source_target_pairs={{0,16},{16,0},{32,48},{48,32},{64,80},{80,64},{96,112},{112,96},{1... | collective-permute-start | bytes 1818632 | tf_op jit(solution)/shard_map/ppermute | solution.py:832
  92.7 0.7 copy.23
  93.4 1.0 %collective-permute-done.3.far = f32[4,8,4736]{2,1,0:T(8,128)S(1)} collective-permute-done((f32[4,8,4736]{2,1,0:T(8,128)S(1)}, f32[4,8,4736]{2,1,0:T(8,128)S(1)}, u32[]{:S(2)}, u32[]{:S(2)}) %collective-permute-start.3) | collective-permute-done | bytes 606240 | tf_op jit(solution)/shard_map/ppermute | solution.py:832
  94.4 1.5 %finish.1 = (f32[3,4096]{1,0:T(4,128)}, f32[3,4096]{1,0:T(4,128)}, f32[4,4096]{1,0:T(4,128)}, f32[1,4096]{1,0:T(1,128)}, f32[48,4096]{1,0:T(8,128)}) custom-call(f32[4,8,4736]{2,1,0:T(8,128)S(1)} %pad_maximum_fusion.near, f32[4,8,4736]{2,1,0:T(8,128)S(1)} %collective-permute-done.3.far, f32[3,4096]{1,0:T(4,128)S(1)} %copy-done.1, f32[4,4096]{1,0:T(4,128)S(1)} %copy-done.2, ...), custom_call_target="tpu_custom_call" | custom-call | tf_op jit(solution)/shard_map/finish/pallas_call | solution.py:833
  (25 shorter events, 0.2 us)
Async XLA Ops:
  2.0 15.1 %all-to-all-start = ((s32[16,4,128]{2,1,0:T(4,128)}), s32[16,4,128]{2,1,0:T(4,128)S(1)}, u32[]{:S(2)}, u32[]{:S(2)}) async-start(s32[16,4,128]{2,1,0:T(4,128)} %reshape.24), calls=%async_computation | async-start | bytes 65536 | tf_op jit(solution)/shard_map/all_to_all | solution.py:776
  17.1 0.9 copy-start.3
  21.1 5.4 %copy-start.9 = (f32[1,48,3,256]{3,1,2,0:T(8,128)S(1)}, f32[1,48,3,256]{3,1,2,0:T(8,128)}, u32[]{:S(2)}) copy-start(f32[1,48,3,256]{3,1,2,0:T(8,128)} %param.19) | copy-start | bytes 442372
  21.1 11.8 %all-to-all-start.1 = ((f32[16,48,128]{2,1,0:T(8,128)}), f32[16,48,128]{2,1,0:T(8,128)S(1)}, u32[]{:S(2)}, u32[]{:S(2)}) async-start(f32[16,48,128]{2,1,0:T(8,128)} %select.1), calls=%async_computation.1 | async-start | bytes 786432 | tf_op jit(solution)/shard_map/all_to_all | solution.py:799
  25.0 0.7 copy-start.10
  26.5 6.5 %copy-start.5 = (bf16[128,256]{1,0:T(8,128)(2,1)S(1)}, bf16[128,256]{1,0:T(8,128)(2,1)}, u32[]{:S(2)}) copy-start(bf16[128,256]{1,0:T(8,128)(2,1)} %constant.4.clone.front) | copy-start | bytes 196612
  26.5 6.5 %copy-start.6 = (s32[1,48,256]{2,1,0:T(8,128)S(1)}, s32[1,48,256]{2,1,0:T(8,128)}, u32[]{:S(2)}) copy-start(s32[1,48,256]{2,1,0:T(8,128)} %param.21) | copy-start | bytes 147460
  26.5 6.4 %copy-start.7 = (s32[1,48,256]{2,1,0:T(8,128)S(1)}, s32[1,48,256]{2,1,0:T(8,128)}, u32[]{:S(2)}) copy-start(s32[1,48,256]{2,1,0:T(8,128)} %param.22) | copy-start | bytes 147460
  26.5 6.4 %copy-start.8 = (bf16[32,256]{1,0:T(8,128)(2,1)S(1)}, bf16[32,256]{1,0:T(8,128)(2,1)}, u32[]{:S(2)}) copy-start(bf16[32,256]{1,0:T(8,128)(2,1)} %constant.5.clone.back) | copy-start | bytes 49156
  61.7 12.3 %copy-start = (f32[16,4224]{1,0:T(8,128)S(1)}, f32[16,4224]{1,0:T(8,128)}, u32[]{:S(2)}) copy-start(f32[16,4224]{1,0:T(8,128)} %get-tuple-element.21.aux) | copy-start | bytes 811012
  77.6 4.6 %collective-permute-start.2 = (f32[8,4736]{1,0:T(8,128)S(1)}, f32[8,4736]{1,0:T(8,128)S(1)}, u32[]{:S(2)}, u32[]{:S(2)}) collective-permute-start(f32[8,4736]{1,0:T(8,128)S(1)} %get-tuple-element.23), channel_id=1, source_target_pairs={{0,96},{16,112},{32,0},{48,16},{64,32},{80,48},{96,64},{112,80},{1... | collective-permute-start | bytes 454664 | tf_op jit(solution)/shard_map/ppermute | solution.py:830
  80.1 6.9 %collective-permute-start.1 = (f32[8,4736]{1,0:T(8,128)S(1)}, f32[8,4736]{1,0:T(8,128)S(1)}, u32[]{:S(2)}, u32[]{:S(2)}) collective-permute-start(f32[8,4736]{1,0:T(8,128)S(1)} %get-tuple-element.23), channel_id=1, source_target_pairs={{0,32},{16,48},{32,64},{48,80},{64,96},{80,112},{96,0},{112,16},{1... | collective-permute-start | bytes 454664 | tf_op jit(solution)/shard_map/ppermute | solution.py:830
  80.1 6.9 %collective-permute-start = (f32[8,4736]{1,0:T(8,128)S(1)}, f32[8,4736]{1,0:T(8,128)S(1)}, u32[]{:S(2)}, u32[]{:S(2)}) collective-permute-start(f32[8,4736]{1,0:T(8,128)S(1)} %get-tuple-element.23), channel_id=1, source_target_pairs={{0,64},{16,80},{32,96},{48,112},{64,0},{80,16},{96,32},{112,48},{1... | collective-permute-start | bytes 454664 | tf_op jit(solution)/shard_map/ppermute | solution.py:830
  87.0 7.3 %collective-permute-start.3 = (f32[4,8,4736]{2,1,0:T(8,128)S(1)}, f32[4,8,4736]{2,1,0:T(8,128)S(1)}, u32[]{:S(2)}, u32[]{:S(2)}) collective-permute-start(f32[4,8,4736]{2,1,0:T(8,128)S(1)} %pad_maximum_fusion.near), channel_id=1, source_target_pairs={{0,16},{16,0},{32,48},{48,32},{64,80},{80,64},{96,112},{112,96},{1... | collective-permute-start | bytes 1818632 | tf_op jit(solution)/shard_map/ppermute | solution.py:832
  92.7 1.7 %copy-start.1 = (f32[3,4096]{1,0:T(4,128)S(1)}, f32[3,4096]{1,0:T(4,128)}, u32[]{:S(2)}) copy-start(f32[3,4096]{1,0:T(4,128)} %log_scales.1) | copy-start | bytes 147460
  92.7 1.7 %copy-start.2 = (f32[4,4096]{1,0:T(4,128)S(1)}, f32[4,4096]{1,0:T(4,128)}, u32[]{:S(2)}) copy-start(f32[4,4096]{1,0:T(4,128)} %rotations.1) | copy-start | bytes 196612
  92.7 1.7 %copy-start.4 = (f32[1,4096]{1,0:T(1,128)S(1)}, f32[1,4096]{1,0:T(1,128)}, u32[]{:S(2)}) copy-start(f32[1,4096]{1,0:T(1,128)} %logit.1) | copy-start | bytes 49156

commit v4 on v3

--- a/solution.py
+++ b/solution.py
@@ -28,7 +28,7 @@
 UNROLL_REDUCE = 4
 TOGETHER = 3
 UNROLL_GATHER = 4
-UNROLL_FORWARD = 4
+UNROLL_FORWARD = 8
 UNROLL_BACKWARD = 8
 UNROLL_SCATTER = 4
 UNROLL_SELECT = 4
@@ -95,9 +95,13 @@
     for at, which in enumerate(order):
         front[8 * at : 8 * at + 8] = parts[which][:8]
         front[40 + at] = parts[which][8]
+    early = pixel % SIDE < SIDE // 2
+    kept = np.where(np.arange(9)[:, None] < 5, early, ~early)
     back = np.zeros((32, PIX), kind)
-    back[0:9] = parts[0]
-    back[16:25] = parts[1]
+    for at in (0, PIX // 2):
+        half = slice(at, at + PIX // 2)
+        back[0:9, half] = np.where(kept, parts[0], 0)[:, : PIX // 2]
+        back[16:25, half] = np.where(kept, parts[1], 0)[:, : PIX // 2]
     return front, back
 
 
@@ -175,45 +179,13 @@
     return jnp.take_along_axis(table, lanes, axis=1)
 
 
-def project_kernel(
-    angles,
-    positions_in,
-    log_scales_in,
-    rotations_in,
-    logit_in,
-    sh_in,
-    parts,
-    aux,
-    tab,
-    positions,
-    log_scales,
-    rotations,
-    logit,
-    sh,
-    arrived,
-):
-    copies = [
-        pltpu.make_async_copy(source, place, arrived.at[i])
-        for i, (source, place) in enumerate(
-            (
-                (positions_in, positions),
-                (rotations_in, rotations),
-                (log_scales_in, log_scales),
-                (logit_in, logit),
-                (sh_in, sh),
-            )
-        )
-    ]
-    for copy in copies:
-        copy.start()
+def project_kernel(angles, positions, log_scales, rotations, logit, sh, parts, aux, tab):
     turns = 0.5 / math.pi
     sin_a, cos_a = wave(angles[0:1, 0:1] * turns)
     sin_e, cos_e = wave(angles[0:1, 1:2] * turns)
     right = (-sin_a, cos_a)
     upward = (-sin_e * cos_a, -sin_e * sin_a, cos_e)
     basis = harmonic_basis(cos_e * cos_a, cos_e * sin_a, sin_e)
-    for copy in copies:
-        copy.wait()
     pos = [positions[i : i + 1, :] for i in range(3)]
     mean_x = right[0] * pos[0] + right[1] * pos[1]
     mean_y = upward[0] * pos[0] + upward[1] * pos[1] + upward[2] * pos[2]
@@ -323,15 +295,44 @@
 
 
 def masked_rows(block, count, high, low):
-    none = jnp.zeros_like(high)
-    tops, lows = [], []
-    for h in range(count):
-        mask = block == jnp.full(block.shape, h, bf16)
-        tops.append(jnp.where(mask, high, none))
-        lows.append(jnp.where(mask, low, none))
-    return jnp.concatenate(
-        [jnp.concatenate(tops, axis=0), jnp.concatenate(lows, axis=0)], axis=1
-    )
+    width = block.shape[1]
+    row = iota((16, width), 0)
+    by_eight = lax.shift_right_logical(row, 3).astype(f32)
+    by_four = lax.shift_right_logical(row, 2).astype(f32)
+    none = jnp.zeros((16, width), bf16)
+    shares = []
+    for value in (high, low):
+        wide = value.astype(f32)
+        head, tail = wide[0:8], wide[8:12]
+        shares.append(
+            (
+                jnp.concatenate([head, head], axis=0).astype(bf16),
+                jnp.concatenate([tail, tail, tail, tail], axis=0).astype(bf16),
+            )
+        )
+    sets = ([], [])
+    for h in range(0, count, 4):
+        masks = [
+            block == (by_eight + h).astype(bf16),
+            block == (by_eight + (h + 2.0)).astype(bf16),
+            block == (by_four + h).astype(bf16),
+        ]
+        for rows, (head, tail) in zip(sets, shares):
+            rows.append(jnp.where(masks[0], head, none))
+            rows.append(jnp.where(masks[1], head, none))
+            rows.append(jnp.where(masks[2], tail, none))
+    return jnp.concatenate(sets[0] + sets[1], axis=0)
+
+
+def place_of(block):
+    base = 48 * (block // 4)
+    return base + 8 * (block % 4), base + 32 + 4 * (block % 4)
+
+
+def add_products(total, left, hot):
+    both = lax.dot_general(left, hot, (((1,), (1,)), ((), ())), preferred_element_type=f32)
+    half = both.shape[0] // 2
+    total[...] += both[0:half] + both[half:]
 
 
 def select_kernel(wanted, parts, send):
@@ -378,8 +379,7 @@
     low_ref,
     hot_ref,
     block_ref,
-    rise_ref,
-    fall_ref,
+    fold_ref,
     grads,
     total,
 ):
@@ -388,6 +388,7 @@
     diagonal = sub == (lane & 7)
     diag_wide = iota((8, CHUNK), 0) == (iota((8, CHUNK), 1) & 7)
     depth = lax.shift_right_logical(lane, 3)
+    early = (iota((CHUNK, 128), 1) & (SIDE - 1)) < SIDE // 2
     total[...] = jnp.zeros_like(total)
     for owner in range(OWNERS):
         pieces = []
@@ -516,7 +517,7 @@
             blank = jnp.zeros((96, PIX), f32)
             form = jnp.concatenate([back[...].astype(f32), blank], axis=0).T
             paint = jnp.concatenate([blank[0:32], errs[g], blank[0:48]], axis=0).T
-            sides.append(jnp.concatenate([form, form, paint, paint], axis=0).astype(bf16))
+            sides.append(jnp.concatenate([form, paint, paint], axis=0).astype(bf16))
 
         def backward(step, carry):
             at = pl.multiple_of((CHUNKS - 1 - step) * CHUNK, CHUNK)
@@ -535,9 +536,13 @@
                     pieces[k] = weight[rows] * gap
                     behind = behind + alpha[rows] * gap
                 result.append(behind)
-                high, low = halves(jnp.concatenate(pieces, axis=0))
-                rise_ref[g, pl.ds(at, CHUNK), :] = high
-                fall_ref[g, pl.ds(at, CHUNK), :] = low
+                whole_rows = jnp.concatenate(pieces, axis=0)
+                upper, lower = whole_rows[:, 0:128], whole_rows[:, 128:256]
+                even, odd = upper + lower, upper - lower
+                folded = jnp.where(
+                    early, even + pltpu.roll(even, 120, 1), odd - pltpu.roll(odd, 8, 1)
+                )
+                fold_ref[g, pl.ds(at, CHUNK), :] = jnp.concatenate(halves(folded), axis=1)
             return tuple(result)
 
         lax.fori_loop(
@@ -553,9 +558,7 @@
             row = iota((8, BLOCK), 0)
             match = row == (iota((8, BLOCK), 1) & 7)
             for g in range(TOGETHER):
-                pieces = [
-                    ref[g, pl.ds(at, BLOCK), :] for ref in (rise_ref, fall_ref, high_ref, low_ref)
-                ]
+                pieces = [ref[g, pl.ds(at, BLOCK), :] for ref in (fold_ref, high_ref, low_ref)]
                 sums = jnp.dot(
                     jnp.concatenate(pieces, axis=1), sides[g], preferred_element_type=f32
                 ).T
@@ -580,11 +583,7 @@
                 high = grads[g, 0, :, pl.ds(at, SCAT)]
                 low = grads[g, 1, :, pl.ds(at, SCAT)]
                 left = masked_rows(block, 32, high, low)
-                hot = hot_ref[g, :, pl.ds(at, SCAT)]
-                hot = jnp.concatenate([hot, hot], axis=1)
-                total[...] += lax.dot_general(
-                    left, hot, (((1,), (1,)), ((), ())), preferred_element_type=f32
-                )
+                add_products(total, left, hot_ref[g, :, pl.ds(at, SCAT)])
             return carry
 
         lax.fori_loop(0, ROWS // SCAT, scatter, 0, unroll=UNROLL_SCATTER)
@@ -593,10 +592,10 @@
     loss = lax.fori_loop(0, GROUPS // TOGETHER, one_set, jnp.zeros((8, 128), f32))
     for owner in range(OWNERS):
         for j in range(4):
-            base = 16 * (2 * owner + j // 2)
+            head, tail = place_of(2 * owner + j // 2)
             lanes = slice(128 * (j % 2), 128 * (j % 2) + 128)
-            answer[owner, 8 * j : 8 * j + 8, :] = total[base : base + 8, lanes]
-            answer[owner, 32 + 4 * j : 36 + 4 * j, :] = total[base + 8 : base + 12, lanes]
+            answer[owner, 8 * j : 8 * j + 8, :] = total[head : head + 8, lanes]
+            answer[owner, 32 + 4 * j : 36 + 4 * j, :] = total[tail : tail + 4, lanes]
         answer[owner, 48:56, :] = loss
 
 
@@ -612,9 +611,8 @@
         pltpu.VMEM((TOGETHER, 256, ROWS), bf16),
         pltpu.VMEM((TOGETHER, 16, ROWS), bf16),
         pltpu.VMEM((TOGETHER, ROWS, PIX), bf16),
-        pltpu.VMEM((TOGETHER, ROWS, PIX), bf16),
         pltpu.VMEM((TOGETHER, 2, 16, ROWS), bf16),
-        pltpu.VMEM((512, 256), f32),
+        pltpu.VMEM((384, 256), f32),
     ]
 
 
@@ -643,11 +641,7 @@
         block = jnp.concatenate(blocks, axis=1)
         spot = jnp.concatenate(spots, axis=1)
         left = masked_rows(small(block), 16, high, low)
-        hot = unit_rows(small(spot), CAP)
-        hot = jnp.concatenate([hot, hot], axis=1)
-        total[...] += lax.dot_general(
-            left, hot, (((1,), (1,)), ((), ())), preferred_element_type=f32
-        )
+        add_products(total, left, unit_rows(small(spot), CAP))
         return squares + back[band, 48:56, :]
 
     squares = lax.fori_loop(
@@ -657,7 +651,9 @@
     loss[...] = whole * (1.0 / (TILES * OWNERS * PIX * 3))
     for h in range(16):
         lanes = slice(256 * h, 256 * h + 256)
-        gain = [total[16 * h + c : 16 * h + c + 1, :] for c in range(12)]
+        head, tail = place_of(h)
+        gain = [total[head + c : head + c + 1, :] for c in range(8)]
+        gain += [total[tail + c : tail + c + 1, :] for c in range(4)]
         ca, sa, cb, sb, c0, c1, c2 = [aux[c : c + 1, lanes] for c in range(7)]
         cos_x, sin_x = 1.0 - 2.0 * sa * sa, 2.0 * sa * ca
         cos_y, sin_y = 1.0 - 2.0 * sb * sb, 2.0 * sb * cb
@@ -781,11 +777,10 @@
     parts, aux = pl.pallas_call(
         project_kernel,
         out_shape=(jax.ShapeDtypeStruct((384, 256), bf16), shape(16, LOCAL + 128)),
-        in_specs=[whole()] + [pl.BlockSpec(memory_space=pl.ANY)] * 5,
+        in_specs=[whole()] * 6,
         out_specs=(whole(), whole()),
-        scratch_shapes=[pltpu.VMEM((rows, LOCAL), f32) for rows in (16, 3, 3, 4, 1, 48)]
-        + [pltpu.SemaphoreType.DMA((5,))],
-        compiler_params=params(56),
+        scratch_shapes=[pltpu.VMEM((16, LOCAL), f32)],
+        compiler_params=params(24),
         name="project",
     )(view_angles, positions, log_scales, rotations, opacity_logit, sh_coeffs)
     send = pl.pallas_call(
@@ -820,7 +815,7 @@
         out_shape=(shape(8, WIDE), shape(1, 1)),
         in_specs=[whole()] * 3,
         out_specs=(whole(), whole()),
-        scratch_shapes=[pltpu.VMEM((256, 256), f32)],
+        scratch_shapes=[pltpu.VMEM((192, 256), f32)],
         compiler_params=params(32),
         name="collect",
     )(returned, wanted, aux)

time: 96.3 us -> 90.3 us (0.938)
  Pallas kernels: 40.4 us -> 32.3 us
  local copies, waits for them, and re-layouts: 3.97 us -> 6.42 us
    pallas_call x1, Pallas kernels: 28.7 us -> 24 us  [local(): pl.pallas_call(blend_kernel, out_shape=(shape(TILES, 3, PIX), shape(OWNER...]
    pallas_call x1, Pallas kernels: 3.5 us -> 0.59 us  [local(): pl.pallas_call(project_kernel, out_shape=(jax.ShapeDtypeStruct((384, 256)...]
    unnamed x25 -> x29, local copies, waits for them, and re-layouts: 2.41 us -> 4.82 us
  transfers between devices with their start and end apart: 6 -> 6, of which waited for: 5 -> 5; matrix products, arithmetic and copies ran while one was open for 2% -> 2% of each run, Pallas kernels for 4% -> 1%
where the time goes in v4:
time: 90.3 us; the launch traced here: 89.8 us
  Pallas kernels  32.3 us (36%)
  starting transfers between devices  22.5 us (25%)
  waiting for transfers between devices  15.1 us (17%)
  blocking collectives  12.1 us (13%)
  local copies, waits for them, and re-layouts  6.42 us (7%)
    pallas_call x1, Pallas kernels, local(): pl.pallas_call(blend_kernel, out_shape=(shape(TILES, 3, PIX), shape(OWNER...  24 us
    all_to_all x1, blocking collectives, local(): lax.all_to_all(answer, 'band', split_axis=0, concat_axis=0, tiled=True)  12.1 us
    all_to_all x1, starting transfers between devices, local(): lax.all_to_all(fetch_index.reshape(OWNERS, 4, 128), 'band', split_axis=0,...  8.6 us
    all_to_all x1, waiting for transfers between devices, local(): lax.all_to_all(send, 'band', split_axis=0, concat_axis=0, tiled=True)  6.46 us
    ppermute x1, starting transfers between devices, local(): far = lax.ppermute(near, 'view', [(v, v ^ 1) for v in range(VIEWS)])  5.37 us
    ppermute x3, waiting for transfers between devices, local(): around.append(lax.ppermute(share, 'view', ring))  5.14 us
    unnamed x29, local copies, waits for them, and re-layouts  4.82 us
    all_to_all x1, starting transfers between devices, local(): lax.all_to_all(send, 'band', split_axis=0, concat_axis=0, tiled=True)  4.29 us
  transfers between devices with their start and end apart: 6, of which 5 were waited for; matrix products, arithmetic and copies ran while one was open for 2% of the time, Pallas kernels for 1%

profile of v4, /device:TPU:1, one launch (start us, length us, event | category | flops | bytes accessed | tf_op | source)
XLA Modules:
  0.0 89.8 jit_solution(12346501664332576873)
XLA Ops:
  0.7 1.4 %reshape.24 = s32[16,4,128]{2,1,0:T(4,128)} reshape(s32[1,1,16,512]{3,2,1,0:T(8,128)} %param.20) | data formatting | bytes 65536 | tf_op jit(solution)/shard_map/reshape | solution.py:773
  2.1 8.6 %all-to-all-start = ((s32[16,4,128]{2,1,0:T(4,128)}), s32[16,4,128]{2,1,0:T(4,128)S(1)}, u32[]{:S(2)}, u32[]{:S(2)}) async-start(s32[16,4,128]{2,1,0:T(4,128)} %reshape.24), calls=%async_computation | async-start | bytes 65536 | tf_op jit(solution)/shard_map/all_to_all | solution.py:772
  10.7 1.1 %copy-done = f32[48,4096]{1,0:T(8,128)S(1)} copy-done((f32[48,4096]{1,0:T(8,128)S(1)}, f32[48,4096]{1,0:T(8,128)}, u32[]{:S(2)}) %copy-start) | copy-done | bytes 786456
  11.8 0.7 copy-done.3
  12.6 0.8 copy-done.5
  13.4 0.7 copy-done.10
  14.0 0.6 project.1
  14.6 2.5 %all-to-all-done.wanted = s32[16,4,128]{2,1,0:T(4,128)S(1)} async-done(((s32[16,4,128]{2,1,0:T(4,128)}), s32[16,4,128]{2,1,0:T(4,128)S(1)}, u32[]{:S(2)}, u32[]{:S(2)}) %all-to-all-start) | async-done | bytes 32800 | tf_op jit(solution)/shard_map/all_to_all | solution.py:772
  17.2 3.1 %select.1 = f32[16,48,128]{2,1,0:T(8,128)} custom-call(s32[16,4,128]{2,1,0:T(4,128)S(1)} %all-to-all-done.wanted, bf16[384,256]{1,0:T(8,128)(2,1)S(1)} %get-tuple-element.18.parts), custom_call_target="tpu_custom_call" | custom-call | tf_op jit(solution)/shard_map/select/pallas_call | solution.py:786
  20.2 4.3 %all-to-all-start.1 = ((f32[16,48,128]{2,1,0:T(8,128)}), f32[16,48,128]{2,1,0:T(8,128)S(1)}, u32[]{:S(2)}, u32[]{:S(2)}) async-start(f32[16,48,128]{2,1,0:T(8,128)} %select.1), calls=%async_computation.1 | async-start | bytes 786432 | tf_op jit(solution)/shard_map/all_to_all | solution.py:794
  24.6 0.5 broadcast.5
  25.2 0.7 reduce.3
  26.2 6.5 %all-to-all-done.1.table = f32[16,48,128]{2,1,0:T(8,128)S(1)} async-done(((f32[16,48,128]{2,1,0:T(8,128)}), f32[16,48,128]{2,1,0:T(8,128)S(1)}, u32[]{:S(2)}, u32[]{:S(2)}) %all-to-all-start.1) | async-done | bytes 393248 | tf_op jit(solution)/shard_map/all_to_all | solution.py:794
  32.7 24.0 %blend.1 = (f32[48,3,256]{2,1,0:T(4,128)S(1)}, f32[16,56,128]{2,1,0:T(8,128)S(1)}) custom-call(f32[16,48,128]{2,1,0:T(8,128)S(1)} %all-to-all-done.1.table, s32[48,256]{1,0:T(8,128)S(1)} %bitcast.16, s32[48,256]{1,0:T(8,128)S(1)} %bitcast.17, s32[6,128]{1,0:T(8,128)S(1)} %tile.12.counts, f32[48,3,256]{2,1,0:T(4,128)S(1)} %bitcast.13, ...), custom_call_target="tpu_custom_call" | custom-call | tf_op jit(solution)/shard_map/blend/pallas_call | solution.py:795
  56.7 12.1 %all_to_all.15.back = f32[16,56,128]{2,1,0:T(8,128)S(1)} all-to-all(f32[16,56,128]{2,1,0:T(8,128)S(1)} %get-tuple-element.20), channel_id=1, replica_groups=mesh['view'=8,'band'=16] {'band'}, dimensions={0} | all-to-all | bytes 917504 | tf_op jit(solution)/shard_map/all_to_all | solution.py:812
  68.8 3.1 %collect.1 = (f32[8,4736]{1,0:T(8,128)S(1)}, f32[1,1]{1,0:T(1,128)}) custom-call(f32[16,56,128]{2,1,0:T(8,128)S(1)} %all_to_all.15.back, s32[16,4,128]{2,1,0:T(4,128)S(1)} %all-to-all-done.wanted, f32[16,4224]{1,0:T(8,128)S(1)} %get-tuple-element.21.aux), custom_call_target="tpu_custom_call" | custom-call | tf_op jit(solution)/shard_map/collect/pallas_call | solution.py:813
  71.9 2.5 %collective-permute-start.2 = (f32[8,4736]{1,0:T(8,128)S(1)}, f32[8,4736]{1,0:T(8,128)S(1)}, u32[]{:S(2)}, u32[]{:S(2)}) collective-permute-start(f32[8,4736]{1,0:T(8,128)S(1)} %get-tuple-element.23), channel_id=1, source_target_pairs={{0,96},{16,112},{32,0},{48,16},{64,32},{80,48},{96,64},{112,80},{1... | collective-permute-start | bytes 454664 | tf_op jit(solution)/shard_map/ppermute | solution.py:825
  74.3 1.7 %collective-permute-start = (f32[8,4736]{1,0:T(8,128)S(1)}, f32[8,4736]{1,0:T(8,128)S(1)}, u32[]{:S(2)}, u32[]{:S(2)}) collective-permute-start(f32[8,4736]{1,0:T(8,128)S(1)} %get-tuple-element.23), channel_id=1, source_target_pairs={{0,64},{16,80},{32,96},{48,112},{64,0},{80,16},{96,32},{112,48},{1... | collective-permute-start | bytes 454664 | tf_op jit(solution)/shard_map/ppermute | solution.py:825
  76.1 0.4 collective-permute-done.2
  76.5 4.7 %collective-permute-done.1 = f32[8,4736]{1,0:T(8,128)S(1)} collective-permute-done((f32[8,4736]{1,0:T(8,128)S(1)}, f32[8,4736]{1,0:T(8,128)S(1)}, u32[]{:S(2)}, u32[]{:S(2)}) %collective-permute-start.1) | collective-permute-done | bytes 151584 | tf_op jit(solution)/shard_map/ppermute | solution.py:825
  81.2 5.4 %collective-permute-start.3 = (f32[4,8,4736]{2,1,0:T(8,128)S(1)}, f32[4,8,4736]{2,1,0:T(8,128)S(1)}, u32[]{:S(2)}, u32[]{:S(2)}) collective-permute-start(f32[4,8,4736]{2,1,0:T(8,128)S(1)} %pad_maximum_fusion.near), channel_id=1, source_target_pairs={{0,16},{16,0},{32,48},{48,32},{64,80},{80,64},{96,112},{112,96},{1... | collective-permute-start | bytes 1818632 | tf_op jit(solution)/shard_map/ppermute | solution.py:827
  86.6 0.7 copy.23
  87.3 1.0 %collective-permute-done.3.far = f32[4,8,4736]{2,1,0:T(8,128)S(1)} collective-permute-done((f32[4,8,4736]{2,1,0:T(8,128)S(1)}, f32[4,8,4736]{2,1,0:T(8,128)S(1)}, u32[]{:S(2)}, u32[]{:S(2)}) %collective-permute-start.3) | collective-permute-done | bytes 606240 | tf_op jit(solution)/shard_map/ppermute | solution.py:827
  88.3 1.5 %finish.1 = (f32[3,4096]{1,0:T(4,128)}, f32[3,4096]{1,0:T(4,128)}, f32[4,4096]{1,0:T(4,128)}, f32[1,4096]{1,0:T(1,128)}, f32[48,4096]{1,0:T(8,128)}) custom-call(f32[4,8,4736]{2,1,0:T(8,128)S(1)} %pad_maximum_fusion.near, f32[4,8,4736]{2,1,0:T(8,128)S(1)} %collective-permute-done.3.far, f32[3,4096]{1,0:T(4,128)S(1)} %copy-done.1, f32[4,4096]{1,0:T(4,128)S(1)} %copy-done.2, ...), custom_call_target="tpu_custom_call" | custom-call | tf_op jit(solution)/shard_map/finish/pallas_call | solution.py:828
  (29 shorter events, 0.5 us)
Async XLA Ops:
  0.6 10.0 %copy-start.2 = (f32[4,4096]{1,0:T(4,128)S(1)}, f32[4,4096]{1,0:T(4,128)}, u32[]{:S(2)}) copy-start(f32[4,4096]{1,0:T(4,128)} %rotations.3) | copy-start | bytes 196612
  0.6 10.0 %copy-start.1 = (f32[3,4096]{1,0:T(4,128)S(1)}, f32[3,4096]{1,0:T(4,128)}, u32[]{:S(2)}) copy-start(f32[3,4096]{1,0:T(4,128)} %log_scales.3) | copy-start | bytes 147460
  2.1 15.1 %all-to-all-start = ((s32[16,4,128]{2,1,0:T(4,128)}), s32[16,4,128]{2,1,0:T(4,128)S(1)}, u32[]{:S(2)}, u32[]{:S(2)}) async-start(s32[16,4,128]{2,1,0:T(4,128)} %reshape.24), calls=%async_computation | async-start | bytes 65536 | tf_op jit(solution)/shard_map/all_to_all | solution.py:772
  10.7 1.1 %copy-start = (f32[48,4096]{1,0:T(8,128)S(1)}, f32[48,4096]{1,0:T(8,128)}, u32[]{:S(2)}) copy-start(f32[48,4096]{1,0:T(8,128)} %sh.1) | copy-start | bytes 2359300
  11.8 0.7 copy-start.3
  12.6 0.8 copy-start.5
  13.4 0.7 copy-start.10
  20.2 5.8 %copy-start.11 = (f32[1,48,3,256]{3,1,2,0:T(8,128)S(1)}, f32[1,48,3,256]{3,1,2,0:T(8,128)}, u32[]{:S(2)}) copy-start(f32[1,48,3,256]{3,1,2,0:T(8,128)} %param.19) | copy-start | bytes 442372
  20.2 12.4 %all-to-all-start.1 = ((f32[16,48,128]{2,1,0:T(8,128)}), f32[16,48,128]{2,1,0:T(8,128)S(1)}, u32[]{:S(2)}, u32[]{:S(2)}) async-start(f32[16,48,128]{2,1,0:T(8,128)} %select.1), calls=%async_computation.1 | async-start | bytes 786432 | tf_op jit(solution)/shard_map/all_to_all | solution.py:794
  24.5 0.7 copy-start.12
  26.1 6.6 %copy-start.6 = (bf16[128,256]{1,0:T(8,128)(2,1)S(1)}, bf16[128,256]{1,0:T(8,128)(2,1)}, u32[]{:S(2)}) copy-start(bf16[128,256]{1,0:T(8,128)(2,1)} %constant.4.clone.front) | copy-start | bytes 196612
  26.1 6.6 %copy-start.7 = (s32[1,48,256]{2,1,0:T(8,128)S(1)}, s32[1,48,256]{2,1,0:T(8,128)}, u32[]{:S(2)}) copy-start(s32[1,48,256]{2,1,0:T(8,128)} %param.21) | copy-start | bytes 147460
  26.1 6.6 %copy-start.8 = (s32[1,48,256]{2,1,0:T(8,128)S(1)}, s32[1,48,256]{2,1,0:T(8,128)}, u32[]{:S(2)}) copy-start(s32[1,48,256]{2,1,0:T(8,128)} %param.22) | copy-start | bytes 147460
  26.1 6.6 %copy-start.9 = (bf16[32,256]{1,0:T(8,128)(2,1)S(1)}, bf16[32,256]{1,0:T(8,128)(2,1)}, u32[]{:S(2)}) copy-start(bf16[32,256]{1,0:T(8,128)(2,1)} %constant.5.clone.back) | copy-start | bytes 49156
  71.9 4.6 %collective-permute-start.2 = (f32[8,4736]{1,0:T(8,128)S(1)}, f32[8,4736]{1,0:T(8,128)S(1)}, u32[]{:S(2)}, u32[]{:S(2)}) collective-permute-start(f32[8,4736]{1,0:T(8,128)S(1)} %get-tuple-element.23), channel_id=1, source_target_pairs={{0,96},{16,112},{32,0},{48,16},{64,32},{80,48},{96,64},{112,80},{1... | collective-permute-start | bytes 454664 | tf_op jit(solution)/shard_map/ppermute | solution.py:825
  74.3 6.9 %collective-permute-start.1 = (f32[8,4736]{1,0:T(8,128)S(1)}, f32[8,4736]{1,0:T(8,128)S(1)}, u32[]{:S(2)}, u32[]{:S(2)}) collective-permute-start(f32[8,4736]{1,0:T(8,128)S(1)} %get-tuple-element.23), channel_id=1, source_target_pairs={{0,32},{16,48},{32,64},{48,80},{64,96},{80,112},{96,0},{112,16},{1... | collective-permute-start | bytes 454664 | tf_op jit(solution)/shard_map/ppermute | solution.py:825
  74.3 6.9 %collective-permute-start = (f32[8,4736]{1,0:T(8,128)S(1)}, f32[8,4736]{1,0:T(8,128)S(1)}, u32[]{:S(2)}, u32[]{:S(2)}) collective-permute-start(f32[8,4736]{1,0:T(8,128)S(1)} %get-tuple-element.23), channel_id=1, source_target_pairs={{0,64},{16,80},{32,96},{48,112},{64,0},{80,16},{96,32},{112,48},{1... | collective-permute-start | bytes 454664 | tf_op jit(solution)/shard_map/ppermute | solution.py:825
  81.2 7.0 %collective-permute-start.3 = (f32[4,8,4736]{2,1,0:T(8,128)S(1)}, f32[4,8,4736]{2,1,0:T(8,128)S(1)}, u32[]{:S(2)}, u32[]{:S(2)}) collective-permute-start(f32[4,8,4736]{2,1,0:T(8,128)S(1)} %pad_maximum_fusion.near), channel_id=1, source_target_pairs={{0,16},{16,0},{32,48},{48,32},{64,80},{80,64},{96,112},{112,96},{1... | collective-permute-start | bytes 1818632 | tf_op jit(solution)/shard_map/ppermute | solution.py:827
  86.6 1.7 %copy-start.4 = (f32[1,4096]{1,0:T(1,128)S(1)}, f32[1,4096]{1,0:T(1,128)}, u32[]{:S(2)}) copy-start(f32[1,4096]{1,0:T(1,128)} %logit.3) | copy-start | bytes 49156

commit v5 on v4

--- a/solution.py
+++ b/solution.py
@@ -31,8 +31,8 @@
 UNROLL_FORWARD = 8
 UNROLL_BACKWARD = 8
 UNROLL_SCATTER = 4
-UNROLL_SELECT = 4
-UNROLL_COLLECT = 4
+UNROLL_SELECT = 8
+UNROLL_COLLECT = 8
 TURN = 2.0 * math.pi / SIDE
 KAPPA = 0.5 / (TURN * TURN)
 LOG2E = 1.4426950408889634
@@ -820,7 +820,7 @@
         name="collect",
     )(returned, wanted, aux)
     around = [share]
-    for step in (4, 2, 6):
+    for step in (2, 6, 4):
         ring = [(v, (v + step) % VIEWS) for v in range(VIEWS)]
         around.append(lax.ppermute(share, "view", ring))
     near = jnp.stack(around)

time: 90.3 us -> 89.3 us (0.989)
  starting transfers between devices: 22.5 us -> 21.1 us
  waiting for transfers between devices: 15.1 us -> 16.2 us
    ppermute x1, starting transfers between devices: 5.37 us -> 3.99 us  [local(): far = lax.ppermute(near, 'view', [(v, v ^ 1) for v in range(VIEWS)])]
    ppermute x3, waiting for transfers between devices: 5.14 us -> 6.28 us  [local(): around.append(lax.ppermute(share, 'view', ring))]
  transfers between devices with their start and end apart: 6 -> 6, of which waited for: 5 -> 6; matrix products, arithmetic and copies ran while one was open for 2% -> 2% of each run, Pallas kernels for 1% -> 1%
where the time goes in v5:
time: 89.3 us; the launch traced here: 88.7 us
  Pallas kernels  31.4 us (35%)
  starting transfers between devices  21.1 us (24%)
  waiting for transfers between devices  16.2 us (18%)
  blocking collectives  12.1 us (14%)
  local copies, waits for them, and re-layouts  6.42 us (7%)
    pallas_call x1, Pallas kernels, local(): pl.pallas_call(blend_kernel, out_shape=(shape(TILES, 3, PIX), shape(OWNER...  24 us
    all_to_all x1, blocking collectives, local(): lax.all_to_all(answer, 'band', split_axis=0, concat_axis=0, tiled=True)  12.1 us
    all_to_all x1, starting transfers between devices, local(): lax.all_to_all(fetch_index.reshape(OWNERS, 4, 128), 'band', split_axis=0,...  8.6 us
    all_to_all x1, waiting for transfers between devices, local(): lax.all_to_all(send, 'band', split_axis=0, concat_axis=0, tiled=True)  6.46 us
    ppermute x3, waiting for transfers between devices, local(): around.append(lax.ppermute(share, 'view', ring))  6.28 us
    unnamed x29, local copies, waits for them, and re-layouts  4.82 us
    all_to_all x1, starting transfers between devices, local(): lax.all_to_all(send, 'band', split_axis=0, concat_axis=0, tiled=True)  4.29 us
    ppermute x3, starting transfers between devices, local(): around.append(lax.ppermute(share, 'view', ring))  4.2 us
  transfers between devices with their start and end apart: 6, of which 6 were waited for; matrix products, arithmetic and copies ran while one was open for 2% of the time, Pallas kernels for 1%

profile of v5, /device:TPU:1, one launch (start us, length us, event | category | flops | bytes accessed | tf_op | source)
XLA Modules:
  0.0 88.7 jit_solution(14013162028709578151)
XLA Ops:
  0.7 1.4 %reshape.24 = s32[16,4,128]{2,1,0:T(4,128)} reshape(s32[1,1,16,512]{3,2,1,0:T(8,128)} %param.20) | data formatting | bytes 65536 | tf_op jit(solution)/shard_map/reshape | solution.py:773
  2.1 8.6 %all-to-all-start = ((s32[16,4,128]{2,1,0:T(4,128)}), s32[16,4,128]{2,1,0:T(4,128)S(1)}, u32[]{:S(2)}, u32[]{:S(2)}) async-start(s32[16,4,128]{2,1,0:T(4,128)} %reshape.24), calls=%async_computation | async-start | bytes 65536 | tf_op jit(solution)/shard_map/all_to_all | solution.py:772
  10.7 1.1 %copy-done = f32[48,4096]{1,0:T(8,128)S(1)} copy-done((f32[48,4096]{1,0:T(8,128)S(1)}, f32[48,4096]{1,0:T(8,128)}, u32[]{:S(2)}) %copy-start) | copy-done | bytes 786456
  11.8 0.7 copy-done.3
  12.6 0.8 copy-done.5
  13.4 0.7 copy-done.10
  14.6 2.5 %all-to-all-done.wanted = s32[16,4,128]{2,1,0:T(4,128)S(1)} async-done(((s32[16,4,128]{2,1,0:T(4,128)}), s32[16,4,128]{2,1,0:T(4,128)S(1)}, u32[]{:S(2)}, u32[]{:S(2)}) %all-to-all-start) | async-done | bytes 32800 | tf_op jit(solution)/shard_map/all_to_all | solution.py:772
  17.2 2.7 %select.1 = f32[16,48,128]{2,1,0:T(8,128)} custom-call(s32[16,4,128]{2,1,0:T(4,128)S(1)} %all-to-all-done.wanted, bf16[384,256]{1,0:T(8,128)(2,1)S(1)} %get-tuple-element.18.parts), custom_call_target="tpu_custom_call" | custom-call | tf_op jit(solution)/shard_map/select/pallas_call | solution.py:786
  19.9 4.3 %all-to-all-start.1 = ((f32[16,48,128]{2,1,0:T(8,128)}), f32[16,48,128]{2,1,0:T(8,128)S(1)}, u32[]{:S(2)}, u32[]{:S(2)}) async-start(f32[16,48,128]{2,1,0:T(8,128)} %select.1), calls=%async_computation.1 | async-start | bytes 786432 | tf_op jit(solution)/shard_map/all_to_all | solution.py:794
  24.9 0.7 reduce.3
  25.9 6.5 %all-to-all-done.1.table = f32[16,48,128]{2,1,0:T(8,128)S(1)} async-done(((f32[16,48,128]{2,1,0:T(8,128)}), f32[16,48,128]{2,1,0:T(8,128)S(1)}, u32[]{:S(2)}, u32[]{:S(2)}) %all-to-all-start.1) | async-done | bytes 393248 | tf_op jit(solution)/shard_map/all_to_all | solution.py:794
  32.4 24.0 %blend.1 = (f32[48,3,256]{2,1,0:T(4,128)S(1)}, f32[16,56,128]{2,1,0:T(8,128)S(1)}) custom-call(f32[16,48,128]{2,1,0:T(8,128)S(1)} %all-to-all-done.1.table, s32[48,256]{1,0:T(8,128)S(1)} %bitcast.16, s32[48,256]{1,0:T(8,128)S(1)} %bitcast.17, s32[6,128]{1,0:T(8,128)S(1)} %tile.12.counts, f32[48,3,256]{2,1,0:T(4,128)S(1)} %bitcast.13, ...), custom_call_target="tpu_custom_call" | custom-call | tf_op jit(solution)/shard_map/blend/pallas_call | solution.py:795
  56.3 12.1 %all_to_all.15.back = f32[16,56,128]{2,1,0:T(8,128)S(1)} all-to-all(f32[16,56,128]{2,1,0:T(8,128)S(1)} %get-tuple-element.20), channel_id=1, replica_groups=mesh['view'=8,'band'=16] {'band'}, dimensions={0} | all-to-all | bytes 917504 | tf_op jit(solution)/shard_map/all_to_all | solution.py:812
  68.4 2.6 %collect.1 = (f32[8,4736]{1,0:T(8,128)S(1)}, f32[1,1]{1,0:T(1,128)}) custom-call(f32[16,56,128]{2,1,0:T(8,128)S(1)} %all_to_all.15.back, s32[16,4,128]{2,1,0:T(4,128)S(1)} %all-to-all-done.wanted, f32[16,4224]{1,0:T(8,128)S(1)} %get-tuple-element.21.aux), custom_call_target="tpu_custom_call" | custom-call | tf_op jit(solution)/shard_map/collect/pallas_call | solution.py:813
  71.1 2.7 %collective-permute-start.2 = (f32[8,4736]{1,0:T(8,128)S(1)}, f32[8,4736]{1,0:T(8,128)S(1)}, u32[]{:S(2)}, u32[]{:S(2)}) collective-permute-start(f32[8,4736]{1,0:T(8,128)S(1)} %get-tuple-element.23), channel_id=1, source_target_pairs={{0,64},{16,80},{32,96},{48,112},{64,0},{80,16},{96,32},{112,48},{1... | collective-permute-start | bytes 454664 | tf_op jit(solution)/shard_map/ppermute | solution.py:825
  73.8 0.9 collective-permute-start.1
  74.7 0.6 collective-permute-start
  75.3 1.3 %collective-permute-done.2 = f32[8,4736]{1,0:T(8,128)S(1)} collective-permute-done((f32[8,4736]{1,0:T(8,128)S(1)}, f32[8,4736]{1,0:T(8,128)S(1)}, u32[]{:S(2)}, u32[]{:S(2)}) %collective-permute-start.2) | collective-permute-done | bytes 151584 | tf_op jit(solution)/shard_map/ppermute | solution.py:825
  76.6 1.7 %collective-permute-done.1 = f32[8,4736]{1,0:T(8,128)S(1)} collective-permute-done((f32[8,4736]{1,0:T(8,128)S(1)}, f32[8,4736]{1,0:T(8,128)S(1)}, u32[]{:S(2)}, u32[]{:S(2)}) %collective-permute-start.1) | collective-permute-done | bytes 151584 | tf_op jit(solution)/shard_map/ppermute | solution.py:825
  78.3 3.2 %collective-permute-done = f32[8,4736]{1,0:T(8,128)S(1)} collective-permute-done((f32[8,4736]{1,0:T(8,128)S(1)}, f32[8,4736]{1,0:T(8,128)S(1)}, u32[]{:S(2)}, u32[]{:S(2)}) %collective-permute-start) | collective-permute-done | bytes 151584 | tf_op jit(solution)/shard_map/ppermute | solution.py:825
  81.6 4.0 %collective-permute-start.3 = (f32[4,8,4736]{2,1,0:T(8,128)S(1)}, f32[4,8,4736]{2,1,0:T(8,128)S(1)}, u32[]{:S(2)}, u32[]{:S(2)}) collective-permute-start(f32[4,8,4736]{2,1,0:T(8,128)S(1)} %pad_maximum_fusion.near), channel_id=1, source_target_pairs={{0,16},{16,0},{32,48},{48,32},{64,80},{80,64},{96,112},{112,96},{1... | collective-permute-start | bytes 1818632 | tf_op jit(solution)/shard_map/ppermute | solution.py:827
  85.6 0.7 copy.23
  86.3 1.0 %collective-permute-done.3.far = f32[4,8,4736]{2,1,0:T(8,128)S(1)} collective-permute-done((f32[4,8,4736]{2,1,0:T(8,128)S(1)}, f32[4,8,4736]{2,1,0:T(8,128)S(1)}, u32[]{:S(2)}, u32[]{:S(2)}) %collective-permute-start.3) | collective-permute-done | bytes 606240 | tf_op jit(solution)/shard_map/ppermute | solution.py:827
  87.2 1.5 %finish.1 = (f32[3,4096]{1,0:T(4,128)}, f32[3,4096]{1,0:T(4,128)}, f32[4,4096]{1,0:T(4,128)}, f32[1,4096]{1,0:T(1,128)}, f32[48,4096]{1,0:T(8,128)}) custom-call(f32[4,8,4736]{2,1,0:T(8,128)S(1)} %pad_maximum_fusion.near, f32[4,8,4736]{2,1,0:T(8,128)S(1)} %collective-permute-done.3.far, f32[3,4096]{1,0:T(4,128)S(1)} %copy-done.1, f32[4,4096]{1,0:T(4,128)S(1)} %copy-done.2, ...), custom_call_target="tpu_custom_call" | custom-call | tf_op jit(solution)/shard_map/finish/pallas_call | solution.py:828
  (29 shorter events, 1.6 us)
Async XLA Ops:
  0.6 10.0 %copy-start.2 = (f32[4,4096]{1,0:T(4,128)S(1)}, f32[4,4096]{1,0:T(4,128)}, u32[]{:S(2)}) copy-start(f32[4,4096]{1,0:T(4,128)} %rotations.3) | copy-start | bytes 196612
  0.6 10.0 %copy-start.1 = (f32[3,4096]{1,0:T(4,128)S(1)}, f32[3,4096]{1,0:T(4,128)}, u32[]{:S(2)}) copy-start(f32[3,4096]{1,0:T(4,128)} %log_scales.3) | copy-start | bytes 147460
  2.1 15.1 %all-to-all-start = ((s32[16,4,128]{2,1,0:T(4,128)}), s32[16,4,128]{2,1,0:T(4,128)S(1)}, u32[]{:S(2)}, u32[]{:S(2)}) async-start(s32[16,4,128]{2,1,0:T(4,128)} %reshape.24), calls=%async_computation | async-start | bytes 65536 | tf_op jit(solution)/shard_map/all_to_all | solution.py:772
  10.7 1.1 %copy-start = (f32[48,4096]{1,0:T(8,128)S(1)}, f32[48,4096]{1,0:T(8,128)}, u32[]{:S(2)}) copy-start(f32[48,4096]{1,0:T(8,128)} %sh.1) | copy-start | bytes 2359300
  11.8 0.7 copy-start.3
  12.6 0.8 copy-start.5
  13.4 0.7 copy-start.10
  19.9 5.8 %copy-start.11 = (f32[1,48,3,256]{3,1,2,0:T(8,128)S(1)}, f32[1,48,3,256]{3,1,2,0:T(8,128)}, u32[]{:S(2)}) copy-start(f32[1,48,3,256]{3,1,2,0:T(8,128)} %param.19) | copy-start | bytes 442372
  19.9 12.4 %all-to-all-start.1 = ((f32[16,48,128]{2,1,0:T(8,128)}), f32[16,48,128]{2,1,0:T(8,128)S(1)}, u32[]{:S(2)}, u32[]{:S(2)}) async-start(f32[16,48,128]{2,1,0:T(8,128)} %select.1), calls=%async_computation.1 | async-start | bytes 786432 | tf_op jit(solution)/shard_map/all_to_all | solution.py:794
  24.2 0.7 copy-start.12
  25.7 6.6 %copy-start.6 = (bf16[128,256]{1,0:T(8,128)(2,1)S(1)}, bf16[128,256]{1,0:T(8,128)(2,1)}, u32[]{:S(2)}) copy-start(bf16[128,256]{1,0:T(8,128)(2,1)} %constant.4.clone.front) | copy-start | bytes 196612
  25.7 6.6 %copy-start.7 = (s32[1,48,256]{2,1,0:T(8,128)S(1)}, s32[1,48,256]{2,1,0:T(8,128)}, u32[]{:S(2)}) copy-start(s32[1,48,256]{2,1,0:T(8,128)} %param.21) | copy-start | bytes 147460
  25.7 6.6 %copy-start.8 = (s32[1,48,256]{2,1,0:T(8,128)S(1)}, s32[1,48,256]{2,1,0:T(8,128)}, u32[]{:S(2)}) copy-start(s32[1,48,256]{2,1,0:T(8,128)} %param.22) | copy-start | bytes 147460
  25.7 6.6 %copy-start.9 = (bf16[32,256]{1,0:T(8,128)(2,1)S(1)}, bf16[32,256]{1,0:T(8,128)(2,1)}, u32[]{:S(2)}) copy-start(bf16[32,256]{1,0:T(8,128)(2,1)} %constant.5.clone.back) | copy-start | bytes 49156
  71.1 5.5 %collective-permute-start.2 = (f32[8,4736]{1,0:T(8,128)S(1)}, f32[8,4736]{1,0:T(8,128)S(1)}, u32[]{:S(2)}, u32[]{:S(2)}) collective-permute-start(f32[8,4736]{1,0:T(8,128)S(1)} %get-tuple-element.23), channel_id=1, source_target_pairs={{0,64},{16,80},{32,96},{48,112},{64,0},{80,16},{96,32},{112,48},{1... | collective-permute-start | bytes 454664 | tf_op jit(solution)/shard_map/ppermute | solution.py:825
  73.8 4.5 %collective-permute-start.1 = (f32[8,4736]{1,0:T(8,128)S(1)}, f32[8,4736]{1,0:T(8,128)S(1)}, u32[]{:S(2)}, u32[]{:S(2)}) collective-permute-start(f32[8,4736]{1,0:T(8,128)S(1)} %get-tuple-element.23), channel_id=1, source_target_pairs={{0,96},{16,112},{32,0},{48,16},{64,32},{80,48},{96,64},{112,80},{1... | collective-permute-start | bytes 454664 | tf_op jit(solution)/shard_map/ppermute | solution.py:825
  74.7 6.9 %collective-permute-start = (f32[8,4736]{1,0:T(8,128)S(1)}, f32[8,4736]{1,0:T(8,128)S(1)}, u32[]{:S(2)}, u32[]{:S(2)}) collective-permute-start(f32[8,4736]{1,0:T(8,128)S(1)} %get-tuple-element.23), channel_id=1, source_target_pairs={{0,32},{16,48},{32,64},{48,80},{64,96},{80,112},{96,0},{112,16},{1... | collective-permute-start | bytes 454664 | tf_op jit(solution)/shard_map/ppermute | solution.py:825
  81.6 5.6 %collective-permute-start.3 = (f32[4,8,4736]{2,1,0:T(8,128)S(1)}, f32[4,8,4736]{2,1,0:T(8,128)S(1)}, u32[]{:S(2)}, u32[]{:S(2)}) collective-permute-start(f32[4,8,4736]{2,1,0:T(8,128)S(1)} %pad_maximum_fusion.near), channel_id=1, source_target_pairs={{0,16},{16,0},{32,48},{48,32},{64,80},{80,64},{96,112},{112,96},{1... | collective-permute-start | bytes 1818632 | tf_op jit(solution)/shard_map/ppermute | solution.py:827
  85.6 1.7 %copy-start.4 = (f32[1,4096]{1,0:T(1,128)S(1)}, f32[1,4096]{1,0:T(1,128)}, u32[]{:S(2)}) copy-start(f32[1,4096]{1,0:T(1,128)} %logit.3) | copy-start | bytes 49156
